TPU v7x, 256 devices: a whole 4x4x8 slice. The times are simulated.
256 devices in a mesh: wide: 32 (over x_hi, z, core), narrow: 8 (over y, x_lo).
Axes of the slice: x: 4 (x_hi: 2, x_lo: 2; x = x_hi * 2 + x_lo), y: 4, z: 8, core: 2. Of those that a mesh axis runs over, the one named last changes fastest.
Arguments:
- leaf_multipoles: float32 [8, 25, 64, 4096], P('narrow', None, 'wide'), may hold values from -6 to 6
- leaf_order: int32 [8, 64, 4096], P('narrow', 'wide'), may hold values from 2 to 4
- subtree_octant: int32 [8, 64, 4096], P('narrow', 'wide'), may hold values from 0 to 7, as said below
- m2m_operators: float32 [8, 25, 25], replicated, may hold values from -0.4375 to 0.4375
- coupling: float32 [25, 25], replicated, may hold values from -1.25 to 1.25
- kernel_spectrum: float32 [2, 9, 64, 64, 64], P(None, None, None, 'wide', 'narrow'), may hold values from -6 to 6
- l2l_operators: float32 [8, 25, 25], replicated, may hold values from -1.25 to 1.25
Outputs:
- leaf_locals: float32 [8, 25, 64, 4096], P('narrow', None, 'wide')
Inputs may be any that keep to these rules, and one draw needn't show every extreme that they name: `subtree_octant`: for every coarse box the 8 slots hold its octants 0 to 7, each once.
All inputs are finite; a program needn't handle non-finite values.
Results may differ from a plain program's by a relative error of at most 0.0001.
Values sent between devices are 32-bit elements; how exact they have to be, the bound alone decides.
No kernel may reach another device: no remote copies, remote signals or barrier semaphores. Data moves between devices by JAX's collectives and lax.ppermute only.
A program may use at most 64 MiB of HBM per device.

v0:
```python
import numpy as np
import ml_dtypes

import jax
import jax.numpy as jnp
from jax import lax
from jax.experimental import pallas as pl
from jax.experimental.pallas import tpu as pltpu
from jax.sharding import PartitionSpec as P

ORDER = 4
GRID = 64
NC = 25
SLOTS = 5
BF = jnp.bfloat16
F32 = jnp.float32
VMEM_LIMIT = 48 * 1024 * 1024

DEGREE = np.array([n for n in range(ORDER + 1) for _ in range(2 * n + 1)])


def halves(table):
    high = table.astype(ml_dtypes.bfloat16)
    low = (table - high.astype(np.float64)).astype(ml_dtypes.bfloat16)
    return high, low


def stack_left(table):
    high, low = halves(table)
    return np.concatenate([high, low, high], axis=1)


def stack_right(table):
    high, low = halves(table)
    return np.concatenate([high, low, high], axis=0)


def wave(a, b):
    angle = 2.0 * np.pi * ((a * b) % GRID) / GRID
    return np.cos(angle), np.sin(angle)


def complex_table(cosine, sine, sign):
    return np.stack([np.stack([cosine, -sign * sine]), np.stack([sign * sine, cosine])])


def z_tables():
    z = np.arange(GRID)
    forward, inverse = [], []
    for n in range(8):
        rows = []
        for t in range(SLOTS):
            for m in range(8):
                rows.append(8 * (n ^ m) + t)
        cosine, sine = wave(np.array(rows)[:, None], z[None, :])
        table = np.concatenate([cosine, -sine], axis=0)
        high, low = halves(table)
        forward.append(np.concatenate([high, low], axis=0))
        inverse.append(stack_left(table.T / GRID))
    return np.stack(forward), np.stack(inverse)


def y_tables():
    ky = np.arange(GRID)
    cosine, sine = wave(ky[:, None], ky[None, :])

    def place(table):
        table = table.reshape(2, 2, 32, 2, 32, 2)
        table = table.transpose(2, 3, 0, 1, 5, 4)
        full = np.zeros((32, 2, 2, 2, 2, 2, 32, 2))
        for xl in range(2):
            full[:, xl, :, :, :, :, :, xl] = table
        return full.reshape(256, 256)

    forward = place(complex_table(cosine, sine, -1))
    back = complex_table(cosine, sine, 1) / GRID
    inverse = place(back.transpose(1, 0, 2, 3))
    return stack_left(forward), stack_right(inverse)


def x_tables():
    kx = np.arange(GRID)
    cosine, sine = wave(kx[:, None], kx[None, :])

    def place(table):
        table = table.reshape(2, 2, GRID, 32, 2).transpose(0, 2, 3, 4, 1)
        full = np.zeros((2, 2, GRID, 32, 2, 2, 2))
        for k2 in range(2):
            full[k2, :, :, :, :, k2, :] = table
        return full.reshape(256, 256)

    forward = place(complex_table(cosine, sine, -1))
    back = complex_table(cosine, sine, 1) / GRID
    inverse = place(back.transpose(1, 0, 2, 3)).T
    return stack_left(forward), stack_left(inverse)


def expand_tables():
    own = np.zeros((72, 640), np.float32)
    mirror = np.zeros((72, 640), np.float32)
    rows = np.zeros((128, NC), np.float32)
    lanes = np.zeros((NC, 640), np.float32)
    mask = np.zeros((128, 640), np.float32)
    for t in range(SLOTS):
        for c in range(NC):
            rows[t * NC + c, c] = 1
            for s in range(ORDER + 1):
                lane = s * 128 + t * NC + c
                lanes[c, lane] = 1
                d = DEGREE[c] + s
                own[d * 8 + t, lane] = 1
                if 1 <= t <= 3:
                    mirror[d * 8 + 8 - t, lane] = 1
                for j in range(NC):
                    if DEGREE[j] == s:
                        mask[t * NC + j, lane] = 1
    flip = np.zeros((GRID, GRID), np.float32)
    for k in range(GRID):
        flip[(-k) % GRID, k] = 1
    return np.concatenate([own, mirror], axis=0), rows, lanes, mask, flip


def split(value):
    high = value.astype(BF)
    low = (value - high.astype(F32)).astype(BF)
    return high, low


def stacked(value, axis):
    high, low = split(value)
    return jnp.concatenate([high, high, low], axis=axis)


def dot(a, b, dims=((1,), (0,)), precision=None):
    return lax.dot_general(a, b, (dims, ((), ())), precision=precision, preferred_element_type=F32)


def degree_column():
    row = lax.broadcasted_iota(jnp.int32, (32, 1), 0)
    one = lambda bound: (row >= bound).astype(jnp.int32)
    return one(1) + one(4) + one(9) + one(16) + 90 * one(25)


def load_operators(op_ref, w_ref):
    w_ref[...] = jnp.zeros_like(w_ref)
    w_ref[0:200, 0:NC] = op_ref[...]
    rows = [w_ref[pl.ds(octant, 32, stride=8), :][:, 0:32] for octant in range(8)]
    high, low = split(jnp.concatenate(rows, axis=0))
    return jnp.concatenate([high, low, high], axis=1)


def lane_rows(ref, first, count):
    return jnp.concatenate([ref[pl.ds(first + i, 1), :] for i in range(count)], axis=1)


def translate(w_cat, value, octant):
    product = dot(w_cat, stacked(value, 0))
    total = product[0:32]
    for o in range(1, 8):
        total = jnp.where(octant == o, product[32 * o : 32 * o + 32], total)
    return total


GROUP = 4


def head_kernel(leaf_ref, order_ref, octant_ref, op_ref, table_ref, out_ref, xs, ws, ms, sem):
    copy = pltpu.make_async_copy(leaf_ref, xs.at[pl.ds(0, NC * 64)], sem)
    copy.start()
    w_cat = load_operators(op_ref, ws)
    degree = degree_column()
    me = lax.axis_index("narrow")
    table = table_ref[me]
    for m in range(16):
        out_ref[m * 128 + 120 : m * 128 + 128, :] = jnp.zeros((8, 128), F32)
    copy.wait()

    def group(g, carry):
        b = g * GROUP
        x = jnp.concatenate([xs[pl.ds(b + i, 32, stride=64), :] for i in range(GROUP)], axis=1)
        kept = jnp.where(degree <= lane_rows(order_ref, b, GROUP), x, 0.0)
        total = translate(w_cat, kept, lane_rows(octant_ref, b, GROUP))
        for i in range(GROUP):
            ms[pl.ds(b + i, NC, stride=64), :] = total[0:NC, 128 * i : 128 * i + 128]
        return carry

    lax.fori_loop(0, 64 // GROUP, group, 0)

    def coefficient(c, carry):
        plane = ms[pl.ds(pl.multiple_of(c * 64, 64), 64), :]
        plane = jnp.concatenate([plane[:, 0:64], plane[:, 64:128]], axis=0)
        high, low = split(plane)
        both = dot(table, high, ((1,), (1,)))
        result = both[0:80] + both[80:160] + dot(table[0:80], low, ((1,), (1,)))
        for p in range(2):
            for t in range(SLOTS):
                row = 40 * p + 8 * t
                out_ref[pl.ds(p * 128 + t * NC + c, 8, stride=256), :] = result[row : row + 8]
        return carry

    lax.fori_loop(0, NC, coefficient, 0)


def y_forward_kernel(*refs):
    *parts, table_ref, out_ref = refs
    total = parts[0][...]
    for part in parts[1:]:
        total = total + part[...]
    total = jnp.concatenate([total[0:128], total[128:256]], axis=1)
    out_ref[...] = dot(table_ref[...], stacked(total, 1), ((1,), (1,)))


def prepare_kernel(k_ref, r0_ref, r1_ref, coupling_ref, expand_ref, rows_ref, lanes_ref, mask_ref, flip_ref, k_out, c_out):
    exact = lax.Precision.HIGHEST
    for part in range(2):
        for k2 in range(2):
            own = k_ref[part, :, k2].reshape(72, GRID)
            mirror = (r0_ref, r1_ref)[k2][part].reshape(72, GRID)
            mirror = dot(mirror, flip_ref[...], precision=exact)
            if part == 1:
                mirror = -mirror
            both = jnp.concatenate([own, mirror], axis=0).T
            k_out[part, k2 * 64 : k2 * 64 + 64, :] = dot(both, expand_ref[...], precision=exact)
    spread = dot(coupling_ref[...], lanes_ref[...], ((0,), (0,)), precision=exact)
    spread = dot(rows_ref[...], spread, precision=exact) * mask_ref[...]
    high, low = split(spread)
    c_out[...] = jnp.concatenate([high, low, high], axis=0)


def middle_kernel(a_ref, forward_ref, c_ref, k_ref, inverse_ref, out_ref):
    freq = dot(forward_ref[...], stacked(a_ref[...], 0))
    terms = dot(stacked(freq, 1), c_ref[...])
    pieces = []
    for k2 in range(2):
        real = jnp.zeros((64, 128), F32)
        imag = jnp.zeros((64, 128), F32)
        for s in range(ORDER + 1):
            lanes = slice(128 * s, 128 * s + 128)
            tr = terms[k2 * 128 : k2 * 128 + 64, lanes]
            ti = terms[k2 * 128 + 64 : k2 * 128 + 128, lanes]
            kr = k_ref[0, k2 * 64 : k2 * 64 + 64, lanes]
            ki = k_ref[1, k2 * 64 : k2 * 64 + 64, lanes]
            real = real + kr * tr - ki * ti
            imag = imag + kr * ti + ki * tr
        pieces += [real, imag]
    field = jnp.concatenate(pieces, axis=0)
    out_ref[...] = dot(inverse_ref[...], stacked(field, 0))


def y_inverse_kernel(a_ref, table_ref, out_ref):
    result = dot(stacked(a_ref[...].T, 1), table_ref[...])
    out_ref[0:128, :] = result[:, 0:128]
    out_ref[128:256, :] = result[:, 128:256]


def tail_kernel(*refs):
    parts = refs[0:8]
    octant_ref, op_ref, table_ref, out_ref, fs, ws, ls = refs[8:]
    for m in range(8):
        fs[m * 256 : m * 256 + 256, :] = parts[m][...]
    w_cat = load_operators(op_ref, ws)
    ls[pl.ds(NC * 64, 7 * 64), :] = jnp.zeros((7 * 64, 128), F32)
    me = lax.axis_index("narrow")
    table = table_ref[me]

    def coefficient(c, carry):
        rows = []
        for p in range(2):
            for t in range(SLOTS):
                rows.append(fs[pl.ds(p * 128 + t * NC + c, 8, stride=256), :])
        freq = jnp.concatenate(rows, axis=0)
        plane = dot(table, stacked(freq, 0)).T
        ls[pl.ds(pl.multiple_of(c * 64, 64), 64), :] = jnp.concatenate([plane[0:64], plane[64:128]], axis=1)
        return carry

    lax.fori_loop(0, NC, coefficient, 0)

    def group(g, carry):
        b = g * GROUP
        x = jnp.concatenate([ls[pl.ds(b + i, 32, stride=64), :] for i in range(GROUP)], axis=1)
        total = translate(w_cat, x, lane_rows(octant_ref, b, GROUP))
        for i in range(GROUP):
            out_ref[pl.ds(b + i, NC, stride=64), :] = total[0:NC, 128 * i : 128 * i + 128]
        return carry

    lax.fori_loop(0, 64 // GROUP, group, 0)


def call(kernel, out_shape, scratch=(), in_specs=None):
    args = {}
    if in_specs is not None:
        args["in_specs"] = in_specs
    return pl.pallas_call(
        kernel,
        out_shape=out_shape,
        scratch_shapes=list(scratch),
        compiler_params=pltpu.CompilerParams(vmem_limit_bytes=VMEM_LIMIT),
        **args,
    )


def shape(*dims, dtype=F32):
    return jax.ShapeDtypeStruct(dims, dtype)


Z_FORWARD, Z_INVERSE = z_tables()
Y_FORWARD, Y_INVERSE = y_tables()
X_FORWARD, X_INVERSE = x_tables()
EXPAND, ROWS, LANES, MASK, FLIP = expand_tables()


def block_rows(array):
    lead = array.shape[:-2]
    array = array.reshape(lead + (2, 32, 128))
    array = jnp.swapaxes(array, -3, -2)
    return array.reshape(-1, 128)


def swap(array, m):
    return lax.ppermute(array, "narrow", [(i, i ^ m) for i in range(8)])


def shards(leaf_multipoles, leaf_order, subtree_octant, m2m_operators, coupling, kernel_spectrum, l2l_operators):
    leaves = block_rows(leaf_multipoles[0])
    orders = block_rows(leaf_order[0])
    octants = block_rows(subtree_octant[0])
    m2m = jnp.swapaxes(m2m_operators, 0, 1).reshape(NC * 8, NC)
    l2l = jnp.swapaxes(l2l_operators, 0, 1).reshape(NC * 8, NC)
    kernel = kernel_spectrum.transpose(0, 1, 3, 4, 2)

    to_even = [(w * 8 + n, ((32 - w) % 32) * 8 + 7 - n) for w in range(32) for n in range(8)]
    to_odd = [(w * 8 + n, (31 - w) * 8 + 7 - n) for w in range(32) for n in range(8)]
    mirror0 = lax.ppermute(kernel[:, :, 0], ("wide", "narrow"), to_even)
    mirror1 = lax.ppermute(kernel[:, :, 1], ("wide", "narrow"), to_odd)

    vmem = pl.BlockSpec(memory_space=pltpu.VMEM)
    chunks = call(
        head_kernel,
        shape(2048, 128),
        [pltpu.VMEM((2048, 128), F32), pltpu.VMEM((256, 128), F32), pltpu.VMEM((NC * 64, 128), F32), pltpu.SemaphoreType.DMA],
        [pl.BlockSpec(memory_space=pl.ANY)] + [vmem] * 4,
    )(leaves, orders, octants, m2m, jnp.asarray(Z_FORWARD))
    chunks = chunks.reshape(8, 256, 128)
    received = [chunks[0]] + [swap(chunks[m], m) for m in range(1, 8)]

    kernels, couplings = call(prepare_kernel, (shape(2, 128, 640), shape(384, 640, dtype=BF)))(
        kernel, mirror0, mirror1, coupling,
        jnp.asarray(EXPAND), jnp.asarray(ROWS), jnp.asarray(LANES), jnp.asarray(MASK), jnp.asarray(FLIP),
    )

    along = call(y_forward_kernel, shape(256, 128))(*received, jnp.asarray(Y_FORWARD))
    along = lax.all_to_all(along.reshape(32, 8, 128), "wide", split_axis=0, concat_axis=0, tiled=True)
    along = call(middle_kernel, shape(256, 128))(
        along.reshape(256, 128), jnp.asarray(X_FORWARD), couplings, kernels, jnp.asarray(X_INVERSE)
    )
    along = lax.all_to_all(along.reshape(32, 8, 128), "wide", split_axis=0, concat_axis=0, tiled=True)
    plane = call(y_inverse_kernel, shape(256, 128))(along.reshape(256, 128), jnp.asarray(Y_INVERSE))

    planes = [plane] + [swap(plane, m) for m in range(1, 8)]
    children = call(
        tail_kernel,
        shape(NC * 64, 128),
        [pltpu.VMEM((2048, 128), F32), pltpu.VMEM((256, 128), F32), pltpu.VMEM((2048, 128), F32)],
    )(*planes, octants, l2l, jnp.asarray(Z_INVERSE))
    children = children.reshape(NC, 32, 2, 128).swapaxes(1, 2)
    return children.reshape(1, NC, 2, 4096)


def solution(mesh):
    return jax.shard_map(
        shards,
        mesh=mesh,
        in_specs=(
            P("narrow", None, "wide", None),
            P("narrow", "wide", None),
            P("narrow", "wide", None),
            P(),
            P(),
            P(None, None, None, "wide", "narrow"),
            P(),
        ),
        out_specs=P("narrow", None, "wide", None),
        check_vma=False,
    )
```

profile of v0, /device:TPU:2, one launch (start us, length us, event | category | flops | bytes accessed | tf_op | source)
XLA Modules:
  0.0 119.8 jit_solution(16200039807915320707)
XLA Ops:
  0.0 1.1 copy-done
  1.1 1.0 copy-done.8
  2.1 0.8 copy-done.10
  2.9 0.9 copy-done.12
  3.8 0.8 copy-done.16
  4.5 10.7 %shard_map.172 = f32[2048,128]{1,0:T(8,128)S(1)} custom-call(f32[1600,128]{1,0:T(8,128)S(1)} %bitcast.38, s32[64,128]{1,0:T(8,128)S(1)} %bitcast.47, s32[64,128]{1,0:T(8,128)S(1)} %bitcast.43, f32[200,25]{1,0:T(8,128)S(1)} %bitcast.45, bf16[8,160,64]{2,1,0:T(8,128)(2,1)S(1)} %copy-done.8), custom_call_target="tpu_custom_call" | custom-call | tf_op jit(solution)/shard_map/pallas_call | solution.py:337
  15.3 2.4 %collective-permute-start = (f32[256,128]{1,0:T(8,128)S(1)}, f32[256,128]{1,0:T(8,128)S(1)}, u32[]{:S(2)}, u32[]{:S(2)}) collective-permute-start(f32[256,128]{1,0:T(8,128)S(1)} %get-tuple-element.15), channel_id=1, source_target_pairs={{0,1},{1,0},{2,3},{3,2},{4,5},{5,4},{6,7},{7,6},{8,9},{9,8},{10,11... | collective-permute-start | bytes 393224 | tf_op jit(solution)/shard_map/ppermute | solution.py:320
  17.7 1.6 %collective-permute-start.2 = (f32[256,128]{1,0:T(8,128)S(1)}, f32[256,128]{1,0:T(8,128)S(1)}, u32[]{:S(2)}, u32[]{:S(2)}) collective-permute-start(f32[256,128]{1,0:T(8,128)S(1)} %get-tuple-element.13), channel_id=1, source_target_pairs={{0,3},{1,2},{2,1},{3,0},{4,7},{5,6},{6,5},{7,4},{8,11},{9,10},{10,... | collective-permute-start | bytes 393224 | tf_op jit(solution)/shard_map/ppermute | solution.py:320
  19.3 2.9 %collective-permute-start.3 = (f32[256,128]{1,0:T(8,128)S(1)}, f32[256,128]{1,0:T(8,128)S(1)}, u32[]{:S(2)}, u32[]{:S(2)}) collective-permute-start(f32[256,128]{1,0:T(8,128)S(1)} %get-tuple-element.12), channel_id=1, source_target_pairs={{0,4},{1,5},{2,6},{3,7},{4,0},{5,1},{6,2},{7,3},{8,12},{9,13},{10,... | collective-permute-start | bytes 393224 | tf_op jit(solution)/shard_map/ppermute | solution.py:320
  22.1 2.0 %collective-permute-start.4 = (f32[256,128]{1,0:T(8,128)S(1)}, f32[256,128]{1,0:T(8,128)S(1)}, u32[]{:S(2)}, u32[]{:S(2)}) collective-permute-start(f32[256,128]{1,0:T(8,128)S(1)} %get-tuple-element.11), channel_id=1, source_target_pairs={{0,5},{1,4},{2,7},{3,6},{4,1},{5,0},{6,3},{7,2},{8,13},{9,12},{10,... | collective-permute-start | bytes 393224 | tf_op jit(solution)/shard_map/ppermute | solution.py:320
  24.2 1.3 %collective-permute-start.5 = (f32[256,128]{1,0:T(8,128)S(1)}, f32[256,128]{1,0:T(8,128)S(1)}, u32[]{:S(2)}, u32[]{:S(2)}) collective-permute-start(f32[256,128]{1,0:T(8,128)S(1)} %get-tuple-element.10), channel_id=1, source_target_pairs={{0,6},{1,7},{2,4},{3,5},{4,2},{5,3},{6,0},{7,1},{8,14},{9,15},{10,... | collective-permute-start | bytes 393224 | tf_op jit(solution)/shard_map/ppermute | solution.py:320
  25.4 2.7 %collective-permute-done.1.refs_2_ = f32[256,128]{1,0:T(8,128)S(1)} collective-permute-done((f32[256,128]{1,0:T(8,128)S(1)}, f32[256,128]{1,0:T(8,128)S(1)}, u32[]{:S(2)}, u32[]{:S(2)}) %collective-permute-start.1) | collective-permute-done | bytes 131104 | tf_op jit(solution)/shard_map/ppermute | solution.py:320
  28.2 3.8 %collective-permute-start.6 = (f32[256,128]{1,0:T(8,128)S(1)}, f32[256,128]{1,0:T(8,128)S(1)}, u32[]{:S(2)}, u32[]{:S(2)}) collective-permute-start(f32[256,128]{1,0:T(8,128)S(1)} %get-tuple-element.9), channel_id=1, source_target_pairs={{0,7},{1,6},{2,5},{3,4},{4,3},{5,2},{6,1},{7,0},{8,15},{9,14},{10,... | collective-permute-start | bytes 393224 | tf_op jit(solution)/shard_map/ppermute | solution.py:320
  32.0 1.0 collective-permute-done.3.refs_4_
  32.9 2.7 %collective-permute-done.5.refs_6_ = f32[256,128]{1,0:T(8,128)S(1)} collective-permute-done((f32[256,128]{1,0:T(8,128)S(1)}, f32[256,128]{1,0:T(8,128)S(1)}, u32[]{:S(2)}, u32[]{:S(2)}) %collective-permute-start.5) | collective-permute-done | bytes 131104 | tf_op jit(solution)/shard_map/ppermute | solution.py:320
  35.7 0.9 shard_map.173
  36.6 10.6 %all-to-all-start = ((f32[32,8,128]{2,1,0:T(8,128)}), f32[32,8,128]{2,1,0:T(8,128)S(1)}, u32[]{:S(2)}, u32[]{:S(2)}) async-start(f32[32,8,128]{2,1,0:T(8,128)} %bitcast.11), calls=%async_computation | async-start | bytes 262144 | tf_op jit(solution)/shard_map/all_to_all | solution.py:352
  47.2 4.0 %collective-permute-start.7 = (f32[2,9,8,64]{3,2,1,0:T(8,128)S(1)}, f32[2,9,8,64]{3,2,1,0:T(8,128)S(1)}, u32[]{:S(2)}, u32[]{:S(2)}) collective-permute-start(f32[2,9,8,64]{3,2,1,0:T(8,128)S(1)} %get-tuple-element.18), channel_id=1, source_target_pairs={{0,7},{1,6},{2,5},{3,4},{4,3},{5,2},{6,1},{7,0},{8,255},{9,254},{1... | collective-permute-start | bytes 110600 | tf_op jit(solution)/shard_map/ppermute | solution.py:333
  51.3 3.3 %collective-permute-start.8 = (f32[2,9,8,64]{3,2,1,0:T(8,128)S(1)}, f32[2,9,8,64]{3,2,1,0:T(8,128)S(1)}, u32[]{:S(2)}, u32[]{:S(2)}) collective-permute-start(f32[2,9,8,64]{3,2,1,0:T(8,128)S(1)} %get-tuple-element.17), channel_id=1, source_target_pairs={{0,255},{1,254},{2,253},{3,252},{4,251},{5,250},{6,249},{7,248},{8... | collective-permute-start | bytes 110600 | tf_op jit(solution)/shard_map/ppermute | solution.py:334
  54.5 8.2 %collective-permute-done.8.r1_ref = f32[2,9,8,64]{3,2,1,0:T(8,128)S(1)} collective-permute-done((f32[2,9,8,64]{3,2,1,0:T(8,128)S(1)}, f32[2,9,8,64]{3,2,1,0:T(8,128)S(1)}, u32[]{:S(2)}, u32[]{:S(2)}) %collective-permute-start.8) | collective-permute-done | bytes 36896 | tf_op jit(solution)/shard_map/ppermute | solution.py:334
  62.8 2.4 %shard_map.174 = (f32[2,128,640]{2,1,0:T(8,128)S(1)}, bf16[384,640]{1,0:T(8,128)(2,1)S(1)}) custom-call(f32[2,9,2,8,64]{4,3,2,1,0:T(8,128)S(1)} %bitcast.39, f32[2,9,8,64]{3,2,1,0:T(8,128)S(1)} %collective-permute-done.7.r0_ref, f32[2,9,8,64]{3,2,1,0:T(8,128)S(1)} %collective-permute-done.8.r1_ref, f32[25,25]{1,0:T(8,128)S(1)} %copy-done.18, ...), custom_call_target="tpu_custom_call" | custom-call | tf_op jit(solution)/shard_map/pallas_call | solution.py:346
  65.2 0.9 shard_map.175
  66.1 20.9 %all_to_all.10 = f32[32,8,128]{2,1,0:T(8,128)S(1)} all-to-all(f32[32,8,128]{2,1,0:T(8,128)S(1)} %bitcast.41), channel_id=1, replica_groups=mesh['wide'=32,'narrow'=8] {'wide'}, dimensions={0} | all-to-all | bytes 262144 | tf_op jit(solution)/shard_map/all_to_all | solution.py:356
  87.4 2.3 %collective-permute-start.11 = (f32[256,128]{1,0:T(8,128)S(1)}, f32[256,128]{1,0:T(8,128)S(1)}, u32[]{:S(2)}, u32[]{:S(2)}) collective-permute-start(f32[256,128]{1,0:T(8,128)S(1)} %shard_map.176.refs_0_), channel_id=1, source_target_pairs={{0,3},{1,2},{2,1},{3,0},{4,7},{5,6},{6,5},{7,4},{8,11},{9,10},{10,... | collective-permute-start | bytes 393224 | tf_op jit(solution)/shard_map/ppermute | solution.py:320
  89.8 1.1 collective-permute-start.12
  90.9 3.0 %collective-permute-start.13 = (f32[256,128]{1,0:T(8,128)S(1)}, f32[256,128]{1,0:T(8,128)S(1)}, u32[]{:S(2)}, u32[]{:S(2)}) collective-permute-start(f32[256,128]{1,0:T(8,128)S(1)} %shard_map.176.refs_0_), channel_id=1, source_target_pairs={{0,5},{1,4},{2,7},{3,6},{4,1},{5,0},{6,3},{7,2},{8,13},{9,12},{10,... | collective-permute-start | bytes 393224 | tf_op jit(solution)/shard_map/ppermute | solution.py:320
  93.9 1.9 %collective-permute-start.14 = (f32[256,128]{1,0:T(8,128)S(1)}, f32[256,128]{1,0:T(8,128)S(1)}, u32[]{:S(2)}, u32[]{:S(2)}) collective-permute-start(f32[256,128]{1,0:T(8,128)S(1)} %shard_map.176.refs_0_), channel_id=1, source_target_pairs={{0,6},{1,7},{2,4},{3,5},{4,2},{5,3},{6,0},{7,1},{8,14},{9,15},{10,... | collective-permute-start | bytes 393224 | tf_op jit(solution)/shard_map/ppermute | solution.py:320
  95.8 2.6 %collective-permute-done.10.refs_2_ = f32[256,128]{1,0:T(8,128)S(1)} collective-permute-done((f32[256,128]{1,0:T(8,128)S(1)}, f32[256,128]{1,0:T(8,128)S(1)}, u32[]{:S(2)}, u32[]{:S(2)}) %collective-permute-start.10) | collective-permute-done | bytes 131104 | tf_op jit(solution)/shard_map/ppermute | solution.py:320
  98.4 1.2 collective-permute-start.15
  99.6 2.3 %collective-permute-start.9 = (f32[256,128]{1,0:T(8,128)S(1)}, f32[256,128]{1,0:T(8,128)S(1)}, u32[]{:S(2)}, u32[]{:S(2)}) collective-permute-start(f32[256,128]{1,0:T(8,128)S(1)} %shard_map.176.refs_0_), channel_id=1, source_target_pairs={{0,1},{1,0},{2,3},{3,2},{4,5},{5,4},{6,7},{7,6},{8,9},{9,8},{10,11... | collective-permute-start | bytes 393224 | tf_op jit(solution)/shard_map/ppermute | solution.py:320
  102.4 3.6 %collective-permute-done.14.refs_6_ = f32[256,128]{1,0:T(8,128)S(1)} collective-permute-done((f32[256,128]{1,0:T(8,128)S(1)}, f32[256,128]{1,0:T(8,128)S(1)}, u32[]{:S(2)}, u32[]{:S(2)}) %collective-permute-start.14) | collective-permute-done | bytes 131104 | tf_op jit(solution)/shard_map/ppermute | solution.py:320
  106.2 13.6 %shard_map.177 = f32[1600,128]{1,0:T(8,128)} custom-call(f32[256,128]{1,0:T(8,128)S(1)} %shard_map.176.refs_0_, f32[256,128]{1,0:T(8,128)S(1)} %collective-permute-done.9.refs_1_, f32[256,128]{1,0:T(8,128)S(1)} %collective-permute-done.10.refs_2_, f32[256,128]{1,0:T(8,128)S(1)} %collective-permute-done.11.refs_3_, ...), custom_call_target="tpu_custom_call" | custom-call | tf_op jit(solution)/shard_map/pallas_call | solution.py:360
  (50 shorter events, 1.3 us)
Async XLA Ops:
  0.0 1.1 copy-start
  15.2 16.7 %copy-start.1 = (f32[2,9,64,2,8]{2,4,3,1,0:T(8,128)S(1)}, f32[2,9,64,2,8]{2,4,3,1,0:T(8,128)}, u32[]{:S(2)}) copy-start(f32[2,9,64,2,8]{2,4,3,1,0:T(8,128)} %param.23) | copy-start | bytes 221188
  15.2 20.4 %copy-start.3 = (bf16[256,768]{1,0:T(8,128)(2,1)S(1)}, bf16[256,768]{1,0:T(8,128)(2,1)}, u32[]{:S(2)}) copy-start(bf16[256,768]{1,0:T(8,128)(2,1)} %constant.28.clone.refs_8_) | copy-start | bytes 1179652
  15.3 8.8 %collective-permute-start = (f32[256,128]{1,0:T(8,128)S(1)}, f32[256,128]{1,0:T(8,128)S(1)}, u32[]{:S(2)}, u32[]{:S(2)}) collective-permute-start(f32[256,128]{1,0:T(8,128)S(1)} %get-tuple-element.15), channel_id=1, source_target_pairs={{0,1},{1,0},{2,3},{3,2},{4,5},{5,4},{6,7},{7,6},{8,9},{9,8},{10,11... | collective-permute-start | bytes 393224 | tf_op jit(solution)/shard_map/ppermute | solution.py:320
  17.7 10.5 %collective-permute-start.1 = (f32[256,128]{1,0:T(8,128)S(1)}, f32[256,128]{1,0:T(8,128)S(1)}, u32[]{:S(2)}, u32[]{:S(2)}) collective-permute-start(f32[256,128]{1,0:T(8,128)S(1)} %get-tuple-element.14), channel_id=1, source_target_pairs={{0,2},{1,3},{2,0},{3,1},{4,6},{5,7},{6,4},{7,5},{8,10},{9,11},{10,... | collective-permute-start | bytes 393224 | tf_op jit(solution)/shard_map/ppermute | solution.py:320
  17.7 14.3 %collective-permute-start.2 = (f32[256,128]{1,0:T(8,128)S(1)}, f32[256,128]{1,0:T(8,128)S(1)}, u32[]{:S(2)}, u32[]{:S(2)}) collective-permute-start(f32[256,128]{1,0:T(8,128)S(1)} %get-tuple-element.13), channel_id=1, source_target_pairs={{0,3},{1,2},{2,1},{3,0},{4,7},{5,6},{6,5},{7,4},{8,11},{9,10},{10,... | collective-permute-start | bytes 393224 | tf_op jit(solution)/shard_map/ppermute | solution.py:320
  19.3 13.7 %collective-permute-start.3 = (f32[256,128]{1,0:T(8,128)S(1)}, f32[256,128]{1,0:T(8,128)S(1)}, u32[]{:S(2)}, u32[]{:S(2)}) collective-permute-start(f32[256,128]{1,0:T(8,128)S(1)} %get-tuple-element.12), channel_id=1, source_target_pairs={{0,4},{1,5},{2,6},{3,7},{4,0},{5,1},{6,2},{7,3},{8,12},{9,13},{10,... | collective-permute-start | bytes 393224 | tf_op jit(solution)/shard_map/ppermute | solution.py:320
  22.1 10.8 %collective-permute-start.4 = (f32[256,128]{1,0:T(8,128)S(1)}, f32[256,128]{1,0:T(8,128)S(1)}, u32[]{:S(2)}, u32[]{:S(2)}) collective-permute-start(f32[256,128]{1,0:T(8,128)S(1)} %get-tuple-element.11), channel_id=1, source_target_pairs={{0,5},{1,4},{2,7},{3,6},{4,1},{5,0},{6,3},{7,2},{8,13},{9,12},{10,... | collective-permute-start | bytes 393224 | tf_op jit(solution)/shard_map/ppermute | solution.py:320
  24.2 11.5 %collective-permute-start.5 = (f32[256,128]{1,0:T(8,128)S(1)}, f32[256,128]{1,0:T(8,128)S(1)}, u32[]{:S(2)}, u32[]{:S(2)}) collective-permute-start(f32[256,128]{1,0:T(8,128)S(1)} %get-tuple-element.10), channel_id=1, source_target_pairs={{0,6},{1,7},{2,4},{3,5},{4,2},{5,3},{6,0},{7,1},{8,14},{9,15},{10,... | collective-permute-start | bytes 393224 | tf_op jit(solution)/shard_map/ppermute | solution.py:320
  28.2 7.5 %collective-permute-start.6 = (f32[256,128]{1,0:T(8,128)S(1)}, f32[256,128]{1,0:T(8,128)S(1)}, u32[]{:S(2)}, u32[]{:S(2)}) collective-permute-start(f32[256,128]{1,0:T(8,128)S(1)} %get-tuple-element.9), channel_id=1, source_target_pairs={{0,7},{1,6},{2,5},{3,4},{4,3},{5,2},{6,1},{7,0},{8,15},{9,14},{10,... | collective-permute-start | bytes 393224 | tf_op jit(solution)/shard_map/ppermute | solution.py:320
  35.7 27.0 %copy-start.7 = (f32[128,640]{1,0:T(8,128)S(1)}, f32[128,640]{1,0:T(8,128)}, u32[]{:S(2)}) copy-start(f32[128,640]{1,0:T(8,128)} %constant.26.clone.mask_ref) | copy-start | bytes 983044
  36.6 26.1 %copy-start.6 = (f32[144,640]{1,0:T(8,128)S(1)}, f32[144,640]{1,0:T(8,128)}, u32[]{:S(2)}) copy-start(f32[144,640]{1,0:T(8,128)} %constant.23.clone.expand_ref) | copy-start | bytes 1105924
  36.6 28.6 %all-to-all-start = ((f32[32,8,128]{2,1,0:T(8,128)}), f32[32,8,128]{2,1,0:T(8,128)S(1)}, u32[]{:S(2)}, u32[]{:S(2)}) async-start(f32[32,8,128]{2,1,0:T(8,128)} %bitcast.11), calls=%async_computation | async-start | bytes 262144 | tf_op jit(solution)/shard_map/all_to_all | solution.py:352
  47.2 15.5 %copy-start.14 = (f32[25,640]{1,0:T(8,128)S(1)}, f32[25,640]{1,0:T(8,128)}, u32[]{:S(2)}) copy-start(f32[25,640]{1,0:T(8,128)} %constant.25.clone.lanes_ref) | copy-start | bytes 192004
  47.2 15.5 %copy-start.15 = (f32[128,25]{1,0:T(8,128)S(1)}, f32[128,25]{1,0:T(8,128)}, u32[]{:S(2)}) copy-start(f32[128,25]{1,0:T(8,128)} %constant.24.clone.rows_ref) | copy-start | bytes 38404
  47.2 15.5 %copy-start.17 = (f32[64,64]{1,0:T(8,128)S(1)}, f32[64,64]{1,0:T(8,128)}, u32[]{:S(2)}) copy-start(f32[64,64]{1,0:T(8,128)} %constant.27.clone.flip_ref) | copy-start | bytes 49156
  47.2 15.5 %copy-start.18 = (f32[25,25]{1,0:T(8,128)S(1)}, f32[25,25]{1,0:T(8,128)}, u32[]{:S(2)}) copy-start(f32[25,25]{1,0:T(8,128)} %coupling_ref.1) | copy-start | bytes 7504
  47.2 7.3 %collective-permute-start.7 = (f32[2,9,8,64]{3,2,1,0:T(8,128)S(1)}, f32[2,9,8,64]{3,2,1,0:T(8,128)S(1)}, u32[]{:S(2)}, u32[]{:S(2)}) collective-permute-start(f32[2,9,8,64]{3,2,1,0:T(8,128)S(1)} %get-tuple-element.18), channel_id=1, source_target_pairs={{0,7},{1,6},{2,5},{3,4},{4,3},{5,2},{6,1},{7,0},{8,255},{9,254},{1... | collective-permute-start | bytes 110600 | tf_op jit(solution)/shard_map/ppermute | solution.py:333
  51.3 11.4 %collective-permute-start.8 = (f32[2,9,8,64]{3,2,1,0:T(8,128)S(1)}, f32[2,9,8,64]{3,2,1,0:T(8,128)S(1)}, u32[]{:S(2)}, u32[]{:S(2)}) collective-permute-start(f32[2,9,8,64]{3,2,1,0:T(8,128)S(1)} %get-tuple-element.17), channel_id=1, source_target_pairs={{0,255},{1,254},{2,253},{3,252},{4,251},{5,250},{6,249},{7,248},{8... | collective-permute-start | bytes 110600 | tf_op jit(solution)/shard_map/ppermute | solution.py:334
  62.7 2.5 %copy-start.4 = (bf16[256,768]{1,0:T(8,128)(2,1)S(1)}, bf16[256,768]{1,0:T(8,128)(2,1)}, u32[]{:S(2)}) copy-start(bf16[256,768]{1,0:T(8,128)(2,1)} %constant.29.clone.forward_ref) | copy-start | bytes 1179652
  62.8 2.5 %copy-start.5 = (bf16[256,768]{1,0:T(8,128)(2,1)S(1)}, bf16[256,768]{1,0:T(8,128)(2,1)}, u32[]{:S(2)}) copy-start(bf16[256,768]{1,0:T(8,128)(2,1)} %constant.30.clone.inverse_ref) | copy-start | bytes 1179652
  65.2 21.8 %copy-start.2 = (bf16[768,256]{1,0:T(8,128)(2,1)S(1)}, bf16[768,256]{1,0:T(8,128)(2,1)}, u32[]{:S(2)}) copy-start(bf16[768,256]{1,0:T(8,128)(2,1)} %constant.31.clone.table_ref) | copy-start | bytes 1179652
  87.1 19.2 %copy-start.9 = (bf16[8,64,240]{2,1,0:T(8,128)(2,1)S(1)}, bf16[8,64,240]{2,1,0:T(8,128)(2,1)}, u32[]{:S(2)}) copy-start(bf16[8,64,240]{2,1,0:T(8,128)(2,1)} %constant.32.clone.refs_10_) | copy-start | bytes 737284
  87.1 19.2 %copy-start.11 = (s32[1,2,4096]{2,1,0:T(2,128)S(1)}, s32[1,2,4096]{2,1,0:T(2,128)}, u32[]{:S(2)}) copy-start(s32[1,2,4096]{2,1,0:T(2,128)} %param.20) | copy-start | bytes 98308
  87.1 19.2 %copy-start.13 = (f32[8,25,25]{2,0,1:T(8,128)S(1)}, f32[8,25,25]{2,0,1:T(8,128)}, u32[]{:S(2)}) copy-start(f32[8,25,25]{2,0,1:T(8,128)} %param.24) | copy-start | bytes 60004
  87.3 11.0 %collective-permute-start.10 = (f32[256,128]{1,0:T(8,128)S(1)}, f32[256,128]{1,0:T(8,128)S(1)}, u32[]{:S(2)}, u32[]{:S(2)}) collective-permute-start(f32[256,128]{1,0:T(8,128)S(1)} %shard_map.176.refs_0_), channel_id=1, source_target_pairs={{0,2},{1,3},{2,0},{3,1},{4,6},{5,7},{6,4},{7,5},{8,10},{9,11},{10,... | collective-permute-start | bytes 393224 | tf_op jit(solution)/shard_map/ppermute | solution.py:320
  87.4 12.1 %collective-permute-start.11 = (f32[256,128]{1,0:T(8,128)S(1)}, f32[256,128]{1,0:T(8,128)S(1)}, u32[]{:S(2)}, u32[]{:S(2)}) collective-permute-start(f32[256,128]{1,0:T(8,128)S(1)} %shard_map.176.refs_0_), channel_id=1, source_target_pairs={{0,3},{1,2},{2,1},{3,0},{4,7},{5,6},{6,5},{7,4},{8,11},{9,10},{10,... | collective-permute-start | bytes 393224 | tf_op jit(solution)/shard_map/ppermute | solution.py:320
  89.8 12.6 %collective-permute-start.12 = (f32[256,128]{1,0:T(8,128)S(1)}, f32[256,128]{1,0:T(8,128)S(1)}, u32[]{:S(2)}, u32[]{:S(2)}) collective-permute-start(f32[256,128]{1,0:T(8,128)S(1)} %shard_map.176.refs_0_), channel_id=1, source_target_pairs={{0,4},{1,5},{2,6},{3,7},{4,0},{5,1},{6,2},{7,3},{8,12},{9,13},{10,... | collective-permute-start | bytes 393224 | tf_op jit(solution)/shard_map/ppermute | solution.py:320
  90.9 11.5 %collective-permute-start.13 = (f32[256,128]{1,0:T(8,128)S(1)}, f32[256,128]{1,0:T(8,128)S(1)}, u32[]{:S(2)}, u32[]{:S(2)}) collective-permute-start(f32[256,128]{1,0:T(8,128)S(1)} %shard_map.176.refs_0_), channel_id=1, source_target_pairs={{0,5},{1,4},{2,7},{3,6},{4,1},{5,0},{6,3},{7,2},{8,13},{9,12},{10,... | collective-permute-start | bytes 393224 | tf_op jit(solution)/shard_map/ppermute | solution.py:320
  93.9 12.1 %collective-permute-start.14 = (f32[256,128]{1,0:T(8,128)S(1)}, f32[256,128]{1,0:T(8,128)S(1)}, u32[]{:S(2)}, u32[]{:S(2)}) collective-permute-start(f32[256,128]{1,0:T(8,128)S(1)} %shard_map.176.refs_0_), channel_id=1, source_target_pairs={{0,6},{1,7},{2,4},{3,5},{4,2},{5,3},{6,0},{7,1},{8,14},{9,15},{10,... | collective-permute-start | bytes 393224 | tf_op jit(solution)/shard_map/ppermute | solution.py:320
  98.4 7.6 %collective-permute-start.15 = (f32[256,128]{1,0:T(8,128)S(1)}, f32[256,128]{1,0:T(8,128)S(1)}, u32[]{:S(2)}, u32[]{:S(2)}) collective-permute-start(f32[256,128]{1,0:T(8,128)S(1)} %shard_map.176.refs_0_), channel_id=1, source_target_pairs={{0,7},{1,6},{2,5},{3,4},{4,3},{5,2},{6,1},{7,0},{8,15},{9,14},{10,... | collective-permute-start | bytes 393224 | tf_op jit(solution)/shard_map/ppermute | solution.py:320
  99.6 6.7 %collective-permute-start.9 = (f32[256,128]{1,0:T(8,128)S(1)}, f32[256,128]{1,0:T(8,128)S(1)}, u32[]{:S(2)}, u32[]{:S(2)}) collective-permute-start(f32[256,128]{1,0:T(8,128)S(1)} %shard_map.176.refs_0_), channel_id=1, source_target_pairs={{0,1},{1,0},{2,3},{3,2},{4,5},{5,4},{6,7},{7,6},{8,9},{9,8},{10,11... | collective-permute-start | bytes 393224 | tf_op jit(solution)/shard_map/ppermute | solution.py:320
  (4 other events, 3.4 us)
where the time goes:
time: 120 us
  starting transfers between devices  43.6 us (36%)
  Pallas kernels  28.8 us (24%)
  waiting for transfers between devices  21.5 us (18%)
  blocking collectives  20.9 us (17%)
  local copies, waits for them, and re-layouts  4.7 us (4%)
    ppermute x14, starting transfers between devices, swap(): return lax.ppermute(array, 'narrow', [(i, i ^ m) for i in range(8)])  25.8 us
    all_to_all x1, blocking collectives, shards(): lax.all_to_all(along.reshape(32, 8, 128), 'wide', split_axis=0, concat_ax...  20.9 us
    pallas_call x1, Pallas kernels, shards(): call(tail_kernel, shape(NC * 64, 128), [pltpu.VMEM((2048, 128), F32), plt...  13.6 us
    ppermute x14, waiting for transfers between devices, swap(): return lax.ppermute(array, 'narrow', [(i, i ^ m) for i in range(8)])  13.4 us
    pallas_call x1, Pallas kernels, shards(): call(head_kernel, shape(2048, 128), [pltpu.VMEM((2048, 128), F32), pltpu....  10.7 us
    all_to_all x1, starting transfers between devices, shards(): lax.all_to_all(along.reshape(32, 8, 128), 'wide', split_axis=0, concat_ax...  10.6 us
    ppermute x1, waiting for transfers between devices, shards(): mirror1 = lax.ppermute(kernel[:, :, 1], ('wide', 'narrow'), to_odd)  8.15 us
    unnamed x39, local copies, waits for them, and re-layouts  4.61 us
  transfers between devices with their start and end apart: 17, of which 8 were waited for; matrix products, arithmetic and copies ran while one was open for 0% of the time, Pallas kernels for 2%

commit v1 on v0

--- a/solution.py
+++ b/solution.py
@@ -16,6 +16,8 @@
 F32 = jnp.float32
 VMEM_LIMIT = 48 * 1024 * 1024
 
+STEPS = ((0, 0), (2, 0), (1, 0), (-1, 0), (0, 1), (2, 1), (1, 1), (-1, 1))
+
 DEGREE = np.array([n for n in range(ORDER + 1) for _ in range(2 * n + 1)])
 
 
@@ -44,19 +46,21 @@
     return np.stack([np.stack([cosine, -sign * sine]), np.stack([sign * sine, cosine])])
 
 
+def stepped(n, step, sign):
+    return (n // 2 + sign * step[0]) % 4 * 2 + (n + step[1]) % 2
+
+
 def z_tables():
     z = np.arange(GRID)
     forward, inverse = [], []
     for n in range(8):
-        rows = []
-        for t in range(SLOTS):
-            for m in range(8):
-                rows.append(8 * (n ^ m) + t)
-        cosine, sine = wave(np.array(rows)[:, None], z[None, :])
-        table = np.concatenate([cosine, -sine], axis=0)
-        high, low = halves(table)
-        forward.append(np.concatenate([high, low], axis=0))
-        inverse.append(stack_left(table.T / GRID))
+        tables = []
+        for sign in (1, -1):
+            rows = [8 * stepped(n, step, sign) + t for t in range(SLOTS) for step in STEPS]
+            cosine, sine = wave(np.array(rows)[:, None], z[None, :])
+            tables.append(np.concatenate([cosine, -sine], axis=0))
+        forward.append(stack_left(tables[0]))
+        inverse.append(stack_left(tables[1].T / GRID))
     return np.stack(forward), np.stack(inverse)
 
 
@@ -161,19 +165,24 @@
     return total
 
 
-GROUP = 4
-
-
-def head_kernel(leaf_ref, order_ref, octant_ref, op_ref, table_ref, out_ref, xs, ws, ms, sem):
-    copy = pltpu.make_async_copy(leaf_ref, xs.at[pl.ds(0, NC * 64)], sem)
-    copy.start()
+GROUP = 8
+BATCH = 5
+
+
+def head_kernel(leaf_hbm, order_hbm, octant_hbm, op_hbm, ms, xs, order_ref, octant_ref, op_ref, ws, sems):
+    copies = [
+        pltpu.make_async_copy(op_hbm, op_ref, sems.at[0]),
+        pltpu.make_async_copy(leaf_hbm, xs.at[pl.ds(0, NC * 64)], sems.at[1]),
+        pltpu.make_async_copy(order_hbm, order_ref, sems.at[2]),
+        pltpu.make_async_copy(octant_hbm, octant_ref, sems.at[3]),
+    ]
+    for copy in copies:
+        copy.start()
+    copies[0].wait()
     w_cat = load_operators(op_ref, ws)
     degree = degree_column()
-    me = lax.axis_index("narrow")
-    table = table_ref[me]
-    for m in range(16):
-        out_ref[m * 128 + 120 : m * 128 + 128, :] = jnp.zeros((8, 128), F32)
-    copy.wait()
+    for copy in copies[1:]:
+        copy.wait()
 
     def group(g, carry):
         b = g * GROUP
@@ -186,23 +195,35 @@
 
     lax.fori_loop(0, 64 // GROUP, group, 0)
 
-    def coefficient(c, carry):
-        plane = ms[pl.ds(pl.multiple_of(c * 64, 64), 64), :]
-        plane = jnp.concatenate([plane[:, 0:64], plane[:, 64:128]], axis=0)
-        high, low = split(plane)
-        both = dot(table, high, ((1,), (1,)))
-        result = both[0:80] + both[80:160] + dot(table[0:80], low, ((1,), (1,)))
-        for p in range(2):
-            for t in range(SLOTS):
-                row = 40 * p + 8 * t
-                out_ref[pl.ds(p * 128 + t * NC + c, 8, stride=256), :] = result[row : row + 8]
+
+def z_forward_kernel(ms, table_ref, _0, _1, out_ref):
+    me = lax.axis_index("narrow")
+    table = table_ref[me]
+    for m in range(16):
+        out_ref[m * 128 + 120 : m * 128 + 128, :] = jnp.zeros((8, 128), F32)
+
+    def coefficients(g, carry):
+        first = g * BATCH
+        rows = pl.ds(pl.multiple_of(first * 64, 64), 64 * BATCH)
+        pieces = []
+        for part in split(ms[rows, :]):
+            halves_ = [part[64 * i : 64 * i + 64, 64 * y2 : 64 * y2 + 64] for i in range(BATCH) for y2 in range(2)]
+            pieces.append(jnp.concatenate(halves_, axis=0))
+        high, low = pieces
+        result = dot(table, jnp.concatenate([high, high, low], axis=1), ((1,), (1,)))
+        for i in range(BATCH):
+            for p in range(2):
+                for t in range(SLOTS):
+                    row = 40 * p + 8 * t
+                    value = result[row : row + 8, 128 * i : 128 * i + 128]
+                    out_ref[pl.ds(p * 128 + t * NC + first + i, 8, stride=256), :] = value
         return carry
 
-    lax.fori_loop(0, NC, coefficient, 0)
+    lax.fori_loop(0, NC // BATCH, coefficients, 0)
 
 
 def y_forward_kernel(*refs):
-    *parts, table_ref, out_ref = refs
+    *parts, table_ref, _, out_ref = refs
     total = parts[0][...]
     for part in parts[1:]:
         total = total + part[...]
@@ -253,27 +274,36 @@
     out_ref[128:256, :] = result[:, 128:256]
 
 
-def tail_kernel(*refs):
+def z_inverse_kernel(*refs):
     parts = refs[0:8]
-    octant_ref, op_ref, table_ref, out_ref, fs, ws, ls = refs[8:]
+    table_ref, ls, fs = refs[8:]
     for m in range(8):
         fs[m * 256 : m * 256 + 256, :] = parts[m][...]
-    w_cat = load_operators(op_ref, ws)
     ls[pl.ds(NC * 64, 7 * 64), :] = jnp.zeros((7 * 64, 128), F32)
     me = lax.axis_index("narrow")
     table = table_ref[me]
 
-    def coefficient(c, carry):
-        rows = []
-        for p in range(2):
-            for t in range(SLOTS):
-                rows.append(fs[pl.ds(p * 128 + t * NC + c, 8, stride=256), :])
-        freq = jnp.concatenate(rows, axis=0)
-        plane = dot(table, stacked(freq, 0)).T
-        ls[pl.ds(pl.multiple_of(c * 64, 64), 64), :] = jnp.concatenate([plane[0:64], plane[64:128]], axis=1)
+    def coefficients(g, carry):
+        first = g * BATCH
+        freqs = []
+        for i in range(BATCH):
+            rows = []
+            for p in range(2):
+                for t in range(SLOTS):
+                    rows.append(fs[pl.ds(p * 128 + t * NC + first + i, 8, stride=256), :])
+            freqs.append(jnp.concatenate(rows, axis=0))
+        result = dot(table, stacked(jnp.concatenate(freqs, axis=1), 0))
+        for i in range(BATCH):
+            plane = result[:, 128 * i : 128 * i + 128].T
+            rows = pl.ds(pl.multiple_of((first + i) * 64, 64), 64)
+            ls[rows, :] = jnp.concatenate([plane[0:64], plane[64:128]], axis=1)
         return carry
 
-    lax.fori_loop(0, NC, coefficient, 0)
+    lax.fori_loop(0, NC // BATCH, coefficients, 0)
+
+
+def tail_kernel(ls, octant_ref, op_ref, out_ref, ws):
+    w_cat = load_operators(op_ref, ws)
 
     def group(g, carry):
         b = g * GROUP
@@ -316,8 +346,8 @@
     return array.reshape(-1, 128)
 
 
-def swap(array, m):
-    return lax.ppermute(array, "narrow", [(i, i ^ m) for i in range(8)])
+def shift(array, step):
+    return lax.ppermute(array, "narrow", [(n, stepped(n, step, 1)) for n in range(8)])
 
 
 def shards(leaf_multipoles, leaf_order, subtree_octant, m2m_operators, coupling, kernel_spectrum, l2l_operators):
@@ -333,22 +363,34 @@
     mirror0 = lax.ppermute(kernel[:, :, 0], ("wide", "narrow"), to_even)
     mirror1 = lax.ppermute(kernel[:, :, 1], ("wide", "narrow"), to_odd)
 
-    vmem = pl.BlockSpec(memory_space=pltpu.VMEM)
     chunks = call(
         head_kernel,
-        shape(2048, 128),
-        [pltpu.VMEM((2048, 128), F32), pltpu.VMEM((256, 128), F32), pltpu.VMEM((NC * 64, 128), F32), pltpu.SemaphoreType.DMA],
-        [pl.BlockSpec(memory_space=pl.ANY)] + [vmem] * 4,
-    )(leaves, orders, octants, m2m, jnp.asarray(Z_FORWARD))
+        shape(NC * 64, 128),
+        [
+            pltpu.VMEM((2048, 128), F32),
+            pltpu.VMEM((64, 128), jnp.int32),
+            pltpu.VMEM((64, 128), jnp.int32),
+            pltpu.VMEM((NC * 8, NC), F32),
+            pltpu.VMEM((256, 128), F32),
+            pltpu.SemaphoreType.DMA((4,)),
+        ],
+        [pl.BlockSpec(memory_space=pltpu.HBM)] * 4,
+    )(leaves, orders, octants, m2m)
+    whole = pl.BlockSpec(memory_space=pltpu.VMEM)
+    anywhere = pl.BlockSpec(memory_space=pl.ANY)
+    chunks = call(z_forward_kernel, shape(2048, 128), (), [whole] * 2 + [anywhere] * 2)(
+        chunks, jnp.asarray(Z_FORWARD), mirror0, mirror1
+    )
     chunks = chunks.reshape(8, 256, 128)
-    received = [chunks[0]] + [swap(chunks[m], m) for m in range(1, 8)]
+    across = chunks[4] + sum(shift(chunks[4 + m], STEPS[m]) for m in (1, 2, 3))
+    received = [chunks[0]] + [shift(chunks[m], STEPS[m]) for m in (1, 2, 3)] + [shift(across, STEPS[4])]
 
     kernels, couplings = call(prepare_kernel, (shape(2, 128, 640), shape(384, 640, dtype=BF)))(
         kernel, mirror0, mirror1, coupling,
         jnp.asarray(EXPAND), jnp.asarray(ROWS), jnp.asarray(LANES), jnp.asarray(MASK), jnp.asarray(FLIP),
     )
 
-    along = call(y_forward_kernel, shape(256, 128))(*received, jnp.asarray(Y_FORWARD))
+    along = call(y_forward_kernel, shape(256, 128), (), [whole] * 6 + [anywhere])(*received, jnp.asarray(Y_FORWARD), kernels)
     along = lax.all_to_all(along.reshape(32, 8, 128), "wide", split_axis=0, concat_axis=0, tiled=True)
     along = call(middle_kernel, shape(256, 128))(
         along.reshape(256, 128), jnp.asarray(X_FORWARD), couplings, kernels, jnp.asarray(X_INVERSE)
@@ -356,12 +398,11 @@
     along = lax.all_to_all(along.reshape(32, 8, 128), "wide", split_axis=0, concat_axis=0, tiled=True)
     plane = call(y_inverse_kernel, shape(256, 128))(along.reshape(256, 128), jnp.asarray(Y_INVERSE))
 
-    planes = [plane] + [swap(plane, m) for m in range(1, 8)]
-    children = call(
-        tail_kernel,
-        shape(NC * 64, 128),
-        [pltpu.VMEM((2048, 128), F32), pltpu.VMEM((256, 128), F32), pltpu.VMEM((2048, 128), F32)],
-    )(*planes, octants, l2l, jnp.asarray(Z_INVERSE))
+    other = shift(plane, STEPS[4])
+    planes = [plane] + [shift(plane, STEPS[m]) for m in (1, 2, 3)]
+    planes += [other] + [shift(other, STEPS[m]) for m in (1, 2, 3)]
+    local = call(z_inverse_kernel, shape(2048, 128), [pltpu.VMEM((2048, 128), F32)])(*planes, jnp.asarray(Z_INVERSE))
+    children = call(tail_kernel, shape(NC * 64, 128), [pltpu.VMEM((256, 128), F32)])(local, octants, l2l)
     children = children.reshape(NC, 32, 2, 128).swapaxes(1, 2)
     return children.reshape(1, NC, 2, 4096)
 

time: 120 us -> 101 us (0.84)
  starting transfers between devices: 43.6 us -> 27.3 us
  Pallas kernels: 28.8 us -> 15.5 us
  blocking collectives: 20.9 us -> 33.6 us
  local copies, waits for them, and re-layouts: 4.7 us -> 2.19 us
    pallas_call x3 -> x5, Pallas kernels: 25.3 us -> 12 us  [the longest x1 3.76 us: shards(): call(tail_kernel, shape(NC * 64, 128), [pltpu.VMEM((256, 128), F32)])]
    all_to_all x1 -> x2, blocking collectives: 20.9 us -> 33.6 us  [shards(): lax.all_to_all(along.reshape(32, 8, 128), 'wide', split_axis=0, concat_ax...]
    all_to_all x1 -> x0, starting transfers between devices: 10.6 us -> none  [shards(): lax.all_to_all(along.reshape(32, 8, 128), 'wide', split_axis=0, concat_ax...]
    ppermute x14, starting transfers between devices: 25.8 us -> 17.1 us  [shift(): lax.ppermute(array, 'narrow', [(n, stepped(n, step, 1)) for n in range(8)])]
    ppermute x14, waiting for transfers between devices: 13.4 us -> 21.7 us  [shift(): lax.ppermute(array, 'narrow', [(n, stepped(n, step, 1)) for n in range(8)])]
    ppermute x1, waiting for transfers between devices: 8.15 us -> 0.01 us  [shards(): mirror1 = lax.ppermute(kernel[:, :, 1], ('wide', 'narrow'), to_odd)]
    ppermute x1, starting transfers between devices: 3.27 us -> 8.76 us  [shards(): mirror1 = lax.ppermute(kernel[:, :, 1], ('wide', 'narrow'), to_odd)]
    ppermute x1, starting transfers between devices: 4.02 us -> 1.46 us  [shards(): mirror0 = lax.ppermute(kernel[:, :, 0], ('wide', 'narrow'), to_even)]
  transfers between devices with their start and end apart: 17 -> 16, of which waited for: 8 -> 10; matrix products, arithmetic and copies ran while one was open for 0% -> 0% of each run, Pallas kernels for 2% -> 6%
where the time goes in v1:
time: 101 us
  blocking collectives  33.6 us (33%)
  starting transfers between devices  27.3 us (27%)
  waiting for transfers between devices  22.3 us (22%)
  Pallas kernels  15.5 us (15%)
  local copies, waits for them, and re-layouts  2.19 us (2%)
    all_to_all x2, blocking collectives, shards(): lax.all_to_all(along.reshape(32, 8, 128), 'wide', split_axis=0, concat_ax...  33.6 us
    ppermute x14, waiting for transfers between devices, shift(): lax.ppermute(array, 'narrow', [(n, stepped(n, step, 1)) for n in range(8)])  21.7 us
    ppermute x14, starting transfers between devices, shift(): lax.ppermute(array, 'narrow', [(n, stepped(n, step, 1)) for n in range(8)])  17.1 us
    ppermute x1, starting transfers between devices, shards(): mirror1 = lax.ppermute(kernel[:, :, 1], ('wide', 'narrow'), to_odd)  8.76 us
    pallas_call x1, Pallas kernels, shards(): call(tail_kernel, shape(NC * 64, 128), [pltpu.VMEM((256, 128), F32)])  3.76 us
    pallas_call x1, Pallas kernels, shards(): call(head_kernel, shape(NC * 64, 128), [pltpu.VMEM((2048, 128), F32), plt...  3.25 us
    pallas_call x1, Pallas kernels, shards(): call(z_inverse_kernel, shape(2048, 128), [pltpu.VMEM((2048, 128), F32)])  2.44 us
    pallas_call x1, Pallas kernels, shards(): call(prepare_kernel, (shape(2, 128, 640), shape(384, 640, dtype=BF)))  2.42 us
  transfers between devices with their start and end apart: 16, of which 10 were waited for; matrix products, arithmetic and copies ran while one was open for 0% of the time, Pallas kernels for 6%

profile of v1, /device:TPU:2, one launch (start us, length us, event | category | flops | bytes accessed | tf_op | source)
XLA Modules:
  0.0 101.1 jit_solution(7983124758015432408)
XLA Ops:
  0.0 0.9 copy.27
  1.0 8.8 %collective-permute-start.1 = (f32[2,9,8,64]{3,2,1,0:T(8,128)S(1)}, f32[2,9,8,64]{3,2,1,0:T(8,128)S(1)}, u32[]{:S(2)}, u32[]{:S(2)}) collective-permute-start(f32[2,9,8,64]{3,2,1,0:T(8,128)S(1)} %get-tuple-element.17), channel_id=1, source_target_pairs={{0,255},{1,254},{2,253},{3,252},{4,251},{5,250},{6,249},{7,248},{8... | collective-permute-start | bytes 110600 | tf_op jit(solution)/shard_map/ppermute | solution.py:364
  9.7 1.5 %collective-permute-start = (f32[2,9,8,64]{3,2,1,0:T(8,128)S(1)}, f32[2,9,8,64]{3,2,1,0:T(8,128)S(1)}, u32[]{:S(2)}, u32[]{:S(2)}) collective-permute-start(f32[2,9,8,64]{3,2,1,0:T(8,128)S(1)} %get-tuple-element.18), channel_id=1, source_target_pairs={{0,7},{1,6},{2,5},{3,4},{4,3},{5,2},{6,1},{7,0},{8,255},{9,254},{1... | collective-permute-start | bytes 110600 | tf_op jit(solution)/shard_map/ppermute | solution.py:363
  11.2 1.1 %copy-done = f32[1,25,2,4096]{3,2,1,0:T(2,128)S(1)} copy-done((f32[1,25,2,4096]{3,2,1,0:T(2,128)S(1)}, f32[1,25,2,4096]{3,2,1,0:T(2,128)}, u32[]{:S(2)}) %copy-start) | copy-done | bytes 819224
  12.4 3.2 %shard_map.172.ms = f32[1600,128]{1,0:T(8,128)S(1)} custom-call(f32[1600,128]{1,0:T(8,128)S(1)} %bitcast.38, s32[64,128]{1,0:T(8,128)S(1)} %bitcast.48, s32[64,128]{1,0:T(8,128)S(1)} %bitcast.44, f32[200,25]{1,0:T(8,128)S(1)} %bitcast.46), custom_call_target="tpu_custom_call" | custom-call | tf_op jit(solution)/shard_map/pallas_call | solution.py:366
  15.6 0.6 collective-permute-done._0.r0_ref
  16.2 2.3 %shard_map.173 = f32[2048,128]{1,0:T(8,128)S(1)} custom-call(f32[1600,128]{1,0:T(8,128)S(1)} %shard_map.172.ms, bf16[8,80,192]{2,1,0:T(8,128)(2,1)S(1)} %copy-done.8, f32[2,9,8,64]{3,2,1,0:T(8,128)S(1)} %collective-permute-done._0.r0_ref, f32[2,9,8,64]{3,2,1,0:T(8,128)S(1)} %collective-permute-done.1._1.r1_ref), custom_call_target="tpu_custom_call" | custom-call | tf_op jit(solution)/shard_map/pallas_call | solution.py:381
  18.6 3.2 %collective-permute-start.7 = (f32[256,128]{1,0:T(8,128)S(1)}, f32[256,128]{1,0:T(8,128)S(1)}, u32[]{:S(2)}, u32[]{:S(2)}) collective-permute-start(f32[256,128]{1,0:T(8,128)S(1)} %get-tuple-element.15), channel_id=1, source_target_pairs={{0,6},{1,7},{2,0},{3,1},{4,2},{5,3},{6,4},{7,5},{8,14},{9,15},{10,... | collective-permute-start | bytes 393224 | tf_op jit(solution)/shard_map/ppermute | solution.py:350
  21.9 0.8 collective-permute-start.5
  22.6 2.9 %collective-permute-done.6 = f32[256,128]{1,0:T(8,128)S(1)} collective-permute-done((f32[256,128]{1,0:T(8,128)S(1)}, f32[256,128]{1,0:T(8,128)S(1)}, u32[]{:S(2)}, u32[]{:S(2)}) %collective-permute-start.6) | collective-permute-done | bytes 131104 | tf_op jit(solution)/shard_map/ppermute | solution.py:350
  25.5 2.5 %collective-permute-done.7 = f32[256,128]{1,0:T(8,128)S(1)} collective-permute-done((f32[256,128]{1,0:T(8,128)S(1)}, f32[256,128]{1,0:T(8,128)S(1)}, u32[]{:S(2)}, u32[]{:S(2)}) %collective-permute-start.7) | collective-permute-done | bytes 131104 | tf_op jit(solution)/shard_map/ppermute | solution.py:350
  28.1 1.6 %collective-permute-done.5 = f32[256,128]{1,0:T(8,128)S(1)} collective-permute-done((f32[256,128]{1,0:T(8,128)S(1)}, f32[256,128]{1,0:T(8,128)S(1)}, u32[]{:S(2)}, u32[]{:S(2)}) %collective-permute-start.5) | collective-permute-done | bytes 131104 | tf_op jit(solution)/shard_map/ppermute | solution.py:350
  29.8 0.6 collective-permute-start.8
  30.4 2.7 %collective-permute-start.4 = (f32[256,128]{1,0:T(8,128)S(1)}, f32[256,128]{1,0:T(8,128)S(1)}, u32[]{:S(2)}, u32[]{:S(2)}) collective-permute-start(f32[256,128]{1,0:T(8,128)S(1)} %get-tuple-element.10), channel_id=1, source_target_pairs={{0,6},{1,7},{2,0},{3,1},{4,2},{5,3},{6,4},{7,5},{8,14},{9,15},{10,... | collective-permute-start | bytes 393224 | tf_op jit(solution)/shard_map/ppermute | solution.py:350
  33.1 1.5 %collective-permute-start.2 = (f32[256,128]{1,0:T(8,128)S(1)}, f32[256,128]{1,0:T(8,128)S(1)}, u32[]{:S(2)}, u32[]{:S(2)}) collective-permute-start(f32[256,128]{1,0:T(8,128)S(1)} %get-tuple-element.12), channel_id=1, source_target_pairs={{0,4},{1,5},{2,6},{3,7},{4,0},{5,1},{6,2},{7,3},{8,12},{9,13},{10,... | collective-permute-start | bytes 393224 | tf_op jit(solution)/shard_map/ppermute | solution.py:350
  34.6 2.4 %shard_map.174 = (f32[2,128,640]{2,1,0:T(8,128)S(1)}, bf16[384,640]{1,0:T(8,128)(2,1)S(1)}) custom-call(f32[2,9,2,8,64]{4,3,2,1,0:T(8,128)S(1)} %bitcast.39, f32[2,9,8,64]{3,2,1,0:T(8,128)S(1)} %collective-permute-done._0.r0_ref, f32[2,9,8,64]{3,2,1,0:T(8,128)S(1)} %collective-permute-done.1._1.r1_ref, f32[25,25]{1,0:T(8,128)S(1)} %copy-done.17, ...), custom_call_target="tpu_custom_call" | custom-call | tf_op jit(solution)/shard_map/pallas_call | solution.py:388
  37.1 5.8 %collective-permute-done.3.refs_2_ = f32[256,128]{1,0:T(8,128)S(1)} collective-permute-done((f32[256,128]{1,0:T(8,128)S(1)}, f32[256,128]{1,0:T(8,128)S(1)}, u32[]{:S(2)}, u32[]{:S(2)}) %collective-permute-start.3) | collective-permute-done | bytes 131104 | tf_op jit(solution)/shard_map/ppermute | solution.py:350
  43.2 18.6 %all_to_all.10 = f32[32,8,128]{2,1,0:T(8,128)S(1)} all-to-all(f32[32,8,128]{2,1,0:T(8,128)S(1)} %bitcast.40), channel_id=1, replica_groups=mesh['wide'=32,'narrow'=8] {'wide'}, dimensions={0} | all-to-all | bytes 262144 | tf_op jit(solution)/shard_map/all_to_all | solution.py:394
  61.8 0.9 shard_map.176
  62.7 14.9 %all_to_all.11 = f32[32,8,128]{2,1,0:T(8,128)S(1)} all-to-all(f32[32,8,128]{2,1,0:T(8,128)S(1)} %bitcast.42), channel_id=1, replica_groups=mesh['wide'=32,'narrow'=8] {'wide'}, dimensions={0} | all-to-all | bytes 262144 | tf_op jit(solution)/shard_map/all_to_all | solution.py:398
  77.9 2.3 %collective-permute-start.12 = (f32[256,128]{1,0:T(8,128)S(1)}, f32[256,128]{1,0:T(8,128)S(1)}, u32[]{:S(2)}, u32[]{:S(2)}) collective-permute-start(f32[256,128]{1,0:T(8,128)S(1)} %shard_map.177.refs_0_), channel_id=1, source_target_pairs={{0,1},{1,0},{2,3},{3,2},{4,5},{5,4},{6,7},{7,6},{8,9},{9,8},{10,11... | collective-permute-start | bytes 393224 | tf_op jit(solution)/shard_map/ppermute | solution.py:350
  80.2 0.8 collective-permute-start.11
  81.0 1.2 %collective-permute-start.10 = (f32[256,128]{1,0:T(8,128)S(1)}, f32[256,128]{1,0:T(8,128)S(1)}, u32[]{:S(2)}, u32[]{:S(2)}) collective-permute-start(f32[256,128]{1,0:T(8,128)S(1)} %shard_map.177.refs_0_), channel_id=1, source_target_pairs={{0,2},{1,3},{2,4},{3,5},{4,6},{5,7},{6,0},{7,1},{8,10},{9,11},{10,... | collective-permute-start | bytes 393224 | tf_op jit(solution)/shard_map/ppermute | solution.py:350
  82.2 0.6 collective-permute-start.9
  83.2 1.8 %collective-permute-start.15 = (f32[256,128]{1,0:T(8,128)S(1)}, f32[256,128]{1,0:T(8,128)S(1)}, u32[]{:S(2)}, u32[]{:S(2)}) collective-permute-start(f32[256,128]{1,0:T(8,128)S(1)} %collective-permute-done.12.refs_4_), channel_id=1, source_target_pairs={{0,6},{1,7},{2,0},{3,1},{4,2},{5,3},{6,4},{7,5},{8,14},{9,15},{10,... | collective-permute-start | bytes 393224 | tf_op jit(solution)/shard_map/ppermute | solution.py:350
  85.2 1.4 %collective-permute-done.11.refs_3_ = f32[256,128]{1,0:T(8,128)S(1)} collective-permute-done((f32[256,128]{1,0:T(8,128)S(1)}, f32[256,128]{1,0:T(8,128)S(1)}, u32[]{:S(2)}, u32[]{:S(2)}) %collective-permute-start.11) | collective-permute-done | bytes 131104 | tf_op jit(solution)/shard_map/ppermute | solution.py:350
  86.6 1.2 %collective-permute-start.13 = (f32[256,128]{1,0:T(8,128)S(1)}, f32[256,128]{1,0:T(8,128)S(1)}, u32[]{:S(2)}, u32[]{:S(2)}) collective-permute-start(f32[256,128]{1,0:T(8,128)S(1)} %collective-permute-done.12.refs_4_), channel_id=1, source_target_pairs={{0,4},{1,5},{2,6},{3,7},{4,0},{5,1},{6,2},{7,3},{8,12},{9,13},{10,... | collective-permute-start | bytes 393224 | tf_op jit(solution)/shard_map/ppermute | solution.py:350
  87.8 3.2 %collective-permute-done.10.refs_2_ = f32[256,128]{1,0:T(8,128)S(1)} collective-permute-done((f32[256,128]{1,0:T(8,128)S(1)}, f32[256,128]{1,0:T(8,128)S(1)}, u32[]{:S(2)}, u32[]{:S(2)}) %collective-permute-start.10) | collective-permute-done | bytes 131104 | tf_op jit(solution)/shard_map/ppermute | solution.py:350
  91.0 1.2 %collective-permute-done.15.refs_7_ = f32[256,128]{1,0:T(8,128)S(1)} collective-permute-done((f32[256,128]{1,0:T(8,128)S(1)}, f32[256,128]{1,0:T(8,128)S(1)}, u32[]{:S(2)}, u32[]{:S(2)}) %collective-permute-start.15) | collective-permute-done | bytes 131104 | tf_op jit(solution)/shard_map/ppermute | solution.py:350
  92.1 2.8 %collective-permute-done.14.refs_6_ = f32[256,128]{1,0:T(8,128)S(1)} collective-permute-done((f32[256,128]{1,0:T(8,128)S(1)}, f32[256,128]{1,0:T(8,128)S(1)}, u32[]{:S(2)}, u32[]{:S(2)}) %collective-permute-start.14) | collective-permute-done | bytes 131104 | tf_op jit(solution)/shard_map/ppermute | solution.py:350
  94.9 2.4 %shard_map.178.ls = f32[2048,128]{1,0:T(8,128)S(1)} custom-call(f32[256,128]{1,0:T(8,128)S(1)} %shard_map.177.refs_0_, f32[256,128]{1,0:T(8,128)S(1)} %collective-permute-done.9.refs_1_, f32[256,128]{1,0:T(8,128)S(1)} %collective-permute-done.10.refs_2_, f32[256,128]{1,0:T(8,128)S(1)} %collective-permute-done.11.refs_3_, ...), custom_call_target="tpu_custom_call" | custom-call | tf_op jit(solution)/shard_map/pallas_call | solution.py:404
  97.4 3.8 %shard_map.179 = f32[1600,128]{1,0:T(8,128)} custom-call(f32[2048,128]{1,0:T(8,128)S(1)} %shard_map.178.ls, s32[64,128]{1,0:T(8,128)S(1)} %bitcast.45, f32[200,25]{1,0:T(8,128)S(1)} %bitcast.47), custom_call_target="tpu_custom_call" | custom-call | tf_op jit(solution)/shard_map/pallas_call | solution.py:405
  (50 shorter events, 1.4 us)
Async XLA Ops:
  0.9 10.3 %copy-start.10 = (s32[1,2,4096]{2,1,0:T(2,128)S(1)}, s32[1,2,4096]{2,1,0:T(2,128)}, u32[]{:S(2)}) copy-start(s32[1,2,4096]{2,1,0:T(2,128)} %param.20) | copy-start | bytes 98308
  0.9 10.3 %copy-start.11 = (f32[8,25,25]{2,0,1:T(8,128)S(1)}, f32[8,25,25]{2,0,1:T(8,128)}, u32[]{:S(2)}) copy-start(f32[8,25,25]{2,0,1:T(8,128)} %param.21) | copy-start | bytes 60004
  0.9 10.3 %copy-start.15 = (s32[1,2,4096]{2,1,0:T(2,128)S(1)}, s32[1,2,4096]{2,1,0:T(2,128)}, u32[]{:S(2)}) copy-start(s32[1,2,4096]{2,1,0:T(2,128)} %param.19) | copy-start | bytes 98308
  1.0 14.6 %collective-permute-start.1 = (f32[2,9,8,64]{3,2,1,0:T(8,128)S(1)}, f32[2,9,8,64]{3,2,1,0:T(8,128)S(1)}, u32[]{:S(2)}, u32[]{:S(2)}) collective-permute-start(f32[2,9,8,64]{3,2,1,0:T(8,128)S(1)} %get-tuple-element.17), channel_id=1, source_target_pairs={{0,255},{1,254},{2,253},{3,252},{4,251},{5,250},{6,249},{7,248},{8... | collective-permute-start | bytes 110600 | tf_op jit(solution)/shard_map/ppermute | solution.py:364
  9.7 6.5 %collective-permute-start = (f32[2,9,8,64]{3,2,1,0:T(8,128)S(1)}, f32[2,9,8,64]{3,2,1,0:T(8,128)S(1)}, u32[]{:S(2)}, u32[]{:S(2)}) collective-permute-start(f32[2,9,8,64]{3,2,1,0:T(8,128)S(1)} %get-tuple-element.18), channel_id=1, source_target_pairs={{0,7},{1,6},{2,5},{3,4},{4,3},{5,2},{6,1},{7,0},{8,255},{9,254},{1... | collective-permute-start | bytes 110600 | tf_op jit(solution)/shard_map/ppermute | solution.py:363
  18.5 7.0 %collective-permute-start.6 = (f32[256,128]{1,0:T(8,128)S(1)}, f32[256,128]{1,0:T(8,128)S(1)}, u32[]{:S(2)}, u32[]{:S(2)}) collective-permute-start(f32[256,128]{1,0:T(8,128)S(1)} %get-tuple-element.14), channel_id=1, source_target_pairs={{0,2},{1,3},{2,4},{3,5},{4,6},{5,7},{6,0},{7,1},{8,10},{9,11},{10,... | collective-permute-start | bytes 393224 | tf_op jit(solution)/shard_map/ppermute | solution.py:350
  18.6 9.5 %collective-permute-start.7 = (f32[256,128]{1,0:T(8,128)S(1)}, f32[256,128]{1,0:T(8,128)S(1)}, u32[]{:S(2)}, u32[]{:S(2)}) collective-permute-start(f32[256,128]{1,0:T(8,128)S(1)} %get-tuple-element.15), channel_id=1, source_target_pairs={{0,6},{1,7},{2,0},{3,1},{4,2},{5,3},{6,4},{7,5},{8,14},{9,15},{10,... | collective-permute-start | bytes 393224 | tf_op jit(solution)/shard_map/ppermute | solution.py:350
  21.8 12.7 %copy-start.1 = (f32[2,9,64,2,8]{2,4,3,1,0:T(8,128)S(1)}, f32[2,9,64,2,8]{2,4,3,1,0:T(8,128)}, u32[]{:S(2)}) copy-start(f32[2,9,64,2,8]{2,4,3,1,0:T(8,128)} %param.23) | copy-start | bytes 221188
  21.8 12.7 %copy-start.6 = (f32[144,640]{1,0:T(8,128)S(1)}, f32[144,640]{1,0:T(8,128)}, u32[]{:S(2)}) copy-start(f32[144,640]{1,0:T(8,128)} %constant.23.clone.expand_ref) | copy-start | bytes 1105924
  21.8 12.7 %copy-start.7 = (f32[128,640]{1,0:T(8,128)S(1)}, f32[128,640]{1,0:T(8,128)}, u32[]{:S(2)}) copy-start(f32[128,640]{1,0:T(8,128)} %constant.26.clone.mask_ref) | copy-start | bytes 983044
  21.8 12.7 %copy-start.13 = (f32[25,640]{1,0:T(8,128)S(1)}, f32[25,640]{1,0:T(8,128)}, u32[]{:S(2)}) copy-start(f32[25,640]{1,0:T(8,128)} %constant.25.clone.lanes_ref) | copy-start | bytes 192004
  21.8 12.7 %copy-start.14 = (f32[128,25]{1,0:T(8,128)S(1)}, f32[128,25]{1,0:T(8,128)}, u32[]{:S(2)}) copy-start(f32[128,25]{1,0:T(8,128)} %constant.24.clone.rows_ref) | copy-start | bytes 38404
  21.8 12.7 %copy-start.16 = (f32[64,64]{1,0:T(8,128)S(1)}, f32[64,64]{1,0:T(8,128)}, u32[]{:S(2)}) copy-start(f32[64,64]{1,0:T(8,128)} %constant.27.clone.flip_ref) | copy-start | bytes 49156
  21.9 7.9 %collective-permute-start.5 = (f32[256,128]{1,0:T(8,128)S(1)}, f32[256,128]{1,0:T(8,128)S(1)}, u32[]{:S(2)}, u32[]{:S(2)}) collective-permute-start(f32[256,128]{1,0:T(8,128)S(1)} %get-tuple-element.16), channel_id=1, source_target_pairs={{0,4},{1,5},{2,6},{3,7},{4,0},{5,1},{6,2},{7,3},{8,12},{9,13},{10,... | collective-permute-start | bytes 393224 | tf_op jit(solution)/shard_map/ppermute | solution.py:350
  29.7 4.9 %copy-start.17 = (f32[25,25]{1,0:T(8,128)S(1)}, f32[25,25]{1,0:T(8,128)}, u32[]{:S(2)}) copy-start(f32[25,25]{1,0:T(8,128)} %coupling_ref.1) | copy-start | bytes 7504
  29.8 7.3 %collective-permute-start.8 = (f32[256,128]{1,0:T(8,128)S(1)}, f32[256,128]{1,0:T(8,128)S(1)}, u32[]{:S(2)}, u32[]{:S(2)}) collective-permute-start(f32[256,128]{1,0:T(8,128)S(1)} %get-tuple-element.9), channel_id=1, source_target_pairs={{0,1},{1,0},{2,3},{3,2},{4,5},{5,4},{6,7},{7,6},{8,9},{9,8},{10,11... | collective-permute-start | bytes 393224 | tf_op jit(solution)/shard_map/ppermute | solution.py:350
  30.4 6.6 %collective-permute-start.4 = (f32[256,128]{1,0:T(8,128)S(1)}, f32[256,128]{1,0:T(8,128)S(1)}, u32[]{:S(2)}, u32[]{:S(2)}) collective-permute-start(f32[256,128]{1,0:T(8,128)S(1)} %get-tuple-element.10), channel_id=1, source_target_pairs={{0,6},{1,7},{2,0},{3,1},{4,2},{5,3},{6,4},{7,5},{8,14},{9,15},{10,... | collective-permute-start | bytes 393224 | tf_op jit(solution)/shard_map/ppermute | solution.py:350
  33.1 9.8 %collective-permute-start.3 = (f32[256,128]{1,0:T(8,128)S(1)}, f32[256,128]{1,0:T(8,128)S(1)}, u32[]{:S(2)}, u32[]{:S(2)}) collective-permute-start(f32[256,128]{1,0:T(8,128)S(1)} %get-tuple-element.11), channel_id=1, source_target_pairs={{0,2},{1,3},{2,4},{3,5},{4,6},{5,7},{6,0},{7,1},{8,10},{9,11},{10,... | collective-permute-start | bytes 393224 | tf_op jit(solution)/shard_map/ppermute | solution.py:350
  33.1 9.8 %collective-permute-start.2 = (f32[256,128]{1,0:T(8,128)S(1)}, f32[256,128]{1,0:T(8,128)S(1)}, u32[]{:S(2)}, u32[]{:S(2)}) collective-permute-start(f32[256,128]{1,0:T(8,128)S(1)} %get-tuple-element.12), channel_id=1, source_target_pairs={{0,4},{1,5},{2,6},{3,7},{4,0},{5,1},{6,2},{7,3},{8,12},{9,13},{10,... | collective-permute-start | bytes 393224 | tf_op jit(solution)/shard_map/ppermute | solution.py:350
  34.6 8.3 %copy-start.2 = (bf16[256,768]{1,0:T(8,128)(2,1)S(1)}, bf16[256,768]{1,0:T(8,128)(2,1)}, u32[]{:S(2)}) copy-start(bf16[256,768]{1,0:T(8,128)(2,1)} %constant.28.clone.refs_5_) | copy-start | bytes 1179652
  42.9 18.9 %copy-start.4 = (bf16[256,768]{1,0:T(8,128)(2,1)S(1)}, bf16[256,768]{1,0:T(8,128)(2,1)}, u32[]{:S(2)}) copy-start(bf16[256,768]{1,0:T(8,128)(2,1)} %constant.30.clone.inverse_ref) | copy-start | bytes 1179652
  42.9 18.9 %copy-start.5 = (bf16[256,768]{1,0:T(8,128)(2,1)S(1)}, bf16[256,768]{1,0:T(8,128)(2,1)}, u32[]{:S(2)}) copy-start(bf16[256,768]{1,0:T(8,128)(2,1)} %constant.29.clone.forward_ref) | copy-start | bytes 1179652
  61.8 15.8 %copy-start.3 = (bf16[768,256]{1,0:T(8,128)(2,1)S(1)}, bf16[768,256]{1,0:T(8,128)(2,1)}, u32[]{:S(2)}) copy-start(bf16[768,256]{1,0:T(8,128)(2,1)} %constant.31.clone.table_ref) | copy-start | bytes 1179652
  77.6 17.3 %copy-start.9 = (bf16[8,64,240]{2,1,0:T(8,128)(2,1)S(1)}, bf16[8,64,240]{2,1,0:T(8,128)(2,1)}, u32[]{:S(2)}) copy-start(bf16[8,64,240]{2,1,0:T(8,128)(2,1)} %constant.32.clone.refs_8_) | copy-start | bytes 737284
  77.9 19.5 %copy-start.12 = (f32[8,25,25]{2,0,1:T(8,128)S(1)}, f32[8,25,25]{2,0,1:T(8,128)}, u32[]{:S(2)}) copy-start(f32[8,25,25]{2,0,1:T(8,128)} %param.24) | copy-start | bytes 60004
  77.9 5.3 %collective-permute-start.12 = (f32[256,128]{1,0:T(8,128)S(1)}, f32[256,128]{1,0:T(8,128)S(1)}, u32[]{:S(2)}, u32[]{:S(2)}) collective-permute-start(f32[256,128]{1,0:T(8,128)S(1)} %shard_map.177.refs_0_), channel_id=1, source_target_pairs={{0,1},{1,0},{2,3},{3,2},{4,5},{5,4},{6,7},{7,6},{8,9},{9,8},{10,11... | collective-permute-start | bytes 393224 | tf_op jit(solution)/shard_map/ppermute | solution.py:350
  80.2 6.4 %collective-permute-start.11 = (f32[256,128]{1,0:T(8,128)S(1)}, f32[256,128]{1,0:T(8,128)S(1)}, u32[]{:S(2)}, u32[]{:S(2)}) collective-permute-start(f32[256,128]{1,0:T(8,128)S(1)} %shard_map.177.refs_0_), channel_id=1, source_target_pairs={{0,6},{1,7},{2,0},{3,1},{4,2},{5,3},{6,4},{7,5},{8,14},{9,15},{10,... | collective-permute-start | bytes 393224 | tf_op jit(solution)/shard_map/ppermute | solution.py:350
  81.0 10.0 %collective-permute-start.10 = (f32[256,128]{1,0:T(8,128)S(1)}, f32[256,128]{1,0:T(8,128)S(1)}, u32[]{:S(2)}, u32[]{:S(2)}) collective-permute-start(f32[256,128]{1,0:T(8,128)S(1)} %shard_map.177.refs_0_), channel_id=1, source_target_pairs={{0,2},{1,3},{2,4},{3,5},{4,6},{5,7},{6,0},{7,1},{8,10},{9,11},{10,... | collective-permute-start | bytes 393224 | tf_op jit(solution)/shard_map/ppermute | solution.py:350
  82.2 8.7 %collective-permute-start.9 = (f32[256,128]{1,0:T(8,128)S(1)}, f32[256,128]{1,0:T(8,128)S(1)}, u32[]{:S(2)}, u32[]{:S(2)}) collective-permute-start(f32[256,128]{1,0:T(8,128)S(1)} %shard_map.177.refs_0_), channel_id=1, source_target_pairs={{0,4},{1,5},{2,6},{3,7},{4,0},{5,1},{6,2},{7,3},{8,12},{9,13},{10,... | collective-permute-start | bytes 393224 | tf_op jit(solution)/shard_map/ppermute | solution.py:350
  83.2 9.0 %collective-permute-start.15 = (f32[256,128]{1,0:T(8,128)S(1)}, f32[256,128]{1,0:T(8,128)S(1)}, u32[]{:S(2)}, u32[]{:S(2)}) collective-permute-start(f32[256,128]{1,0:T(8,128)S(1)} %collective-permute-done.12.refs_4_), channel_id=1, source_target_pairs={{0,6},{1,7},{2,0},{3,1},{4,2},{5,3},{6,4},{7,5},{8,14},{9,15},{10,... | collective-permute-start | bytes 393224 | tf_op jit(solution)/shard_map/ppermute | solution.py:350
  84.9 10.0 %collective-permute-start.14 = (f32[256,128]{1,0:T(8,128)S(1)}, f32[256,128]{1,0:T(8,128)S(1)}, u32[]{:S(2)}, u32[]{:S(2)}) collective-permute-start(f32[256,128]{1,0:T(8,128)S(1)} %collective-permute-done.12.refs_4_), channel_id=1, source_target_pairs={{0,2},{1,3},{2,4},{3,5},{4,6},{5,7},{6,0},{7,1},{8,10},{9,11},{10,... | collective-permute-start | bytes 393224 | tf_op jit(solution)/shard_map/ppermute | solution.py:350
  86.6 8.3 %collective-permute-start.13 = (f32[256,128]{1,0:T(8,128)S(1)}, f32[256,128]{1,0:T(8,128)S(1)}, u32[]{:S(2)}, u32[]{:S(2)}) collective-permute-start(f32[256,128]{1,0:T(8,128)S(1)} %collective-permute-done.12.refs_4_), channel_id=1, source_target_pairs={{0,4},{1,5},{2,6},{3,7},{4,0},{5,1},{6,2},{7,3},{8,12},{9,13},{10,... | collective-permute-start | bytes 393224 | tf_op jit(solution)/shard_map/ppermute | solution.py:350
  (2 other events, 5.0 us)

commit v2 on v1

--- a/solution.py
+++ b/solution.py
@@ -17,6 +17,7 @@
 VMEM_LIMIT = 48 * 1024 * 1024
 
 STEPS = ((0, 0), (2, 0), (1, 0), (-1, 0), (0, 1), (2, 1), (1, 1), (-1, 1))
+_, FAR, ABOVE, BELOW, ACROSS = STEPS[:5]
 
 DEGREE = np.array([n for n in range(ORDER + 1) for _ in range(2 * n + 1)])
 
@@ -101,7 +102,7 @@
 
 def expand_tables():
     own = np.zeros((72, 640), np.float32)
-    mirror = np.zeros((72, 640), np.float32)
+    mirror = np.zeros((32, 640), np.float32)
     rows = np.zeros((128, NC), np.float32)
     lanes = np.zeros((NC, 640), np.float32)
     mask = np.zeros((128, 640), np.float32)
@@ -114,7 +115,7 @@
                 d = DEGREE[c] + s
                 own[d * 8 + t, lane] = 1
                 if 1 <= t <= 3:
-                    mirror[d * 8 + 8 - t, lane] = 1
+                    mirror[(3 - t) * 9 + d, lane] = 1
                 for j in range(NC):
                     if DEGREE[j] == s:
                         mask[t * NC + j, lane] = 1
@@ -148,9 +149,24 @@
 def load_operators(op_ref, w_ref):
     w_ref[...] = jnp.zeros_like(w_ref)
     w_ref[0:200, 0:NC] = op_ref[...]
-    rows = [w_ref[pl.ds(octant, 32, stride=8), :][:, 0:32] for octant in range(8)]
-    high, low = split(jnp.concatenate(rows, axis=0))
+    rows = [w_ref[pl.ds(octant, 24, stride=8), :] for octant in range(8)] + [w_ref[192:200, :]]
+    high, low = split(jnp.concatenate(rows, axis=0)[:, 0:32])
     return jnp.concatenate([high, low, high], axis=1)
+
+
+def load_blocks(ref, first):
+    blocks = []
+    for i in range(GROUP):
+        last = ref[pl.ds(24 * 64 + first + i, 1), :]
+        blocks.append(jnp.concatenate([ref[pl.ds(first + i, 24, stride=64), :], jnp.broadcast_to(last, (8, 128))], axis=0))
+    return jnp.concatenate(blocks, axis=1)
+
+
+def store_blocks(ref, first, most, last):
+    for i in range(GROUP):
+        lanes = slice(128 * i, 128 * i + 128)
+        ref[pl.ds(first + i, 24, stride=64), :] = most[:, lanes]
+        ref[pl.ds(24 * 64 + first + i, 1), :] = last[:, lanes]
 
 
 def lane_rows(ref, first, count):
@@ -159,38 +175,26 @@
 
 def translate(w_cat, value, octant):
     product = dot(w_cat, stacked(value, 0))
-    total = product[0:32]
+    total = product[0:24]
     for o in range(1, 8):
-        total = jnp.where(octant == o, product[32 * o : 32 * o + 32], total)
-    return total
+        total = jnp.where(octant == o, product[24 * o : 24 * o + 24], total)
+    chosen = octant == lax.broadcasted_iota(jnp.int32, (8, 1), 0)
+    last = jnp.sum(jnp.where(chosen, product[192:200], 0.0), axis=0, keepdims=True)
+    return total, last
 
 
 GROUP = 8
 BATCH = 5
 
 
-def head_kernel(leaf_hbm, order_hbm, octant_hbm, op_hbm, ms, xs, order_ref, octant_ref, op_ref, ws, sems):
-    copies = [
-        pltpu.make_async_copy(op_hbm, op_ref, sems.at[0]),
-        pltpu.make_async_copy(leaf_hbm, xs.at[pl.ds(0, NC * 64)], sems.at[1]),
-        pltpu.make_async_copy(order_hbm, order_ref, sems.at[2]),
-        pltpu.make_async_copy(octant_hbm, octant_ref, sems.at[3]),
-    ]
-    for copy in copies:
-        copy.start()
-    copies[0].wait()
+def head_kernel(leaf_ref, order_ref, octant_ref, op_ref, out_ref, ws):
     w_cat = load_operators(op_ref, ws)
     degree = degree_column()
-    for copy in copies[1:]:
-        copy.wait()
 
     def group(g, carry):
         b = g * GROUP
-        x = jnp.concatenate([xs[pl.ds(b + i, 32, stride=64), :] for i in range(GROUP)], axis=1)
-        kept = jnp.where(degree <= lane_rows(order_ref, b, GROUP), x, 0.0)
-        total = translate(w_cat, kept, lane_rows(octant_ref, b, GROUP))
-        for i in range(GROUP):
-            ms[pl.ds(b + i, NC, stride=64), :] = total[0:NC, 128 * i : 128 * i + 128]
+        kept = jnp.where(degree <= lane_rows(order_ref, b, GROUP), load_blocks(leaf_ref, b), 0.0)
+        store_blocks(out_ref, b, *translate(w_cat, kept, lane_rows(octant_ref, b, GROUP)))
         return carry
 
     lax.fori_loop(0, 64 // GROUP, group, 0)
@@ -226,9 +230,17 @@
     *parts, table_ref, _, out_ref = refs
     total = parts[0][...]
     for part in parts[1:]:
-        total = total + part[...]
+        total = total + part[0:256, :]
     total = jnp.concatenate([total[0:128], total[128:256]], axis=1)
     out_ref[...] = dot(table_ref[...], stacked(total, 1), ((1,), (1,)))
+
+
+def pack_kernel(k_ref, even_ref, odd_ref, rows):
+    for k2, send_ref in enumerate((even_ref, odd_ref)):
+        rows[...] = jnp.concatenate([k_ref[0, :, k2].reshape(72, GRID), k_ref[1, :, k2].reshape(72, GRID)], axis=1)
+        send_ref[...] = jnp.zeros_like(send_ref)
+        for i in range(3):
+            send_ref[9 * i : 9 * i + 9, :] = rows[pl.ds(5 + i, 9, stride=8), :]
 
 
 def prepare_kernel(k_ref, r0_ref, r1_ref, coupling_ref, expand_ref, rows_ref, lanes_ref, mask_ref, flip_ref, k_out, c_out):
@@ -236,7 +248,7 @@
     for part in range(2):
         for k2 in range(2):
             own = k_ref[part, :, k2].reshape(72, GRID)
-            mirror = (r0_ref, r1_ref)[k2][part].reshape(72, GRID)
+            mirror = (r0_ref, r1_ref)[k2][:, 64 * part : 64 * part + 64]
             mirror = dot(mirror, flip_ref[...], precision=exact)
             if part == 1:
                 mirror = -mirror
@@ -277,9 +289,11 @@
 def z_inverse_kernel(*refs):
     parts = refs[0:8]
     table_ref, ls, fs = refs[8:]
-    for m in range(8):
-        fs[m * 256 : m * 256 + 256, :] = parts[m][...]
-    ls[pl.ds(NC * 64, 7 * 64), :] = jnp.zeros((7 * 64, 128), F32)
+    row = 0
+    for part in parts:
+        rows = part.shape[0]
+        fs[row : row + rows, :] = part[...]
+        row += rows
     me = lax.axis_index("narrow")
     table = table_ref[me]
 
@@ -302,15 +316,12 @@
     lax.fori_loop(0, NC // BATCH, coefficients, 0)
 
 
-def tail_kernel(ls, octant_ref, op_ref, out_ref, ws):
+def tail_kernel(local_ref, octant_ref, op_ref, out_ref, ws):
     w_cat = load_operators(op_ref, ws)
 
     def group(g, carry):
         b = g * GROUP
-        x = jnp.concatenate([ls[pl.ds(b + i, 32, stride=64), :] for i in range(GROUP)], axis=1)
-        total = translate(w_cat, x, lane_rows(octant_ref, b, GROUP))
-        for i in range(GROUP):
-            out_ref[pl.ds(b + i, NC, stride=64), :] = total[0:NC, 128 * i : 128 * i + 128]
+        store_blocks(out_ref, b, *translate(w_cat, load_blocks(local_ref, b), lane_rows(octant_ref, b, GROUP)))
         return carry
 
     lax.fori_loop(0, 64 // GROUP, group, 0)
@@ -360,37 +371,29 @@
 
     to_even = [(w * 8 + n, ((32 - w) % 32) * 8 + 7 - n) for w in range(32) for n in range(8)]
     to_odd = [(w * 8 + n, (31 - w) * 8 + 7 - n) for w in range(32) for n in range(8)]
-    mirror0 = lax.ppermute(kernel[:, :, 0], ("wide", "narrow"), to_even)
-    mirror1 = lax.ppermute(kernel[:, :, 1], ("wide", "narrow"), to_odd)
-
-    chunks = call(
-        head_kernel,
-        shape(NC * 64, 128),
-        [
-            pltpu.VMEM((2048, 128), F32),
-            pltpu.VMEM((64, 128), jnp.int32),
-            pltpu.VMEM((64, 128), jnp.int32),
-            pltpu.VMEM((NC * 8, NC), F32),
-            pltpu.VMEM((256, 128), F32),
-            pltpu.SemaphoreType.DMA((4,)),
-        ],
-        [pl.BlockSpec(memory_space=pltpu.HBM)] * 4,
-    )(leaves, orders, octants, m2m)
+    even, odd = call(pack_kernel, (shape(32, 128), shape(32, 128)), [pltpu.VMEM((72, 128), F32)])(kernel)
+    mirror0 = lax.ppermute(even, ("wide", "narrow"), to_even)
+    mirror1 = lax.ppermute(odd, ("wide", "narrow"), to_odd)
+
+    moments = call(head_kernel, shape(NC * 64, 128), [pltpu.VMEM((256, 128), F32)])(leaves, orders, octants, m2m)
     whole = pl.BlockSpec(memory_space=pltpu.VMEM)
     anywhere = pl.BlockSpec(memory_space=pl.ANY)
     chunks = call(z_forward_kernel, shape(2048, 128), (), [whole] * 2 + [anywhere] * 2)(
-        chunks, jnp.asarray(Z_FORWARD), mirror0, mirror1
+        moments, jnp.asarray(Z_FORWARD), mirror0, mirror1
     )
     chunks = chunks.reshape(8, 256, 128)
-    across = chunks[4] + sum(shift(chunks[4 + m], STEPS[m]) for m in (1, 2, 3))
-    received = [chunks[0]] + [shift(chunks[m], STEPS[m]) for m in (1, 2, 3)] + [shift(across, STEPS[4])]
+    far = shift(chunks[1] + shift(chunks[5], ACROSS), FAR)
+    across = chunks[4] + shift(chunks[6], ABOVE) + shift(chunks[7], BELOW)
+    received = [chunks[0], far, shift(chunks[2], ABOVE), shift(chunks[3], BELOW), shift(across, ACROSS)]
 
     kernels, couplings = call(prepare_kernel, (shape(2, 128, 640), shape(384, 640, dtype=BF)))(
         kernel, mirror0, mirror1, coupling,
         jnp.asarray(EXPAND), jnp.asarray(ROWS), jnp.asarray(LANES), jnp.asarray(MASK), jnp.asarray(FLIP),
     )
 
-    along = call(y_forward_kernel, shape(256, 128), (), [whole] * 6 + [anywhere])(*received, jnp.asarray(Y_FORWARD), kernels)
+    along = call(y_forward_kernel, shape(256, 128), (), [whole] * 6 + [anywhere])(
+        *received, jnp.asarray(Y_FORWARD), kernels
+    )
     along = lax.all_to_all(along.reshape(32, 8, 128), "wide", split_axis=0, concat_axis=0, tiled=True)
     along = call(middle_kernel, shape(256, 128))(
         along.reshape(256, 128), jnp.asarray(X_FORWARD), couplings, kernels, jnp.asarray(X_INVERSE)
@@ -398,10 +401,12 @@
     along = lax.all_to_all(along.reshape(32, 8, 128), "wide", split_axis=0, concat_axis=0, tiled=True)
     plane = call(y_inverse_kernel, shape(256, 128))(along.reshape(256, 128), jnp.asarray(Y_INVERSE))
 
-    other = shift(plane, STEPS[4])
-    planes = [plane] + [shift(plane, STEPS[m]) for m in (1, 2, 3)]
-    planes += [other] + [shift(other, STEPS[m]) for m in (1, 2, 3)]
-    local = call(z_inverse_kernel, shape(2048, 128), [pltpu.VMEM((2048, 128), F32)])(*planes, jnp.asarray(Z_INVERSE))
+    other = shift(plane, ACROSS)
+    far = shift(plane, FAR)
+    above, below = shift(plane, ABOVE), shift(plane, BELOW)
+    far_other, above_other, below_other = shift(far, ACROSS), shift(other, ABOVE), shift(other, BELOW)
+    planes = [plane, far, above, below, other, far_other, above_other, below_other]
+    local = call(z_inverse_kernel, shape(NC * 64, 128), [pltpu.VMEM((2048, 128), F32)])(*planes, jnp.asarray(Z_INVERSE))
     children = call(tail_kernel, shape(NC * 64, 128), [pltpu.VMEM((256, 128), F32)])(local, octants, l2l)
     children = children.reshape(NC, 32, 2, 128).swapaxes(1, 2)
     return children.reshape(1, NC, 2, 4096)

time: 101 us -> 96.8 us (0.958)
  waiting for transfers between devices: 22.3 us -> 15.4 us
  blocking collectives: 33.6 us -> 36.9 us
  Pallas kernels: 15.5 us -> 14.3 us
    ppermute x14, waiting for transfers between devices: 21.7 us -> 15.4 us  [shift(): lax.ppermute(array, 'narrow', [(n, stepped(n, step, 1)) for n in range(8)])]
    all_to_all x2, blocking collectives: 33.6 us -> 36.9 us  [shards(): lax.all_to_all(along.reshape(32, 8, 128), 'wide', split_axis=0, concat_ax...]
    ppermute x2, starting transfers between devices: 10.2 us -> 8.86 us  [the longest x1 5.79 us: shards(): mirror1 = lax.ppermute(odd, ('wide', 'narrow'), to_odd)]
    unnamed x37 -> x38, local copies, waits for them, and re-layouts: 2.15 us -> 2.88 us
    pallas_call x2 -> x3, Pallas kernels: 5.69 us -> 5.17 us  [the longest x1 2.66 us: shards(): call(head_kernel, shape(NC * 64, 128), [pltpu.VMEM((256, 128), F32)])]
  transfers between devices with their start and end apart: 16 -> 16, of which waited for: 10 -> 8; matrix products, arithmetic and copies ran while one was open for 0% -> 0% of each run, Pallas kernels for 6% -> 5%
where the time goes in v2:
time: 96.8 us; the launch traced here: 96.5 us
  blocking collectives  36.9 us (38%)
  starting transfers between devices  26.7 us (28%)
  waiting for transfers between devices  15.4 us (16%)
  Pallas kernels  14.3 us (15%)
  local copies, waits for them, and re-layouts  2.9 us (3%)
    all_to_all x2, blocking collectives, shards(): lax.all_to_all(along.reshape(32, 8, 128), 'wide', split_axis=0, concat_ax...  36.9 us
    ppermute x14, starting transfers between devices, shift(): lax.ppermute(array, 'narrow', [(n, stepped(n, step, 1)) for n in range(8)])  17.8 us
    ppermute x14, waiting for transfers between devices, shift(): lax.ppermute(array, 'narrow', [(n, stepped(n, step, 1)) for n in range(8)])  15.4 us
    ppermute x1, starting transfers between devices, shards(): mirror1 = lax.ppermute(odd, ('wide', 'narrow'), to_odd)  5.79 us
    pallas_call x1, Pallas kernels, shards(): call(tail_kernel, shape(NC * 64, 128), [pltpu.VMEM((256, 128), F32)])  3.53 us
    ppermute x1, starting transfers between devices, shards(): mirror0 = lax.ppermute(even, ('wide', 'narrow'), to_even)  3.07 us
    unnamed x38, local copies, waits for them, and re-layouts  2.88 us
    pallas_call x1, Pallas kernels, shards(): call(head_kernel, shape(NC * 64, 128), [pltpu.VMEM((256, 128), F32)])  2.66 us
  transfers between devices with their start and end apart: 16, of which 8 were waited for; matrix products, arithmetic and copies ran while one was open for 0% of the time, Pallas kernels for 5%

profile of v2, /device:TPU:2, one launch (start us, length us, event | category | flops | bytes accessed | tf_op | source)
XLA Modules:
  0.0 96.5 jit_solution(1762677233227925867)
XLA Ops:
  0.0 0.9 copy-done.1
  1.0 3.1 %collective-permute-start = (f32[32,128]{1,0:T(8,128)S(1)}, f32[32,128]{1,0:T(8,128)S(1)}, u32[]{:S(2)}, u32[]{:S(2)}) collective-permute-start(f32[32,128]{1,0:T(8,128)S(1)} %get-tuple-element.9), channel_id=1, source_target_pairs={{0,7},{1,6},{2,5},{3,4},{4,3},{5,2},{6,1},{7,0},{8,255},{9,254},{1... | collective-permute-start | bytes 49160 | tf_op jit(solution)/shard_map/ppermute | solution.py:375
  4.1 5.8 %collective-permute-start.1 = (f32[32,128]{1,0:T(8,128)S(1)}, f32[32,128]{1,0:T(8,128)S(1)}, u32[]{:S(2)}, u32[]{:S(2)}) collective-permute-start(f32[32,128]{1,0:T(8,128)S(1)} %get-tuple-element.10), channel_id=1, source_target_pairs={{0,255},{1,254},{2,253},{3,252},{4,251},{5,250},{6,249},{7,248},{8... | collective-permute-start | bytes 49160 | tf_op jit(solution)/shard_map/ppermute | solution.py:376
  9.9 1.1 %copy-done = f32[1,25,2,4096]{3,2,1,0:T(2,128)S(1)} copy-done((f32[1,25,2,4096]{3,2,1,0:T(2,128)S(1)}, f32[1,25,2,4096]{3,2,1,0:T(2,128)}, u32[]{:S(2)}) %copy-start) | copy-done | bytes 819224
  11.0 0.8 copy-done.16
  11.8 2.7 %shard_map.172.ms = f32[1600,128]{1,0:T(8,128)S(1)} custom-call(f32[1600,128]{1,0:T(8,128)S(1)} %bitcast.31, s32[64,128]{1,0:T(8,128)S(1)} %bitcast.42, s32[64,128]{1,0:T(8,128)S(1)} %bitcast.38, f32[200,25]{1,0:T(8,128)S(1)} %bitcast.40), custom_call_target="tpu_custom_call" | custom-call | tf_op jit(solution)/shard_map/pallas_call | solution.py:378
  14.5 2.3 %shard_map.174 = f32[2048,128]{1,0:T(8,128)S(1)} custom-call(f32[1600,128]{1,0:T(8,128)S(1)} %shard_map.172.ms, bf16[8,80,192]{2,1,0:T(8,128)(2,1)S(1)} %copy-done.7, f32[32,128]{1,0:T(8,128)S(1)} %collective-permute-done._0.r0_ref, f32[32,128]{1,0:T(8,128)S(1)} %collective-permute-done.1._1.r1_ref), custom_call_target="tpu_custom_call" | custom-call | tf_op jit(solution)/shard_map/pallas_call | solution.py:381
  17.0 3.1 %collective-permute-start.7 = (f32[256,128]{1,0:T(8,128)S(1)}, f32[256,128]{1,0:T(8,128)S(1)}, u32[]{:S(2)}, u32[]{:S(2)}) collective-permute-start(f32[256,128]{1,0:T(8,128)S(1)} %get-tuple-element.19), channel_id=1, source_target_pairs={{0,6},{1,7},{2,0},{3,1},{4,2},{5,3},{6,4},{7,5},{8,14},{9,15},{10,... | collective-permute-start | bytes 393224 | tf_op jit(solution)/shard_map/ppermute | solution.py:361
  20.1 2.9 %collective-permute-done.6 = f32[256,128]{1,0:T(8,128)S(1)} collective-permute-done((f32[256,128]{1,0:T(8,128)S(1)}, f32[256,128]{1,0:T(8,128)S(1)}, u32[]{:S(2)}, u32[]{:S(2)}) %collective-permute-start.6) | collective-permute-done | bytes 131104 | tf_op jit(solution)/shard_map/ppermute | solution.py:361
  23.1 1.9 %collective-permute-start.2 = (f32[256,128]{1,0:T(8,128)S(1)}, f32[256,128]{1,0:T(8,128)S(1)}, u32[]{:S(2)}, u32[]{:S(2)}) collective-permute-start(f32[256,128]{1,0:T(8,128)S(1)} %get-tuple-element.16), channel_id=1, source_target_pairs={{0,1},{1,0},{2,3},{3,2},{4,5},{5,4},{6,7},{7,6},{8,9},{9,8},{10,11... | collective-permute-start | bytes 393224 | tf_op jit(solution)/shard_map/ppermute | solution.py:361
  25.2 3.2 %collective-permute-start.5 = (f32[256,128]{1,0:T(8,128)S(1)}, f32[256,128]{1,0:T(8,128)S(1)}, u32[]{:S(2)}, u32[]{:S(2)}) collective-permute-start(f32[256,128]{1,0:T(8,128)S(1)} %get-tuple-element.14), channel_id=1, source_target_pairs={{0,6},{1,7},{2,0},{3,1},{4,2},{5,3},{6,4},{7,5},{8,14},{9,15},{10,... | collective-permute-start | bytes 393224 | tf_op jit(solution)/shard_map/ppermute | solution.py:361
  28.6 1.5 %collective-permute-start.3 = (f32[256,128]{1,0:T(8,128)S(1)}, f32[256,128]{1,0:T(8,128)S(1)}, u32[]{:S(2)}, u32[]{:S(2)}) collective-permute-start(f32[256,128]{1,0:T(8,128)S(1)} %slice_add_fusion.1), channel_id=1, source_target_pairs={{0,4},{1,5},{2,6},{3,7},{4,0},{5,1},{6,2},{7,3},{8,12},{9,13},{10,... | collective-permute-start | bytes 393224 | tf_op jit(solution)/shard_map/ppermute | solution.py:361
  30.2 2.0 %shard_map.175 = (f32[2,128,640]{2,1,0:T(8,128)S(1)}, bf16[384,640]{1,0:T(8,128)(2,1)S(1)}) custom-call(f32[2,9,2,8,64]{4,3,2,1,0:T(8,128)S(1)} %bitcast.33, f32[32,128]{1,0:T(8,128)S(1)} %collective-permute-done._0.r0_ref, f32[32,128]{1,0:T(8,128)S(1)} %collective-permute-done.1._1.r1_ref, f32[25,25]{1,0:T(8,128)S(1)} %copy-done.18, ...), custom_call_target="tpu_custom_call" | custom-call | tf_op jit(solution)/shard_map/pallas_call | solution.py:389
  32.2 6.1 %collective-permute-done.4.refs_2_ = f32[256,128]{1,0:T(8,128)S(1)} collective-permute-done((f32[256,128]{1,0:T(8,128)S(1)}, f32[256,128]{1,0:T(8,128)S(1)}, u32[]{:S(2)}, u32[]{:S(2)}) %collective-permute-start.4) | collective-permute-done | bytes 131104 | tf_op jit(solution)/shard_map/ppermute | solution.py:361
  38.3 0.3 shard_map.176
  38.6 22.0 %all_to_all.10 = f32[32,8,128]{2,1,0:T(8,128)S(1)} all-to-all(f32[32,8,128]{2,1,0:T(8,128)S(1)} %bitcast.34), channel_id=1, replica_groups=mesh['wide'=32,'narrow'=8] {'wide'}, dimensions={0} | all-to-all | bytes 262144 | tf_op jit(solution)/shard_map/all_to_all | solution.py:397
  60.6 0.9 shard_map.177
  61.5 14.9 %all_to_all.11 = f32[32,8,128]{2,1,0:T(8,128)S(1)} all-to-all(f32[32,8,128]{2,1,0:T(8,128)S(1)} %bitcast.36), channel_id=1, replica_groups=mesh['wide'=32,'narrow'=8] {'wide'}, dimensions={0} | all-to-all | bytes 262144 | tf_op jit(solution)/shard_map/all_to_all | solution.py:401
  76.7 1.1 %collective-permute-start.12 = (f32[256,128]{1,0:T(8,128)S(1)}, f32[256,128]{1,0:T(8,128)S(1)}, u32[]{:S(2)}, u32[]{:S(2)}) collective-permute-start(f32[256,128]{1,0:T(8,128)S(1)} %shard_map.178.refs_0_), channel_id=1, source_target_pairs={{0,1},{1,0},{2,3},{3,2},{4,5},{5,4},{6,7},{7,6},{8,9},{9,8},{10,11... | collective-permute-start | bytes 393224 | tf_op jit(solution)/shard_map/ppermute | solution.py:361
  77.7 1.3 %collective-permute-start.9 = (f32[256,128]{1,0:T(8,128)S(1)}, f32[256,128]{1,0:T(8,128)S(1)}, u32[]{:S(2)}, u32[]{:S(2)}) collective-permute-start(f32[256,128]{1,0:T(8,128)S(1)} %shard_map.178.refs_0_), channel_id=1, source_target_pairs={{0,4},{1,5},{2,6},{3,7},{4,0},{5,1},{6,2},{7,3},{8,12},{9,13},{10,... | collective-permute-start | bytes 393224 | tf_op jit(solution)/shard_map/ppermute | solution.py:361
  79.0 0.4 collective-permute-start.11
  79.4 1.6 %collective-permute-start.10 = (f32[256,128]{1,0:T(8,128)S(1)}, f32[256,128]{1,0:T(8,128)S(1)}, u32[]{:S(2)}, u32[]{:S(2)}) collective-permute-start(f32[256,128]{1,0:T(8,128)S(1)} %shard_map.178.refs_0_), channel_id=1, source_target_pairs={{0,2},{1,3},{2,4},{3,5},{4,6},{5,7},{6,0},{7,1},{8,10},{9,11},{10,... | collective-permute-start | bytes 393224 | tf_op jit(solution)/shard_map/ppermute | solution.py:361
  81.0 0.7 collective-permute-done.12.refs_4_
  81.7 2.1 %collective-permute-start.15 = (f32[256,128]{1,0:T(8,128)S(1)}, f32[256,128]{1,0:T(8,128)S(1)}, u32[]{:S(2)}, u32[]{:S(2)}) collective-permute-start(f32[256,128]{1,0:T(8,128)S(1)} %collective-permute-done.12.refs_4_), channel_id=1, source_target_pairs={{0,6},{1,7},{2,0},{3,1},{4,2},{5,3},{6,4},{7,5},{8,14},{9,15},{10,... | collective-permute-start | bytes 393224 | tf_op jit(solution)/shard_map/ppermute | solution.py:361
  83.8 1.8 %collective-permute-done.9.refs_1_ = f32[256,128]{1,0:T(8,128)S(1)} collective-permute-done((f32[256,128]{1,0:T(8,128)S(1)}, f32[256,128]{1,0:T(8,128)S(1)}, u32[]{:S(2)}, u32[]{:S(2)}) %collective-permute-start.9) | collective-permute-done | bytes 131104 | tf_op jit(solution)/shard_map/ppermute | solution.py:361
  85.6 1.0 %collective-permute-start.13 = (f32[256,128]{1,0:T(8,128)S(1)}, f32[256,128]{1,0:T(8,128)S(1)}, u32[]{:S(2)}, u32[]{:S(2)}) collective-permute-start(f32[256,128]{1,0:T(8,128)S(1)} %collective-permute-done.9.refs_1_), channel_id=1, source_target_pairs={{0,1},{1,0},{2,3},{3,2},{4,5},{5,4},{6,7},{7,6},{8,9},{9,8},{10,11... | collective-permute-start | bytes 393224 | tf_op jit(solution)/shard_map/ppermute | solution.py:361
  86.6 0.7 collective-permute-done.10.refs_2_
  87.3 0.6 collective-permute-done.15.refs_7_
  87.9 2.1 %collective-permute-done.14.refs_6_ = f32[256,128]{1,0:T(8,128)S(1)} collective-permute-done((f32[256,128]{1,0:T(8,128)S(1)}, f32[256,128]{1,0:T(8,128)S(1)}, u32[]{:S(2)}, u32[]{:S(2)}) %collective-permute-start.14) | collective-permute-done | bytes 131104 | tf_op jit(solution)/shard_map/ppermute | solution.py:361
  90.0 0.6 collective-permute-done.13.refs_5_
  90.6 2.4 %shard_map.179.local_ref = f32[1600,128]{1,0:T(8,128)S(1)} custom-call(f32[256,128]{1,0:T(8,128)S(1)} %shard_map.178.refs_0_, f32[256,128]{1,0:T(8,128)S(1)} %collective-permute-done.9.refs_1_, f32[256,128]{1,0:T(8,128)S(1)} %collective-permute-done.10.refs_2_, f32[256,128]{1,0:T(8,128)S(1)} %collective-permute-done.11.refs_3_, ...), custom_call_target="tpu_custom_call" | custom-call | tf_op jit(solution)/shard_map/pallas_call | solution.py:409
  93.0 3.5 %shard_map.180 = f32[1600,128]{1,0:T(8,128)} custom-call(f32[1600,128]{1,0:T(8,128)S(1)} %shard_map.179.local_ref, s32[64,128]{1,0:T(8,128)S(1)} %bitcast.39, f32[200,25]{1,0:T(8,128)S(1)} %bitcast.41), custom_call_target="tpu_custom_call" | custom-call | tf_op jit(solution)/shard_map/pallas_call | solution.py:410
  (52 shorter events, 1.1 us)
Async XLA Ops:
  0.9 9.0 %copy-start.11 = (s32[1,2,4096]{2,1,0:T(2,128)S(1)}, s32[1,2,4096]{2,1,0:T(2,128)}, u32[]{:S(2)}) copy-start(s32[1,2,4096]{2,1,0:T(2,128)} %param.20) | copy-start | bytes 98308
  0.9 9.0 %copy-start.12 = (f32[8,25,25]{2,0,1:T(8,128)S(1)}, f32[8,25,25]{2,0,1:T(8,128)}, u32[]{:S(2)}) copy-start(f32[8,25,25]{2,0,1:T(8,128)} %param.21) | copy-start | bytes 60004
  1.0 13.4 %collective-permute-start = (f32[32,128]{1,0:T(8,128)S(1)}, f32[32,128]{1,0:T(8,128)S(1)}, u32[]{:S(2)}, u32[]{:S(2)}) collective-permute-start(f32[32,128]{1,0:T(8,128)S(1)} %get-tuple-element.9), channel_id=1, source_target_pairs={{0,7},{1,6},{2,5},{3,4},{4,3},{5,2},{6,1},{7,0},{8,255},{9,254},{1... | collective-permute-start | bytes 49160 | tf_op jit(solution)/shard_map/ppermute | solution.py:375
  4.1 10.4 %collective-permute-start.1 = (f32[32,128]{1,0:T(8,128)S(1)}, f32[32,128]{1,0:T(8,128)S(1)}, u32[]{:S(2)}, u32[]{:S(2)}) collective-permute-start(f32[32,128]{1,0:T(8,128)S(1)} %get-tuple-element.10), channel_id=1, source_target_pairs={{0,255},{1,254},{2,253},{3,252},{4,251},{5,250},{6,249},{7,248},{8... | collective-permute-start | bytes 49160 | tf_op jit(solution)/shard_map/ppermute | solution.py:376
  11.8 2.7 %copy-start.7 = (bf16[8,80,192]{2,1,0:T(8,128)(2,1)S(1)}, bf16[8,80,192]{2,1,0:T(8,128)(2,1)}, u32[]{:S(2)}) copy-start(bf16[8,80,192]{2,1,0:T(8,128)(2,1)} %constant.22.clone.table_ref) | copy-start | bytes 737284
  16.8 6.3 %collective-permute-start.6 = (f32[256,128]{1,0:T(8,128)S(1)}, f32[256,128]{1,0:T(8,128)S(1)}, u32[]{:S(2)}, u32[]{:S(2)}) collective-permute-start(f32[256,128]{1,0:T(8,128)S(1)} %get-tuple-element.18), channel_id=1, source_target_pairs={{0,2},{1,3},{2,4},{3,5},{4,6},{5,7},{6,0},{7,1},{8,10},{9,11},{10,... | collective-permute-start | bytes 393224 | tf_op jit(solution)/shard_map/ppermute | solution.py:361
  17.0 6.0 %collective-permute-start.7 = (f32[256,128]{1,0:T(8,128)S(1)}, f32[256,128]{1,0:T(8,128)S(1)}, u32[]{:S(2)}, u32[]{:S(2)}) collective-permute-start(f32[256,128]{1,0:T(8,128)S(1)} %get-tuple-element.19), channel_id=1, source_target_pairs={{0,6},{1,7},{2,0},{3,1},{4,2},{5,3},{6,4},{7,5},{8,14},{9,15},{10,... | collective-permute-start | bytes 393224 | tf_op jit(solution)/shard_map/ppermute | solution.py:361
  23.0 7.1 %copy-start.8 = (f32[128,640]{1,0:T(8,128)S(1)}, f32[128,640]{1,0:T(8,128)}, u32[]{:S(2)}) copy-start(f32[128,640]{1,0:T(8,128)} %constant.26.clone.mask_ref) | copy-start | bytes 983044
  23.0 7.1 %copy-start.9 = (f32[104,640]{1,0:T(8,128)S(1)}, f32[104,640]{1,0:T(8,128)}, u32[]{:S(2)}) copy-start(f32[104,640]{1,0:T(8,128)} %constant.23.clone.expand_ref) | copy-start | bytes 798724
  23.1 5.5 %collective-permute-start.2 = (f32[256,128]{1,0:T(8,128)S(1)}, f32[256,128]{1,0:T(8,128)S(1)}, u32[]{:S(2)}, u32[]{:S(2)}) collective-permute-start(f32[256,128]{1,0:T(8,128)S(1)} %get-tuple-element.16), channel_id=1, source_target_pairs={{0,1},{1,0},{2,3},{3,2},{4,5},{5,4},{6,7},{7,6},{8,9},{9,8},{10,11... | collective-permute-start | bytes 393224 | tf_op jit(solution)/shard_map/ppermute | solution.py:361
  25.0 7.2 %collective-permute-start.8 = (f32[256,128]{1,0:T(8,128)S(1)}, f32[256,128]{1,0:T(8,128)S(1)}, u32[]{:S(2)}, u32[]{:S(2)}) collective-permute-start(f32[256,128]{1,0:T(8,128)S(1)} %get-tuple-element.13), channel_id=1, source_target_pairs={{0,1},{1,0},{2,3},{3,2},{4,5},{5,4},{6,7},{7,6},{8,9},{9,8},{10,11... | collective-permute-start | bytes 393224 | tf_op jit(solution)/shard_map/ppermute | solution.py:361
  25.2 7.0 %collective-permute-start.5 = (f32[256,128]{1,0:T(8,128)S(1)}, f32[256,128]{1,0:T(8,128)S(1)}, u32[]{:S(2)}, u32[]{:S(2)}) collective-permute-start(f32[256,128]{1,0:T(8,128)S(1)} %get-tuple-element.14), channel_id=1, source_target_pairs={{0,6},{1,7},{2,0},{3,1},{4,2},{5,3},{6,4},{7,5},{8,14},{9,15},{10,... | collective-permute-start | bytes 393224 | tf_op jit(solution)/shard_map/ppermute | solution.py:361
  28.5 1.7 %copy-start.2 = (f32[2,9,64,2,8]{2,4,3,1,0:T(8,128)S(1)}, f32[2,9,64,2,8]{2,4,3,1,0:T(8,128)}, u32[]{:S(2)}) copy-start(f32[2,9,64,2,8]{2,4,3,1,0:T(8,128)} %param.23) | copy-start | bytes 221188
  28.5 1.7 %copy-start.14 = (f32[25,640]{1,0:T(8,128)S(1)}, f32[25,640]{1,0:T(8,128)}, u32[]{:S(2)}) copy-start(f32[25,640]{1,0:T(8,128)} %constant.25.clone.lanes_ref) | copy-start | bytes 192004
  28.5 1.7 %copy-start.15 = (f32[128,25]{1,0:T(8,128)S(1)}, f32[128,25]{1,0:T(8,128)}, u32[]{:S(2)}) copy-start(f32[128,25]{1,0:T(8,128)} %constant.24.clone.rows_ref) | copy-start | bytes 38404
  28.5 1.7 %copy-start.17 = (f32[64,64]{1,0:T(8,128)S(1)}, f32[64,64]{1,0:T(8,128)}, u32[]{:S(2)}) copy-start(f32[64,64]{1,0:T(8,128)} %constant.27.clone.flip_ref) | copy-start | bytes 49156
  28.5 1.7 %copy-start.18 = (f32[25,25]{1,0:T(8,128)S(1)}, f32[25,25]{1,0:T(8,128)}, u32[]{:S(2)}) copy-start(f32[25,25]{1,0:T(8,128)} %coupling_ref.1) | copy-start | bytes 7504
  28.5 9.8 %collective-permute-start.4 = (f32[256,128]{1,0:T(8,128)S(1)}, f32[256,128]{1,0:T(8,128)S(1)}, u32[]{:S(2)}, u32[]{:S(2)}) collective-permute-start(f32[256,128]{1,0:T(8,128)S(1)} %get-tuple-element.15), channel_id=1, source_target_pairs={{0,2},{1,3},{2,4},{3,5},{4,6},{5,7},{6,0},{7,1},{8,10},{9,11},{10,... | collective-permute-start | bytes 393224 | tf_op jit(solution)/shard_map/ppermute | solution.py:361
  28.6 9.7 %copy-start.3 = (bf16[256,768]{1,0:T(8,128)(2,1)S(1)}, bf16[256,768]{1,0:T(8,128)(2,1)}, u32[]{:S(2)}) copy-start(bf16[256,768]{1,0:T(8,128)(2,1)} %constant.28.clone.refs_5_) | copy-start | bytes 1179652
  28.6 9.7 %collective-permute-start.3 = (f32[256,128]{1,0:T(8,128)S(1)}, f32[256,128]{1,0:T(8,128)S(1)}, u32[]{:S(2)}, u32[]{:S(2)}) collective-permute-start(f32[256,128]{1,0:T(8,128)S(1)} %slice_add_fusion.1), channel_id=1, source_target_pairs={{0,4},{1,5},{2,6},{3,7},{4,0},{5,1},{6,2},{7,3},{8,12},{9,13},{10,... | collective-permute-start | bytes 393224 | tf_op jit(solution)/shard_map/ppermute | solution.py:361
  38.3 22.3 %copy-start.5 = (bf16[256,768]{1,0:T(8,128)(2,1)S(1)}, bf16[256,768]{1,0:T(8,128)(2,1)}, u32[]{:S(2)}) copy-start(bf16[256,768]{1,0:T(8,128)(2,1)} %constant.30.clone.inverse_ref) | copy-start | bytes 1179652
  38.3 22.3 %copy-start.6 = (bf16[256,768]{1,0:T(8,128)(2,1)S(1)}, bf16[256,768]{1,0:T(8,128)(2,1)}, u32[]{:S(2)}) copy-start(bf16[256,768]{1,0:T(8,128)(2,1)} %constant.29.clone.forward_ref) | copy-start | bytes 1179652
  60.6 15.8 %copy-start.4 = (bf16[768,256]{1,0:T(8,128)(2,1)S(1)}, bf16[768,256]{1,0:T(8,128)(2,1)}, u32[]{:S(2)}) copy-start(bf16[768,256]{1,0:T(8,128)(2,1)} %constant.31.clone.table_ref) | copy-start | bytes 1179652
  76.4 14.2 %copy-start.10 = (bf16[8,64,240]{2,1,0:T(8,128)(2,1)S(1)}, bf16[8,64,240]{2,1,0:T(8,128)(2,1)}, u32[]{:S(2)}) copy-start(bf16[8,64,240]{2,1,0:T(8,128)(2,1)} %constant.32.clone.refs_8_) | copy-start | bytes 737284
  76.6 16.3 %copy-start.13 = (f32[8,25,25]{2,0,1:T(8,128)S(1)}, f32[8,25,25]{2,0,1:T(8,128)}, u32[]{:S(2)}) copy-start(f32[8,25,25]{2,0,1:T(8,128)} %param.24) | copy-start | bytes 60004
  76.7 5.1 %collective-permute-start.12 = (f32[256,128]{1,0:T(8,128)S(1)}, f32[256,128]{1,0:T(8,128)S(1)}, u32[]{:S(2)}, u32[]{:S(2)}) collective-permute-start(f32[256,128]{1,0:T(8,128)S(1)} %shard_map.178.refs_0_), channel_id=1, source_target_pairs={{0,1},{1,0},{2,3},{3,2},{4,5},{5,4},{6,7},{7,6},{8,9},{9,8},{10,11... | collective-permute-start | bytes 393224 | tf_op jit(solution)/shard_map/ppermute | solution.py:361
  77.7 7.9 %collective-permute-start.9 = (f32[256,128]{1,0:T(8,128)S(1)}, f32[256,128]{1,0:T(8,128)S(1)}, u32[]{:S(2)}, u32[]{:S(2)}) collective-permute-start(f32[256,128]{1,0:T(8,128)S(1)} %shard_map.178.refs_0_), channel_id=1, source_target_pairs={{0,4},{1,5},{2,6},{3,7},{4,0},{5,1},{6,2},{7,3},{8,12},{9,13},{10,... | collective-permute-start | bytes 393224 | tf_op jit(solution)/shard_map/ppermute | solution.py:361
  79.0 7.6 %collective-permute-start.11 = (f32[256,128]{1,0:T(8,128)S(1)}, f32[256,128]{1,0:T(8,128)S(1)}, u32[]{:S(2)}, u32[]{:S(2)}) collective-permute-start(f32[256,128]{1,0:T(8,128)S(1)} %shard_map.178.refs_0_), channel_id=1, source_target_pairs={{0,6},{1,7},{2,0},{3,1},{4,2},{5,3},{6,4},{7,5},{8,14},{9,15},{10,... | collective-permute-start | bytes 393224 | tf_op jit(solution)/shard_map/ppermute | solution.py:361
  79.4 7.9 %collective-permute-start.10 = (f32[256,128]{1,0:T(8,128)S(1)}, f32[256,128]{1,0:T(8,128)S(1)}, u32[]{:S(2)}, u32[]{:S(2)}) collective-permute-start(f32[256,128]{1,0:T(8,128)S(1)} %shard_map.178.refs_0_), channel_id=1, source_target_pairs={{0,2},{1,3},{2,4},{3,5},{4,6},{5,7},{6,0},{7,1},{8,10},{9,11},{10,... | collective-permute-start | bytes 393224 | tf_op jit(solution)/shard_map/ppermute | solution.py:361
  81.7 6.2 %collective-permute-start.15 = (f32[256,128]{1,0:T(8,128)S(1)}, f32[256,128]{1,0:T(8,128)S(1)}, u32[]{:S(2)}, u32[]{:S(2)}) collective-permute-start(f32[256,128]{1,0:T(8,128)S(1)} %collective-permute-done.12.refs_4_), channel_id=1, source_target_pairs={{0,6},{1,7},{2,0},{3,1},{4,2},{5,3},{6,4},{7,5},{8,14},{9,15},{10,... | collective-permute-start | bytes 393224 | tf_op jit(solution)/shard_map/ppermute | solution.py:361
  83.8 6.2 %collective-permute-start.14 = (f32[256,128]{1,0:T(8,128)S(1)}, f32[256,128]{1,0:T(8,128)S(1)}, u32[]{:S(2)}, u32[]{:S(2)}) collective-permute-start(f32[256,128]{1,0:T(8,128)S(1)} %collective-permute-done.12.refs_4_), channel_id=1, source_target_pairs={{0,2},{1,3},{2,4},{3,5},{4,6},{5,7},{6,0},{7,1},{8,10},{9,11},{10,... | collective-permute-start | bytes 393224 | tf_op jit(solution)/shard_map/ppermute | solution.py:361
  85.6 5.0 %collective-permute-start.13 = (f32[256,128]{1,0:T(8,128)S(1)}, f32[256,128]{1,0:T(8,128)S(1)}, u32[]{:S(2)}, u32[]{:S(2)}) collective-permute-start(f32[256,128]{1,0:T(8,128)S(1)} %collective-permute-done.9.refs_1_), channel_id=1, source_target_pairs={{0,1},{1,0},{2,3},{3,2},{4,5},{5,4},{6,7},{7,6},{8,9},{9,8},{10,11... | collective-permute-start | bytes 393224 | tf_op jit(solution)/shard_map/ppermute | solution.py:361
  (3 other events, 2.8 us)

commit v3 on v2

--- a/solution.py
+++ b/solution.py
@@ -16,8 +16,9 @@
 F32 = jnp.float32
 VMEM_LIMIT = 48 * 1024 * 1024
 
-STEPS = ((0, 0), (2, 0), (1, 0), (-1, 0), (0, 1), (2, 1), (1, 1), (-1, 1))
-_, FAR, ABOVE, BELOW, ACROSS = STEPS[:5]
+FAR, ABOVE, BELOW, ACROSS = (2, 0), (1, 0), (-1, 0), (0, 1)
+GATHER_STEPS = ((0, 0), FAR, ABOVE, BELOW, ACROSS, (2, 1), (1, 1), (-1, 1))
+SUM_PARTNERS = (0, 1, 4, 5, 6, 7, 2, 3)
 
 DEGREE = np.array([n for n in range(ORDER + 1) for _ in range(2 * n + 1)])
 
@@ -56,8 +57,10 @@
     forward, inverse = [], []
     for n in range(8):
         tables = []
-        for sign in (1, -1):
-            rows = [8 * stepped(n, step, sign) + t for t in range(SLOTS) for step in STEPS]
+        towards = [n ^ partner for partner in SUM_PARTNERS]
+        origins = [stepped(n, step, -1) for step in GATHER_STEPS]
+        for devices in (towards, origins):
+            rows = [8 * device + t for t in range(SLOTS) for device in devices]
             cosine, sine = wave(np.array(rows)[:, None], z[None, :])
             tables.append(np.concatenate([cosine, -sine], axis=0))
         forward.append(stack_left(tables[0]))
@@ -67,19 +70,20 @@
 
 def y_tables():
     ky = np.arange(GRID)
-    cosine, sine = wave(ky[:, None], ky[None, :])
 
     def place(table):
-        table = table.reshape(2, 2, 32, 2, 32, 2)
-        table = table.transpose(2, 3, 0, 1, 5, 4)
-        full = np.zeros((32, 2, 2, 2, 2, 2, 32, 2))
+        table = table.reshape(2, 2, 2, 32, 2, 32, 2)
+        table = table.transpose(3, 0, 4, 1, 2, 6, 5)
+        full = np.zeros((32, 2, 2, 2, 2, 2, 2, 32, 2))
         for xl in range(2):
-            full[:, xl, :, :, :, :, :, xl] = table
-        return full.reshape(256, 256)
-
-    forward = place(complex_table(cosine, sine, -1))
-    back = complex_table(cosine, sine, 1) / GRID
-    inverse = place(back.transpose(1, 0, 2, 3))
+            full[:, :, xl, :, :, :, :, :, xl] = table
+        return full
+
+    waves = [wave(sign * ky[:, None], ky[None, :]) for sign in (1, -1)]
+    forward = np.stack([complex_table(*w, -1) for w in waves])
+    back = np.stack([complex_table(*w, 1).transpose(1, 0, 2, 3) for w in waves]) / GRID
+    forward = place(forward).reshape(512, 256)
+    inverse = place(back).reshape(512, 256)
     return stack_left(forward), stack_right(inverse)
 
 
@@ -122,7 +126,10 @@
     flip = np.zeros((GRID, GRID), np.float32)
     for k in range(GRID):
         flip[(-k) % GRID, k] = 1
-    return np.concatenate([own, mirror], axis=0), rows, lanes, mask, flip
+    table = np.zeros((400, 640), ml_dtypes.bfloat16)
+    table[0:72], table[80:112], table[112:137], table[144:272] = own, mirror, lanes, mask
+    table[272:400, 0:NC], table[272:336, 128:192] = rows, flip
+    return table
 
 
 def split(value):
@@ -149,7 +156,11 @@
 def load_operators(op_ref, w_ref):
     w_ref[...] = jnp.zeros_like(w_ref)
     w_ref[0:200, 0:NC] = op_ref[...]
-    rows = [w_ref[pl.ds(octant, 24, stride=8), :] for octant in range(8)] + [w_ref[192:200, :]]
+    return operator_rows(w_ref, 0)
+
+
+def operator_rows(ref, first):
+    rows = [ref[pl.ds(first + octant, 24, stride=8), :] for octant in range(8)] + [ref[first + 192 : first + 200, :]]
     high, low = split(jnp.concatenate(rows, axis=0)[:, 0:32])
     return jnp.concatenate([high, low, high], axis=1)
 
@@ -187,20 +198,21 @@
 BATCH = 5
 
 
-def head_kernel(leaf_ref, order_ref, octant_ref, op_ref, out_ref, ws):
-    w_cat = load_operators(op_ref, ws)
-    degree = degree_column()
+def head_kernel(leaf_ref, aux_ref, out_ref):
+    w_cat = operator_rows(aux_ref, 128)
+    degree = degree_column().astype(F32)
 
     def group(g, carry):
         b = g * GROUP
-        kept = jnp.where(degree <= lane_rows(order_ref, b, GROUP), load_blocks(leaf_ref, b), 0.0)
-        store_blocks(out_ref, b, *translate(w_cat, kept, lane_rows(octant_ref, b, GROUP)))
+        kept = jnp.where(degree <= lane_rows(aux_ref, b, GROUP), load_blocks(leaf_ref, b), 0.0)
+        octant = lane_rows(aux_ref, 64 + b, GROUP).astype(jnp.int32)
+        store_blocks(out_ref, b, *translate(w_cat, kept, octant))
         return carry
 
     lax.fori_loop(0, 64 // GROUP, group, 0)
 
 
-def z_forward_kernel(ms, table_ref, _0, _1, out_ref):
+def z_forward_kernel(ms, table_ref, out_ref):
     me = lax.axis_index("narrow")
     table = table_ref[me]
     for m in range(16):
@@ -226,6 +238,11 @@
     lax.fori_loop(0, NC // BATCH, coefficients, 0)
 
 
+def meet_kernel(here_ref, near_ref, _0, _1, _2, own_ref, across_ref):
+    own_ref[...] = here_ref[0:256, :] + near_ref[0:256, :]
+    across_ref[...] = here_ref[256:512, :] + near_ref[256:512, :]
+
+
 def y_forward_kernel(*refs):
     *parts, table_ref, _, out_ref = refs
     total = parts[0][...]
@@ -235,49 +252,64 @@
     out_ref[...] = dot(table_ref[...], stacked(total, 1), ((1,), (1,)))
 
 
-def pack_kernel(k_ref, even_ref, odd_ref, rows):
-    for k2, send_ref in enumerate((even_ref, odd_ref)):
+def pack_kernel(k_ref, send_ref, rows):
+    send_ref[...] = jnp.zeros_like(send_ref)
+    for k2 in range(2):
         rows[...] = jnp.concatenate([k_ref[0, :, k2].reshape(72, GRID), k_ref[1, :, k2].reshape(72, GRID)], axis=1)
-        send_ref[...] = jnp.zeros_like(send_ref)
         for i in range(3):
-            send_ref[9 * i : 9 * i + 9, :] = rows[pl.ds(5 + i, 9, stride=8), :]
-
-
-def prepare_kernel(k_ref, r0_ref, r1_ref, coupling_ref, expand_ref, rows_ref, lanes_ref, mask_ref, flip_ref, k_out, c_out):
+            first = 32 * k2 + 9 * i
+            send_ref[first : first + 9, :] = rows[pl.ds(5 + i, 9, stride=8), :]
+
+
+def prepare_kernel(k_ref, mirror_ref, coupling_ref, table_ref, k_out, c_out):
     exact = lax.Precision.HIGHEST
+    own_table = table_ref[0:80, :].astype(F32)[0:72]
+    other_table = table_ref[80:112, :].astype(F32)
+    lanes = table_ref[112:144, :].astype(F32)[0:NC]
+    mask = table_ref[144:272, :].astype(F32)
+    rest = table_ref[272:400, 0:256].astype(F32)
+    flip = rest[0:64, 128:192]
     for part in range(2):
         for k2 in range(2):
-            own = k_ref[part, :, k2].reshape(72, GRID)
-            mirror = (r0_ref, r1_ref)[k2][:, 64 * part : 64 * part + 64]
-            mirror = dot(mirror, flip_ref[...], precision=exact)
+            rows = slice(k2 * 64, k2 * 64 + 64)
+            own = k_ref[part, :, k2].reshape(72, GRID).T
+            k_out[0, part, rows, :] = dot(own, own_table, precision=exact)
+            mirror = mirror_ref[32 * k2 : 32 * k2 + 32, 64 * part : 64 * part + 64]
+            mirror = dot(mirror, flip, precision=exact).T
             if part == 1:
                 mirror = -mirror
-            both = jnp.concatenate([own, mirror], axis=0).T
-            k_out[part, k2 * 64 : k2 * 64 + 64, :] = dot(both, expand_ref[...], precision=exact)
-    spread = dot(coupling_ref[...], lanes_ref[...], ((0,), (0,)), precision=exact)
-    spread = dot(rows_ref[...], spread, precision=exact) * mask_ref[...]
+            k_out[1, part, rows, :] = dot(mirror, other_table, precision=exact)
+    spread = dot(coupling_ref[...], lanes, ((0,), (0,)), precision=exact)
+    spread = dot(rest[:, 0:NC], spread, precision=exact) * mask
     high, low = split(spread)
     c_out[...] = jnp.concatenate([high, low, high], axis=0)
 
 
 def middle_kernel(a_ref, forward_ref, c_ref, k_ref, inverse_ref, out_ref):
-    freq = dot(forward_ref[...], stacked(a_ref[...], 0))
+    value = jnp.concatenate([a_ref[:, sign].reshape(256, 128) for sign in range(2)], axis=1)
+    freq = dot(forward_ref[...], stacked(value, 0))
+    freq = jnp.concatenate([freq[:, 0:128], freq[:, 128:256]], axis=0)
     terms = dot(stacked(freq, 1), c_ref[...])
-    pieces = []
-    for k2 in range(2):
-        real = jnp.zeros((64, 128), F32)
-        imag = jnp.zeros((64, 128), F32)
-        for s in range(ORDER + 1):
-            lanes = slice(128 * s, 128 * s + 128)
-            tr = terms[k2 * 128 : k2 * 128 + 64, lanes]
-            ti = terms[k2 * 128 + 64 : k2 * 128 + 128, lanes]
-            kr = k_ref[0, k2 * 64 : k2 * 64 + 64, lanes]
-            ki = k_ref[1, k2 * 64 : k2 * 64 + 64, lanes]
-            real = real + kr * tr - ki * ti
-            imag = imag + kr * ti + ki * tr
-        pieces += [real, imag]
-    field = jnp.concatenate(pieces, axis=0)
-    out_ref[...] = dot(inverse_ref[...], stacked(field, 0))
+    fields = []
+    for sign in range(2):
+        pieces = []
+        for k2 in range(2):
+            real = jnp.zeros((64, 128), F32)
+            imag = jnp.zeros((64, 128), F32)
+            row = sign * 256 + k2 * 128
+            for s in range(ORDER + 1):
+                lanes = slice(128 * s, 128 * s + 128)
+                tr = terms[row : row + 64, lanes]
+                ti = terms[row + 64 : row + 128, lanes]
+                kr = k_ref[sign, 0, k2 * 64 : k2 * 64 + 64, lanes]
+                ki = k_ref[sign, 1, k2 * 64 : k2 * 64 + 64, lanes]
+                real = real + kr * tr - ki * ti
+                imag = imag + kr * ti + ki * tr
+            pieces += [real, imag]
+        fields.append(jnp.concatenate(pieces, axis=0))
+    result = dot(inverse_ref[...], stacked(jnp.concatenate(fields, axis=1), 0))
+    for sign in range(2):
+        out_ref[:, sign] = result[:, 128 * sign : 128 * sign + 128].reshape(32, 8, 128)
 
 
 def y_inverse_kernel(a_ref, table_ref, out_ref):
@@ -347,7 +379,7 @@
 Z_FORWARD, Z_INVERSE = z_tables()
 Y_FORWARD, Y_INVERSE = y_tables()
 X_FORWARD, X_INVERSE = x_tables()
-EXPAND, ROWS, LANES, MASK, FLIP = expand_tables()
+EXPAND = expand_tables()
 
 
 def block_rows(array):
@@ -355,6 +387,10 @@
     array = array.reshape(lead + (2, 32, 128))
     array = jnp.swapaxes(array, -3, -2)
     return array.reshape(-1, 128)
+
+
+def swap(array, partner):
+    return lax.ppermute(array, "narrow", [(n, n ^ partner) for n in range(8)])
 
 
 def shift(array, step):
@@ -369,37 +405,33 @@
     l2l = jnp.swapaxes(l2l_operators, 0, 1).reshape(NC * 8, NC)
     kernel = kernel_spectrum.transpose(0, 1, 3, 4, 2)
 
-    to_even = [(w * 8 + n, ((32 - w) % 32) * 8 + 7 - n) for w in range(32) for n in range(8)]
-    to_odd = [(w * 8 + n, (31 - w) * 8 + 7 - n) for w in range(32) for n in range(8)]
-    even, odd = call(pack_kernel, (shape(32, 128), shape(32, 128)), [pltpu.VMEM((72, 128), F32)])(kernel)
-    mirror0 = lax.ppermute(even, ("wide", "narrow"), to_even)
-    mirror1 = lax.ppermute(odd, ("wide", "narrow"), to_odd)
-
-    moments = call(head_kernel, shape(NC * 64, 128), [pltpu.VMEM((256, 128), F32)])(leaves, orders, octants, m2m)
+    packed = call(pack_kernel, shape(64, 128), [pltpu.VMEM((72, 128), F32)])(kernel)
+    mirror = lax.ppermute(packed, "narrow", [(n, 7 - n) for n in range(8)])
+    aux = [orders.astype(F32), octants.astype(F32), jnp.pad(m2m, ((0, 0), (0, 128 - NC)))]
+    moments = call(head_kernel, shape(NC * 64, 128))(leaves, jnp.concatenate(aux, axis=0))
     whole = pl.BlockSpec(memory_space=pltpu.VMEM)
     anywhere = pl.BlockSpec(memory_space=pl.ANY)
-    chunks = call(z_forward_kernel, shape(2048, 128), (), [whole] * 2 + [anywhere] * 2)(
-        moments, jnp.asarray(Z_FORWARD), mirror0, mirror1
+    chunks = call(z_forward_kernel, shape(2048, 128))(moments, jnp.asarray(Z_FORWARD))
+    chunks = chunks.reshape(8, 256, 128)
+    far = chunks[2] + swap(chunks[3], 1)
+    mid = chunks[4] + swap(chunks[5], 1)
+    near = swap(chunks[6:8].reshape(512, 128), 2)
+    own, across = call(meet_kernel, (shape(256, 128), shape(256, 128)), (), [whole] * 2 + [anywhere] * 3)(
+        chunks[0:2].reshape(512, 128), near, far, mid, mirror
     )
-    chunks = chunks.reshape(8, 256, 128)
-    far = shift(chunks[1] + shift(chunks[5], ACROSS), FAR)
-    across = chunks[4] + shift(chunks[6], ABOVE) + shift(chunks[7], BELOW)
-    received = [chunks[0], far, shift(chunks[2], ABOVE), shift(chunks[3], BELOW), shift(across, ACROSS)]
-
-    kernels, couplings = call(prepare_kernel, (shape(2, 128, 640), shape(384, 640, dtype=BF)))(
-        kernel, mirror0, mirror1, coupling,
-        jnp.asarray(EXPAND), jnp.asarray(ROWS), jnp.asarray(LANES), jnp.asarray(MASK), jnp.asarray(FLIP),
+    received = [own, swap(far, 4), swap(mid, 6), swap(across, 1)]
+
+    kernels, couplings = call(prepare_kernel, (shape(2, 2, 128, 640), shape(384, 640, dtype=BF)))(
+        kernel, mirror, coupling, jnp.asarray(EXPAND)
     )
 
-    along = call(y_forward_kernel, shape(256, 128), (), [whole] * 6 + [anywhere])(
-        *received, jnp.asarray(Y_FORWARD), kernels
+    along = call(y_forward_kernel, shape(512, 128), (), [whole] * 5 + [anywhere])(*received, jnp.asarray(Y_FORWARD), kernels)
+    along = lax.all_to_all(along.reshape(32, 16, 128), "wide", split_axis=0, concat_axis=0, tiled=True)
+    along = call(middle_kernel, shape(32, 2, 8, 128))(
+        along.reshape(32, 2, 8, 128), jnp.asarray(X_FORWARD), couplings, kernels, jnp.asarray(X_INVERSE)
     )
-    along = lax.all_to_all(along.reshape(32, 8, 128), "wide", split_axis=0, concat_axis=0, tiled=True)
-    along = call(middle_kernel, shape(256, 128))(
-        along.reshape(256, 128), jnp.asarray(X_FORWARD), couplings, kernels, jnp.asarray(X_INVERSE)
-    )
-    along = lax.all_to_all(along.reshape(32, 8, 128), "wide", split_axis=0, concat_axis=0, tiled=True)
-    plane = call(y_inverse_kernel, shape(256, 128))(along.reshape(256, 128), jnp.asarray(Y_INVERSE))
+    along = lax.all_to_all(along.reshape(32, 16, 128), "wide", split_axis=0, concat_axis=0, tiled=True)
+    plane = call(y_inverse_kernel, shape(256, 128))(along.reshape(512, 128), jnp.asarray(Y_INVERSE))
 
     other = shift(plane, ACROSS)
     far = shift(plane, FAR)

time: 96.8 us -> 94.6 us (0.977)
  starting transfers between devices: 26.7 us -> 20.8 us
  blocking collectives: 36.9 us -> 41.6 us
  waiting for transfers between devices: 15.4 us -> 12.2 us
  other arithmetic: 0.08 us -> 2.53 us
  local copies, waits for them, and re-layouts: 2.9 us -> 1.25 us
  Pallas kernels: 14.3 us -> 15.7 us
    ppermute x14 -> x7, waiting for transfers between devices: 15.4 us -> 5.44 us  [shift(): lax.ppermute(array, 'narrow', [(n, stepped(n, step, 1)) for n in range(8)])]
    ppermute x14 -> x7, starting transfers between devices: 17.8 us -> 9.97 us  [shift(): lax.ppermute(array, 'narrow', [(n, stepped(n, step, 1)) for n in range(8)])]
    ppermute x2 -> x7, waiting for transfers between devices: 0.01 us -> 6.76 us  [the longest x6 5.97 us: swap(): return lax.ppermute(array, 'narrow', [(n, n ^ partner) for n in range(8)])]
    all_to_all x2, blocking collectives: 36.9 us -> 41.6 us  [shards(): lax.all_to_all(along.reshape(32, 16, 128), 'wide', split_axis=0, concat_a...]
    ppermute x2 -> x7, starting transfers between devices: 8.86 us -> 10.8 us  [the longest x6 8.11 us: swap(): return lax.ppermute(array, 'narrow', [(n, n ^ partner) for n in range(8)])]
    unnamed x38 -> x24, local copies, waits for them, and re-layouts: 2.88 us -> 1.2 us
    convert_element_type x0 -> x2, other arithmetic: none -> 1.58 us  [the longest x1 0.82 us: shards(): orders.astype(F32)]
    pallas_call x6 -> x7, Pallas kernels: 8.1 us -> 9.44 us  [the longest x1 2.69 us: shards(): call(prepare_kernel, (shape(2, 2, 128, 640), shape(384, 640, dtype=BF)))]
  transfers between devices with their start and end apart: 16 -> 14, of which waited for: 8 -> 10; matrix products, arithmetic and copies ran while one was open for 0% -> 0% of each run, Pallas kernels for 5% -> 3%
where the time goes in v3:
time: 94.6 us; the launch traced here: 94.3 us
  blocking collectives  41.6 us (44%)
  starting transfers between devices  20.8 us (22%)
  Pallas kernels  15.7 us (17%)
  waiting for transfers between devices  12.2 us (13%)
  other arithmetic  2.53 us (3%)
  local copies, waits for them, and re-layouts  1.25 us (1%)
    all_to_all x2, blocking collectives, shards(): lax.all_to_all(along.reshape(32, 16, 128), 'wide', split_axis=0, concat_a...  41.6 us
    ppermute x7, starting transfers between devices, shift(): lax.ppermute(array, 'narrow', [(n, stepped(n, step, 1)) for n in range(8)])  9.97 us
    ppermute x6, starting transfers between devices, swap(): return lax.ppermute(array, 'narrow', [(n, n ^ partner) for n in range(8)])  8.11 us
    ppermute x6, waiting for transfers between devices, swap(): return lax.ppermute(array, 'narrow', [(n, n ^ partner) for n in range(8)])  5.97 us
    ppermute x7, waiting for transfers between devices, shift(): lax.ppermute(array, 'narrow', [(n, stepped(n, step, 1)) for n in range(8)])  5.44 us
    pallas_call x1, Pallas kernels, shards(): call(tail_kernel, shape(NC * 64, 128), [pltpu.VMEM((256, 128), F32)])  3.53 us
    pallas_call x1, Pallas kernels, shards(): call(prepare_kernel, (shape(2, 2, 128, 640), shape(384, 640, dtype=BF)))  2.69 us
    ppermute x1, starting transfers between devices, shards(): mirror = lax.ppermute(packed, 'narrow', [(n, 7 - n) for n in range(8)])  2.69 us
  transfers between devices with their start and end apart: 14, of which 10 were waited for; matrix products, arithmetic and copies ran while one was open for 0% of the time, Pallas kernels for 3%

profile of v3, /device:TPU:2, one launch (start us, length us, event | category | flops | bytes accessed | tf_op | source)
XLA Modules:
  0.0 94.3 jit_solution(4988530139699726375)
XLA Ops:
  0.0 0.8 convert_element_type.17
  0.8 0.8 convert_element_type.21
  1.6 0.9 select_maximum_fusion.aux_ref
  2.5 1.1 %copy-done = f32[1,25,2,4096]{3,2,1,0:T(2,128)S(1)} copy-done((f32[1,25,2,4096]{3,2,1,0:T(2,128)S(1)}, f32[1,25,2,4096]{3,2,1,0:T(2,128)}, u32[]{:S(2)}) %copy-start) | copy-done | bytes 819224
  3.6 2.6 %shard_map.136.ms = f32[1600,128]{1,0:T(8,128)S(1)} custom-call(f32[1600,128]{1,0:T(8,128)S(1)} %bitcast.35, f32[328,128]{1,0:T(8,128)S(1)} %select_maximum_fusion.aux_ref), custom_call_target="tpu_custom_call" | custom-call | tf_op jit(solution)/shard_map/pallas_call | solution.py:411
  6.3 2.3 %shard_map.137 = f32[2048,128]{1,0:T(8,128)S(1)} custom-call(f32[1600,128]{1,0:T(8,128)S(1)} %shard_map.136.ms, bf16[8,80,192]{2,1,0:T(8,128)(2,1)S(1)} %copy-done.7), custom_call_target="tpu_custom_call" | custom-call | tf_op jit(solution)/shard_map/pallas_call | solution.py:414
  8.6 2.4 %collective-permute-start.2 = (f32[256,128]{1,0:T(8,128)S(1)}, f32[256,128]{1,0:T(8,128)S(1)}, u32[]{:S(2)}, u32[]{:S(2)}) collective-permute-start(f32[256,128]{1,0:T(8,128)S(1)} %slice.35), channel_id=1, source_target_pairs={{0,1},{1,0},{2,3},{3,2},{4,5},{5,4},{6,7},{7,6},{8,9},{9,8},{10,11... | collective-permute-start | bytes 393224 | tf_op jit(solution)/shard_map/ppermute | solution.py:393
  11.0 3.1 %collective-permute-done.2 = f32[256,128]{1,0:T(8,128)S(1)} collective-permute-done((f32[256,128]{1,0:T(8,128)S(1)}, f32[256,128]{1,0:T(8,128)S(1)}, u32[]{:S(2)}, u32[]{:S(2)}) %collective-permute-start.2) | collective-permute-done | bytes 131104 | tf_op jit(solution)/shard_map/ppermute | solution.py:393
  14.1 2.6 %collective-permute-start.1 = (f32[256,128]{1,0:T(8,128)S(1)}, f32[256,128]{1,0:T(8,128)S(1)}, u32[]{:S(2)}, u32[]{:S(2)}) collective-permute-start(f32[256,128]{1,0:T(8,128)S(1)} %get-tuple-element.14), channel_id=1, source_target_pairs={{0,1},{1,0},{2,3},{3,2},{4,5},{5,4},{6,7},{7,6},{8,9},{9,8},{10,11... | collective-permute-start | bytes 393224 | tf_op jit(solution)/shard_map/ppermute | solution.py:393
  16.9 2.7 %collective-permute-start.3 = (f32[64,128]{1,0:T(8,128)S(1)}, f32[64,128]{1,0:T(8,128)S(1)}, u32[]{:S(2)}, u32[]{:S(2)}) collective-permute-start(f32[64,128]{1,0:T(8,128)S(1)} %shard_map.138), channel_id=1, source_target_pairs={{0,7},{1,6},{2,5},{3,4},{4,3},{5,2},{6,1},{7,0},{8,15},{9,14},{10,... | collective-permute-start | bytes 98312 | tf_op jit(solution)/shard_map/ppermute | solution.py:409
  19.6 1.1 %collective-permute-start.5 = (f32[256,128]{1,0:T(8,128)S(1)}, f32[256,128]{1,0:T(8,128)S(1)}, u32[]{:S(2)}, u32[]{:S(2)}) collective-permute-start(f32[256,128]{1,0:T(8,128)S(1)} %get-tuple-element.13._1), channel_id=1, source_target_pairs={{0,6},{1,7},{2,4},{3,5},{4,2},{5,3},{6,0},{7,1},{8,14},{9,15},{10,... | collective-permute-start | bytes 393224 | tf_op jit(solution)/shard_map/ppermute | solution.py:393
  20.7 1.8 %collective-permute-start.4 = (f32[256,128]{1,0:T(8,128)S(1)}, f32[256,128]{1,0:T(8,128)S(1)}, u32[]{:S(2)}, u32[]{:S(2)}) collective-permute-start(f32[256,128]{1,0:T(8,128)S(1)} %slice_add_fusion.1._0), channel_id=1, source_target_pairs={{0,4},{1,5},{2,6},{3,7},{4,0},{5,1},{6,2},{7,3},{8,12},{9,13},{10,... | collective-permute-start | bytes 393224 | tf_op jit(solution)/shard_map/ppermute | solution.py:393
  22.5 0.8 collective-permute-done.3._2.mirror_ref
  23.3 0.8 collective-permute-done.near_ref
  24.3 2.7 %shard_map.140 = (f32[2,2,128,640]{3,2,1,0:T(8,128)S(1)}, bf16[384,640]{1,0:T(8,128)(2,1)S(1)}) custom-call(f32[2,9,2,8,64]{4,3,2,1,0:T(8,128)S(1)} %bitcast.37, f32[64,128]{1,0:T(8,128)S(1)} %collective-permute-done.3._2.mirror_ref, f32[25,25]{1,0:T(8,128)S(1)} %copy-done.11, bf16[400,640]{1,0:T(8,128)(2,1)S(1)} %copy-done.4), custom_call_target="tpu_custom_call" | custom-call | tf_op jit(solution)/shard_map/pallas_call | solution.py:424
  27.0 0.8 collective-permute-done.5.refs_2_
  27.8 1.3 %collective-permute-done.6.refs_3_ = f32[256,128]{1,0:T(8,128)S(1)} collective-permute-done((f32[256,128]{1,0:T(8,128)S(1)}, f32[256,128]{1,0:T(8,128)S(1)}, u32[]{:S(2)}, u32[]{:S(2)}) %collective-permute-start.6) | collective-permute-done | bytes 131104 | tf_op jit(solution)/shard_map/ppermute | solution.py:393
  29.5 23.8 %all_to_all.10 = f32[32,16,128]{2,1,0:T(8,128)S(1)} all-to-all(f32[32,16,128]{2,1,0:T(8,128)S(1)} %bitcast.34), channel_id=1, replica_groups=mesh['wide'=32,'narrow'=8] {'wide'}, dimensions={0} | all-to-all | bytes 524288 | tf_op jit(solution)/shard_map/all_to_all | solution.py:429
  53.3 1.4 %shard_map.142 = f32[32,2,8,128]{3,2,1,0:T(8,128)S(1)} custom-call(f32[32,2,8,128]{3,2,1,0:T(8,128)S(1)} %bitcast.31, bf16[256,768]{1,0:T(8,128)(2,1)S(1)} %copy-done.6, bf16[384,640]{1,0:T(8,128)(2,1)S(1)} %get-tuple-element.12.c_ref, f32[2,2,128,640]{3,2,1,0:T(8,128)S(1)} %get-tuple-element.11.refs_5_.k_ref, bf16[256,768]{1,0:T(8,128)(2,1)S(1)} %copy-done.5), custom_call_target="tpu_custom_call" | custom-call | tf_op jit(solution)/shard_map/pallas_call | solution.py:430
  54.7 17.8 %all_to_all.11 = f32[32,16,128]{2,1,0:T(8,128)S(1)} all-to-all(f32[32,16,128]{2,1,0:T(8,128)S(1)} %bitcast.32), channel_id=1, replica_groups=mesh['wide'=32,'narrow'=8] {'wide'}, dimensions={0} | all-to-all | bytes 524288 | tf_op jit(solution)/shard_map/all_to_all | solution.py:433
  72.9 2.0 %collective-permute-start.10 = (f32[256,128]{1,0:T(8,128)S(1)}, f32[256,128]{1,0:T(8,128)S(1)}, u32[]{:S(2)}, u32[]{:S(2)}) collective-permute-start(f32[256,128]{1,0:T(8,128)S(1)} %shard_map.143.refs_0_), channel_id=1, source_target_pairs={{0,1},{1,0},{2,3},{3,2},{4,5},{5,4},{6,7},{7,6},{8,9},{9,8},{10,11... | collective-permute-start | bytes 393224 | tf_op jit(solution)/shard_map/ppermute | solution.py:397
  74.9 3.4 %collective-permute-start.7 = (f32[256,128]{1,0:T(8,128)S(1)}, f32[256,128]{1,0:T(8,128)S(1)}, u32[]{:S(2)}, u32[]{:S(2)}) collective-permute-start(f32[256,128]{1,0:T(8,128)S(1)} %shard_map.143.refs_0_), channel_id=1, source_target_pairs={{0,4},{1,5},{2,6},{3,7},{4,0},{5,1},{6,2},{7,3},{8,12},{9,13},{10,... | collective-permute-start | bytes 393224 | tf_op jit(solution)/shard_map/ppermute | solution.py:397
  78.3 0.5 collective-permute-start.9
  78.9 1.5 %collective-permute-start.8 = (f32[256,128]{1,0:T(8,128)S(1)}, f32[256,128]{1,0:T(8,128)S(1)}, u32[]{:S(2)}, u32[]{:S(2)}) collective-permute-start(f32[256,128]{1,0:T(8,128)S(1)} %shard_map.143.refs_0_), channel_id=1, source_target_pairs={{0,2},{1,3},{2,4},{3,5},{4,6},{5,7},{6,0},{7,1},{8,10},{9,11},{10,... | collective-permute-start | bytes 393224 | tf_op jit(solution)/shard_map/ppermute | solution.py:397
  80.4 1.8 %collective-permute-start.13 = (f32[256,128]{1,0:T(8,128)S(1)}, f32[256,128]{1,0:T(8,128)S(1)}, u32[]{:S(2)}, u32[]{:S(2)}) collective-permute-start(f32[256,128]{1,0:T(8,128)S(1)} %collective-permute-done.10.refs_4_), channel_id=1, source_target_pairs={{0,6},{1,7},{2,0},{3,1},{4,2},{5,3},{6,4},{7,5},{8,14},{9,15},{10,... | collective-permute-start | bytes 393224 | tf_op jit(solution)/shard_map/ppermute | solution.py:397
  82.7 0.5 collective-permute-start.11
  83.1 2.2 %collective-permute-done.9.refs_3_ = f32[256,128]{1,0:T(8,128)S(1)} collective-permute-done((f32[256,128]{1,0:T(8,128)S(1)}, f32[256,128]{1,0:T(8,128)S(1)}, u32[]{:S(2)}, u32[]{:S(2)}) %collective-permute-start.9) | collective-permute-done | bytes 131104 | tf_op jit(solution)/shard_map/ppermute | solution.py:397
  85.3 1.0 %collective-permute-done.8.refs_2_ = f32[256,128]{1,0:T(8,128)S(1)} collective-permute-done((f32[256,128]{1,0:T(8,128)S(1)}, f32[256,128]{1,0:T(8,128)S(1)}, u32[]{:S(2)}, u32[]{:S(2)}) %collective-permute-start.8) | collective-permute-done | bytes 131104 | tf_op jit(solution)/shard_map/ppermute | solution.py:397
  86.3 0.4 collective-permute-done.13.refs_7_
  86.7 1.6 %collective-permute-done.12.refs_6_ = f32[256,128]{1,0:T(8,128)S(1)} collective-permute-done((f32[256,128]{1,0:T(8,128)S(1)}, f32[256,128]{1,0:T(8,128)S(1)}, u32[]{:S(2)}, u32[]{:S(2)}) %collective-permute-start.12) | collective-permute-done | bytes 131104 | tf_op jit(solution)/shard_map/ppermute | solution.py:397
  88.3 2.4 %shard_map.144.local_ref = f32[1600,128]{1,0:T(8,128)S(1)} custom-call(f32[256,128]{1,0:T(8,128)S(1)} %shard_map.143.refs_0_, f32[256,128]{1,0:T(8,128)S(1)} %collective-permute-done.7.refs_1_, f32[256,128]{1,0:T(8,128)S(1)} %collective-permute-done.8.refs_2_, f32[256,128]{1,0:T(8,128)S(1)} %collective-permute-done.9.refs_3_, ...), custom_call_target="tpu_custom_call" | custom-call | tf_op jit(solution)/shard_map/pallas_call | solution.py:441
  90.8 3.5 %shard_map.145 = f32[1600,128]{1,0:T(8,128)} custom-call(f32[1600,128]{1,0:T(8,128)S(1)} %shard_map.144.local_ref, s32[64,128]{1,0:T(8,128)S(1)} %bitcast.39, f32[200,25]{1,0:T(8,128)S(1)} %bitcast.40), custom_call_target="tpu_custom_call" | custom-call | tf_op jit(solution)/shard_map/pallas_call | solution.py:442
  (39 shorter events, 1.9 us)
Async XLA Ops:
  0.0 6.3 %copy-start.7 = (bf16[8,80,192]{2,1,0:T(8,128)(2,1)S(1)}, bf16[8,80,192]{2,1,0:T(8,128)(2,1)}, u32[]{:S(2)}) copy-start(bf16[8,80,192]{2,1,0:T(8,128)(2,1)} %constant.17.clone.table_ref) | copy-start | bytes 737284
  2.5 1.1 %copy-start = (f32[1,25,2,4096]{3,2,1,0:T(2,128)S(1)}, f32[1,25,2,4096]{3,2,1,0:T(2,128)}, u32[]{:S(2)}) copy-start(f32[1,25,2,4096]{3,2,1,0:T(2,128)} %param.14) | copy-start | bytes 2457604
  8.6 8.2 %copy-start.3 = (f32[2,9,64,2,8]{2,4,3,1,0:T(8,128)S(1)}, f32[2,9,64,2,8]{2,4,3,1,0:T(8,128)}, u32[]{:S(2)}) copy-start(f32[2,9,64,2,8]{2,4,3,1,0:T(8,128)} %param.19) | copy-start | bytes 221188
  8.6 5.4 %collective-permute-start.2 = (f32[256,128]{1,0:T(8,128)S(1)}, f32[256,128]{1,0:T(8,128)S(1)}, u32[]{:S(2)}, u32[]{:S(2)}) collective-permute-start(f32[256,128]{1,0:T(8,128)S(1)} %slice.35), channel_id=1, source_target_pairs={{0,1},{1,0},{2,3},{3,2},{4,5},{5,4},{6,7},{7,6},{8,9},{9,8},{10,11... | collective-permute-start | bytes 393224 | tf_op jit(solution)/shard_map/ppermute | solution.py:393
  14.1 10.3 %copy-start.4 = (bf16[400,640]{1,0:T(8,128)(2,1)S(1)}, bf16[400,640]{1,0:T(8,128)(2,1)}, u32[]{:S(2)}) copy-start(bf16[400,640]{1,0:T(8,128)(2,1)} %constant.18.clone.table_ref) | copy-start | bytes 1536004
  14.1 10.3 %copy-start.11 = (f32[25,25]{1,0:T(8,128)S(1)}, f32[25,25]{1,0:T(8,128)}, u32[]{:S(2)}) copy-start(f32[25,25]{1,0:T(8,128)} %coupling_ref.1) | copy-start | bytes 7504
  14.1 6.6 %collective-permute-start.1 = (f32[256,128]{1,0:T(8,128)S(1)}, f32[256,128]{1,0:T(8,128)S(1)}, u32[]{:S(2)}, u32[]{:S(2)}) collective-permute-start(f32[256,128]{1,0:T(8,128)S(1)} %get-tuple-element.14), channel_id=1, source_target_pairs={{0,1},{1,0},{2,3},{3,2},{4,5},{5,4},{6,7},{7,6},{8,9},{9,8},{10,11... | collective-permute-start | bytes 393224 | tf_op jit(solution)/shard_map/ppermute | solution.py:393
  16.7 12.4 %copy-start.2 = (bf16[512,768]{1,0:T(8,128)(2,1)S(1)}, bf16[512,768]{1,0:T(8,128)(2,1)}, u32[]{:S(2)}) copy-start(bf16[512,768]{1,0:T(8,128)(2,1)} %constant.19.clone.refs_4_) | copy-start | bytes 2359300
  16.7 7.3 %collective-permute-start = (f32[512,128]{1,0:T(8,128)S(1)}, f32[512,128]{1,0:T(8,128)S(1)}, u32[]{:S(2)}, u32[]{:S(2)}) collective-permute-start(f32[512,128]{1,0:T(8,128)S(1)} %get-tuple-element.15), channel_id=1, source_target_pairs={{0,2},{1,3},{2,0},{3,1},{4,6},{5,7},{6,4},{7,5},{8,10},{9,11},{10,... | collective-permute-start | bytes 786440 | tf_op jit(solution)/shard_map/ppermute | solution.py:393
  16.9 6.3 %collective-permute-start.3 = (f32[64,128]{1,0:T(8,128)S(1)}, f32[64,128]{1,0:T(8,128)S(1)}, u32[]{:S(2)}, u32[]{:S(2)}) collective-permute-start(f32[64,128]{1,0:T(8,128)S(1)} %shard_map.138), channel_id=1, source_target_pairs={{0,7},{1,6},{2,5},{3,4},{4,3},{5,2},{6,1},{7,0},{8,15},{9,14},{10,... | collective-permute-start | bytes 98312 | tf_op jit(solution)/shard_map/ppermute | solution.py:409
  19.6 8.2 %collective-permute-start.5 = (f32[256,128]{1,0:T(8,128)S(1)}, f32[256,128]{1,0:T(8,128)S(1)}, u32[]{:S(2)}, u32[]{:S(2)}) collective-permute-start(f32[256,128]{1,0:T(8,128)S(1)} %get-tuple-element.13._1), channel_id=1, source_target_pairs={{0,6},{1,7},{2,4},{3,5},{4,2},{5,3},{6,0},{7,1},{8,14},{9,15},{10,... | collective-permute-start | bytes 393224 | tf_op jit(solution)/shard_map/ppermute | solution.py:393
  20.7 7.1 %collective-permute-start.4 = (f32[256,128]{1,0:T(8,128)S(1)}, f32[256,128]{1,0:T(8,128)S(1)}, u32[]{:S(2)}, u32[]{:S(2)}) collective-permute-start(f32[256,128]{1,0:T(8,128)S(1)} %slice_add_fusion.1._0), channel_id=1, source_target_pairs={{0,4},{1,5},{2,6},{3,7},{4,0},{5,1},{6,2},{7,3},{8,12},{9,13},{10,... | collective-permute-start | bytes 393224 | tf_op jit(solution)/shard_map/ppermute | solution.py:393
  24.1 5.1 %collective-permute-start.6 = (f32[256,128]{1,0:T(8,128)S(1)}, f32[256,128]{1,0:T(8,128)S(1)}, u32[]{:S(2)}, u32[]{:S(2)}) collective-permute-start(f32[256,128]{1,0:T(8,128)S(1)} %get-tuple-element.10), channel_id=1, source_target_pairs={{0,1},{1,0},{2,3},{3,2},{4,5},{5,4},{6,7},{7,6},{8,9},{9,8},{10,11... | collective-permute-start | bytes 393224 | tf_op jit(solution)/shard_map/ppermute | solution.py:393
  29.1 24.2 %copy-start.5 = (bf16[256,768]{1,0:T(8,128)(2,1)S(1)}, bf16[256,768]{1,0:T(8,128)(2,1)}, u32[]{:S(2)}) copy-start(bf16[256,768]{1,0:T(8,128)(2,1)} %constant.21.clone.inverse_ref) | copy-start | bytes 1179652
  29.1 24.2 %copy-start.6 = (bf16[256,768]{1,0:T(8,128)(2,1)S(1)}, bf16[256,768]{1,0:T(8,128)(2,1)}, u32[]{:S(2)}) copy-start(bf16[256,768]{1,0:T(8,128)(2,1)} %constant.20.clone.forward_ref) | copy-start | bytes 1179652
  53.3 19.2 %copy-start.1 = (bf16[1536,256]{1,0:T(8,128)(2,1)S(1)}, bf16[1536,256]{1,0:T(8,128)(2,1)}, u32[]{:S(2)}) copy-start(bf16[1536,256]{1,0:T(8,128)(2,1)} %constant.22.clone.table_ref) | copy-start | bytes 2359300
  54.7 33.6 %copy-start.8 = (bf16[8,64,240]{2,1,0:T(8,128)(2,1)S(1)}, bf16[8,64,240]{2,1,0:T(8,128)(2,1)}, u32[]{:S(2)}) copy-start(bf16[8,64,240]{2,1,0:T(8,128)(2,1)} %constant.23.clone.refs_8_) | copy-start | bytes 737284
  72.9 17.9 %copy-start.9 = (s32[1,2,4096]{2,1,0:T(2,128)S(1)}, s32[1,2,4096]{2,1,0:T(2,128)}, u32[]{:S(2)}) copy-start(s32[1,2,4096]{2,1,0:T(2,128)} %param.16) | copy-start | bytes 98308
  72.9 17.9 %copy-start.10 = (f32[8,25,25]{2,0,1:T(8,128)S(1)}, f32[8,25,25]{2,0,1:T(8,128)}, u32[]{:S(2)}) copy-start(f32[8,25,25]{2,0,1:T(8,128)} %param.20) | copy-start | bytes 60004
  72.9 7.5 %collective-permute-start.10 = (f32[256,128]{1,0:T(8,128)S(1)}, f32[256,128]{1,0:T(8,128)S(1)}, u32[]{:S(2)}, u32[]{:S(2)}) collective-permute-start(f32[256,128]{1,0:T(8,128)S(1)} %shard_map.143.refs_0_), channel_id=1, source_target_pairs={{0,1},{1,0},{2,3},{3,2},{4,5},{5,4},{6,7},{7,6},{8,9},{9,8},{10,11... | collective-permute-start | bytes 393224 | tf_op jit(solution)/shard_map/ppermute | solution.py:397
  74.9 7.7 %collective-permute-start.7 = (f32[256,128]{1,0:T(8,128)S(1)}, f32[256,128]{1,0:T(8,128)S(1)}, u32[]{:S(2)}, u32[]{:S(2)}) collective-permute-start(f32[256,128]{1,0:T(8,128)S(1)} %shard_map.143.refs_0_), channel_id=1, source_target_pairs={{0,4},{1,5},{2,6},{3,7},{4,0},{5,1},{6,2},{7,3},{8,12},{9,13},{10,... | collective-permute-start | bytes 393224 | tf_op jit(solution)/shard_map/ppermute | solution.py:397
  78.3 7.0 %collective-permute-start.9 = (f32[256,128]{1,0:T(8,128)S(1)}, f32[256,128]{1,0:T(8,128)S(1)}, u32[]{:S(2)}, u32[]{:S(2)}) collective-permute-start(f32[256,128]{1,0:T(8,128)S(1)} %shard_map.143.refs_0_), channel_id=1, source_target_pairs={{0,6},{1,7},{2,0},{3,1},{4,2},{5,3},{6,4},{7,5},{8,14},{9,15},{10,... | collective-permute-start | bytes 393224 | tf_op jit(solution)/shard_map/ppermute | solution.py:397
  78.9 7.5 %collective-permute-start.8 = (f32[256,128]{1,0:T(8,128)S(1)}, f32[256,128]{1,0:T(8,128)S(1)}, u32[]{:S(2)}, u32[]{:S(2)}) collective-permute-start(f32[256,128]{1,0:T(8,128)S(1)} %shard_map.143.refs_0_), channel_id=1, source_target_pairs={{0,2},{1,3},{2,4},{3,5},{4,6},{5,7},{6,0},{7,1},{8,10},{9,11},{10,... | collective-permute-start | bytes 393224 | tf_op jit(solution)/shard_map/ppermute | solution.py:397
  80.4 6.4 %collective-permute-start.13 = (f32[256,128]{1,0:T(8,128)S(1)}, f32[256,128]{1,0:T(8,128)S(1)}, u32[]{:S(2)}, u32[]{:S(2)}) collective-permute-start(f32[256,128]{1,0:T(8,128)S(1)} %collective-permute-done.10.refs_4_), channel_id=1, source_target_pairs={{0,6},{1,7},{2,0},{3,1},{4,2},{5,3},{6,4},{7,5},{8,14},{9,15},{10,... | collective-permute-start | bytes 393224 | tf_op jit(solution)/shard_map/ppermute | solution.py:397
  82.1 6.2 %collective-permute-start.12 = (f32[256,128]{1,0:T(8,128)S(1)}, f32[256,128]{1,0:T(8,128)S(1)}, u32[]{:S(2)}, u32[]{:S(2)}) collective-permute-start(f32[256,128]{1,0:T(8,128)S(1)} %collective-permute-done.10.refs_4_), channel_id=1, source_target_pairs={{0,2},{1,3},{2,4},{3,5},{4,6},{5,7},{6,0},{7,1},{8,10},{9,11},{10,... | collective-permute-start | bytes 393224 | tf_op jit(solution)/shard_map/ppermute | solution.py:397
  82.7 5.6 %collective-permute-start.11 = (f32[256,128]{1,0:T(8,128)S(1)}, f32[256,128]{1,0:T(8,128)S(1)}, u32[]{:S(2)}, u32[]{:S(2)}) collective-permute-start(f32[256,128]{1,0:T(8,128)S(1)} %collective-permute-done.7.refs_1_), channel_id=1, source_target_pairs={{0,1},{1,0},{2,3},{3,2},{4,5},{5,4},{6,7},{7,6},{8,9},{9,8},{10,11... | collective-permute-start | bytes 393224 | tf_op jit(solution)/shard_map/ppermute | solution.py:397

commit v4 on v3

--- a/solution.py
+++ b/solution.py
@@ -194,8 +194,8 @@
     return total, last
 
 
-GROUP = 8
-BATCH = 5
+GROUP = 32
+BATCH = 25
 
 
 def head_kernel(leaf_ref, aux_ref, out_ref):
@@ -238,6 +238,11 @@
     lax.fori_loop(0, NC // BATCH, coefficients, 0)
 
 
+def lift_kernel(far_ref, mid_ref, far_other, mid_other, far_out, mid_out):
+    far_out[...] = far_ref[...] + far_other[...]
+    mid_out[...] = mid_ref[...] + mid_other[...]
+
+
 def meet_kernel(here_ref, near_ref, _0, _1, _2, own_ref, across_ref):
     own_ref[...] = here_ref[0:256, :] + near_ref[0:256, :]
     across_ref[...] = here_ref[256:512, :] + near_ref[256:512, :]
@@ -261,27 +266,33 @@
             send_ref[first : first + 9, :] = rows[pl.ds(5 + i, 9, stride=8), :]
 
 
+def spread(value, table):
+    high, low = split(value)
+    return dot(high, table) + dot(low, table)
+
+
 def prepare_kernel(k_ref, mirror_ref, coupling_ref, table_ref, k_out, c_out):
-    exact = lax.Precision.HIGHEST
-    own_table = table_ref[0:80, :].astype(F32)[0:72]
-    other_table = table_ref[80:112, :].astype(F32)
-    lanes = table_ref[112:144, :].astype(F32)[0:NC]
+    own_table = table_ref[0:80, :]
+    other_table = table_ref[80:112, :]
+    lanes = table_ref[112:144, :]
     mask = table_ref[144:272, :].astype(F32)
     rest = table_ref[272:400, 0:256].astype(F32)
-    flip = rest[0:64, 128:192]
+    flip = rest[0:64, 128:192].astype(BF)
+    rows = rest[:, 0:32].astype(BF)
+    zeros = jnp.zeros((8, GRID), F32)
     for part in range(2):
         for k2 in range(2):
-            rows = slice(k2 * 64, k2 * 64 + 64)
-            own = k_ref[part, :, k2].reshape(72, GRID).T
-            k_out[0, part, rows, :] = dot(own, own_table, precision=exact)
+            place = slice(k2 * 64, k2 * 64 + 64)
+            own = jnp.concatenate([k_ref[part, :, k2].reshape(72, GRID), zeros], axis=0).T
+            k_out[0, part, place, :] = spread(own, own_table)
             mirror = mirror_ref[32 * k2 : 32 * k2 + 32, 64 * part : 64 * part + 64]
-            mirror = dot(mirror, flip, precision=exact).T
+            mirror = spread(mirror, flip).T
             if part == 1:
                 mirror = -mirror
-            k_out[1, part, rows, :] = dot(mirror, other_table, precision=exact)
-    spread = dot(coupling_ref[...], lanes, ((0,), (0,)), precision=exact)
-    spread = dot(rest[:, 0:NC], spread, precision=exact) * mask
-    high, low = split(spread)
+            k_out[1, part, place, :] = spread(mirror, other_table)
+    high, low = split(spread(coupling_ref[...].T, lanes))
+    placed = (dot(rows, high) + dot(rows, low)) * mask
+    high, low = split(placed)
     c_out[...] = jnp.concatenate([high, low, high], axis=0)
 
 
@@ -413,8 +424,9 @@
     anywhere = pl.BlockSpec(memory_space=pl.ANY)
     chunks = call(z_forward_kernel, shape(2048, 128))(moments, jnp.asarray(Z_FORWARD))
     chunks = chunks.reshape(8, 256, 128)
-    far = chunks[2] + swap(chunks[3], 1)
-    mid = chunks[4] + swap(chunks[5], 1)
+    far, mid = call(lift_kernel, (shape(256, 128), shape(256, 128)))(
+        chunks[2], chunks[4], swap(chunks[3], 1), swap(chunks[5], 1)
+    )
     near = swap(chunks[6:8].reshape(512, 128), 2)
     own, across = call(meet_kernel, (shape(256, 128), shape(256, 128)), (), [whole] * 2 + [anywhere] * 3)(
         chunks[0:2].reshape(512, 128), near, far, mid, mirror
@@ -422,7 +434,7 @@
     received = [own, swap(far, 4), swap(mid, 6), swap(across, 1)]
 
     kernels, couplings = call(prepare_kernel, (shape(2, 2, 128, 640), shape(384, 640, dtype=BF)))(
-        kernel, mirror, coupling, jnp.asarray(EXPAND)
+        kernel, mirror, jnp.pad(coupling, ((0, 32 - NC), (0, 32 - NC))), jnp.asarray(EXPAND)
     )
 
     along = call(y_forward_kernel, shape(512, 128), (), [whole] * 5 + [anywhere])(*received, jnp.asarray(Y_FORWARD), kernels)

time: 94.6 us -> 89.3 us (0.944)
  Pallas kernels: 15.7 us -> 10.9 us
  starting transfers between devices: 20.8 us -> 17.5 us
  waiting for transfers between devices: 12.2 us -> 14 us
  blocking collectives: 41.6 us -> 42.7 us
    ppermute x7, starting transfers between devices: 9.97 us -> 7.31 us  [shift(): lax.ppermute(array, 'narrow', [(n, stepped(n, step, 1)) for n in range(8)])]
    ppermute x7, waiting for transfers between devices: 5.44 us -> 7.02 us  [shift(): lax.ppermute(array, 'narrow', [(n, stepped(n, step, 1)) for n in range(8)])]
    pallas_call x1, Pallas kernels: 2.43 us -> 1.23 us  [shards(): call(z_inverse_kernel, shape(NC * 64, 128), [pltpu.VMEM((2048, 128), F32)])]
    all_to_all x2, blocking collectives: 41.6 us -> 42.7 us  [shards(): lax.all_to_all(along.reshape(32, 16, 128), 'wide', split_axis=0, concat_a...]
    pallas_call x1, Pallas kernels: 2.26 us -> 1.18 us  [shards(): call(z_forward_kernel, shape(2048, 128))(moments, jnp.asarray(Z_FORWARD))]
    ppermute x6, waiting for transfers between devices: 5.97 us -> 7 us  [swap(): return lax.ppermute(array, 'narrow', [(n, n ^ partner) for n in range(8)])]
    pallas_call x1, Pallas kernels: 2.69 us -> 1.67 us  [shards(): call(prepare_kernel, (shape(2, 2, 128, 640), shape(384, 640, dtype=BF)))]
  transfers between devices with their start and end apart: 14 -> 14, of which waited for: 10 -> 11; matrix products, arithmetic and copies ran while one was open for 0% -> 0% of each run, Pallas kernels for 3% -> 2%
where the time goes in v4:
time: 89.3 us; the launch traced here: 89 us
  blocking collectives  42.7 us (48%)
  starting transfers between devices  17.5 us (20%)
  waiting for transfers between devices  14 us (16%)
  Pallas kernels  10.9 us (12%)
  other arithmetic  2.49 us (3%)
  local copies, waits for them, and re-layouts  1.28 us (1%)
    all_to_all x2, blocking collectives, shards(): lax.all_to_all(along.reshape(32, 16, 128), 'wide', split_axis=0, concat_a...  42.7 us
    ppermute x6, starting transfers between devices, swap(): return lax.ppermute(array, 'narrow', [(n, n ^ partner) for n in range(8)])  7.94 us
    ppermute x7, starting transfers between devices, shift(): lax.ppermute(array, 'narrow', [(n, stepped(n, step, 1)) for n in range(8)])  7.31 us
    ppermute x7, waiting for transfers between devices, shift(): lax.ppermute(array, 'narrow', [(n, stepped(n, step, 1)) for n in range(8)])  7.02 us
    ppermute x6, waiting for transfers between devices, swap(): return lax.ppermute(array, 'narrow', [(n, n ^ partner) for n in range(8)])  7 us
    pallas_call x1, Pallas kernels, shards(): call(tail_kernel, shape(NC * 64, 128), [pltpu.VMEM((256, 128), F32)])  2.69 us
    ppermute x1, starting transfers between devices, shards(): mirror = lax.ppermute(packed, 'narrow', [(n, 7 - n) for n in range(8)])  2.24 us
    pallas_call x1, Pallas kernels, shards(): call(head_kernel, shape(NC * 64, 128))(leaves, jnp.concatenate(aux, axis=0))  1.85 us
  transfers between devices with their start and end apart: 14, of which 11 were waited for; matrix products, arithmetic and copies ran while one was open for 0% of the time, Pallas kernels for 2%

profile of v4, /device:TPU:2, one launch (start us, length us, event | category | flops | bytes accessed | tf_op | source)
XLA Modules:
  0.0 89.0 jit_solution(3370245456178291093)
XLA Ops:
  0.0 0.8 convert_element_type.19
  0.8 0.8 convert_element_type.23
  1.6 0.9 %select_maximum_fusion.aux_ref = f32[328,128]{1,0:T(8,128)S(1)} fusion(f32[200,25]{1,0:T(8,128)} %bitcast.42, f32[64,128]{1,0:T(8,128)S(1)} %convert_element_type.23, f32[64,128]{1,0:T(8,128)S(1)} %bitcast.41), kind=kLoop, calls=%fused_computation | loop fusion | flops 167936 | bytes 253472 | tf_op jit(solution)/shard_map/concatenate | solution.py:422
  2.5 1.1 %copy-done = f32[1,25,2,4096]{3,2,1,0:T(2,128)S(1)} copy-done((f32[1,25,2,4096]{3,2,1,0:T(2,128)S(1)}, f32[1,25,2,4096]{3,2,1,0:T(2,128)}, u32[]{:S(2)}) %copy-start) | copy-done | bytes 819224
  3.6 1.8 %shard_map.136.ms = f32[1600,128]{1,0:T(8,128)S(1)} custom-call(f32[1600,128]{1,0:T(8,128)S(1)} %bitcast.35, f32[328,128]{1,0:T(8,128)S(1)} %select_maximum_fusion.aux_ref), custom_call_target="tpu_custom_call" | custom-call | tf_op jit(solution)/shard_map/pallas_call | solution.py:422
  5.5 1.2 %shard_map.137 = f32[2048,128]{1,0:T(8,128)S(1)} custom-call(f32[1600,128]{1,0:T(8,128)S(1)} %shard_map.136.ms, bf16[8,80,192]{2,1,0:T(8,128)(2,1)S(1)} %copy-done.7), custom_call_target="tpu_custom_call" | custom-call | tf_op jit(solution)/shard_map/pallas_call | solution.py:425
  6.8 1.7 %collective-permute-start = (f32[512,128]{1,0:T(8,128)S(1)}, f32[512,128]{1,0:T(8,128)S(1)}, u32[]{:S(2)}, u32[]{:S(2)}) collective-permute-start(f32[512,128]{1,0:T(8,128)S(1)} %get-tuple-element.21), channel_id=1, source_target_pairs={{0,2},{1,3},{2,0},{3,1},{4,6},{5,7},{6,4},{7,5},{8,10},{9,11},{10,... | collective-permute-start | bytes 786440 | tf_op jit(solution)/shard_map/ppermute | solution.py:404
  8.5 0.8 collective-permute-start.2
  9.3 1.3 %collective-permute-start.1 = (f32[256,128]{1,0:T(8,128)S(1)}, f32[256,128]{1,0:T(8,128)S(1)}, u32[]{:S(2)}, u32[]{:S(2)}) collective-permute-start(f32[256,128]{1,0:T(8,128)S(1)} %get-tuple-element.18), channel_id=1, source_target_pairs={{0,1},{1,0},{2,3},{3,2},{4,5},{5,4},{6,7},{7,6},{8,9},{9,8},{10,11... | collective-permute-start | bytes 393224 | tf_op jit(solution)/shard_map/ppermute | solution.py:404
  10.7 2.2 %collective-permute-start.3 = (f32[64,128]{1,0:T(8,128)S(1)}, f32[64,128]{1,0:T(8,128)S(1)}, u32[]{:S(2)}, u32[]{:S(2)}) collective-permute-start(f32[64,128]{1,0:T(8,128)S(1)} %shard_map.139), channel_id=1, source_target_pairs={{0,7},{1,6},{2,5},{3,4},{4,3},{5,2},{6,1},{7,0},{8,15},{9,14},{10,... | collective-permute-start | bytes 98312 | tf_op jit(solution)/shard_map/ppermute | solution.py:420
  12.9 2.1 %collective-permute-done.2.mid_other = f32[256,128]{1,0:T(8,128)S(1)} collective-permute-done((f32[256,128]{1,0:T(8,128)S(1)}, f32[256,128]{1,0:T(8,128)S(1)}, u32[]{:S(2)}, u32[]{:S(2)}) %collective-permute-start.2) | collective-permute-done | bytes 131104 | tf_op jit(solution)/shard_map/ppermute | solution.py:404
  15.0 1.7 %collective-permute-done.1.far_other = f32[256,128]{1,0:T(8,128)S(1)} collective-permute-done((f32[256,128]{1,0:T(8,128)S(1)}, f32[256,128]{1,0:T(8,128)S(1)}, u32[]{:S(2)}, u32[]{:S(2)}) %collective-permute-start.1) | collective-permute-done | bytes 131104 | tf_op jit(solution)/shard_map/ppermute | solution.py:404
  16.7 3.0 %collective-permute-start.4 = (f32[256,128]{1,0:T(8,128)S(1)}, f32[256,128]{1,0:T(8,128)S(1)}, u32[]{:S(2)}, u32[]{:S(2)}) collective-permute-start(f32[256,128]{1,0:T(8,128)S(1)} %get-tuple-element.11._0), channel_id=1, source_target_pairs={{0,4},{1,5},{2,6},{3,7},{4,0},{5,1},{6,2},{7,3},{8,12},{9,13},{10,... | collective-permute-start | bytes 393224 | tf_op jit(solution)/shard_map/ppermute | solution.py:404
  20.0 1.0 %collective-permute-start.6 = (f32[256,128]{1,0:T(8,128)S(1)}, f32[256,128]{1,0:T(8,128)S(1)}, u32[]{:S(2)}, u32[]{:S(2)}) collective-permute-start(f32[256,128]{1,0:T(8,128)S(1)} %get-tuple-element.14), channel_id=1, source_target_pairs={{0,1},{1,0},{2,3},{3,2},{4,5},{5,4},{6,7},{7,6},{8,9},{9,8},{10,11... | collective-permute-start | bytes 393224 | tf_op jit(solution)/shard_map/ppermute | solution.py:404
  21.0 1.7 %shard_map.141 = (f32[2,2,128,640]{3,2,1,0:T(8,128)S(1)}, bf16[384,640]{1,0:T(8,128)(2,1)S(1)}) custom-call(f32[2,9,2,8,64]{4,3,2,1,0:T(8,128)S(1)} %bitcast.37, f32[64,128]{1,0:T(8,128)S(1)} %collective-permute-done.3._2.mirror_ref, f32[32,32]{1,0:T(8,128)S(1)} %pad.9.coupling_ref, bf16[400,640]{1,0:T(8,128)(2,1)S(1)} %copy-done.4), custom_call_target="tpu_custom_call" | custom-call | tf_op jit(solution)/shard_map/pallas_call | solution.py:436
  22.6 0.7 collective-permute-done.4.refs_1_
  23.4 2.5 %collective-permute-done.5.refs_2_ = f32[256,128]{1,0:T(8,128)S(1)} collective-permute-done((f32[256,128]{1,0:T(8,128)S(1)}, f32[256,128]{1,0:T(8,128)S(1)}, u32[]{:S(2)}, u32[]{:S(2)}) %collective-permute-start.5) | collective-permute-done | bytes 131104 | tf_op jit(solution)/shard_map/ppermute | solution.py:404
  26.3 24.9 %all_to_all.10 = f32[32,16,128]{2,1,0:T(8,128)S(1)} all-to-all(f32[32,16,128]{2,1,0:T(8,128)S(1)} %bitcast.34), channel_id=1, replica_groups=mesh['wide'=32,'narrow'=8] {'wide'}, dimensions={0} | all-to-all | bytes 524288 | tf_op jit(solution)/shard_map/all_to_all | solution.py:441
  51.2 1.4 %shard_map.143 = f32[32,2,8,128]{3,2,1,0:T(8,128)S(1)} custom-call(f32[32,2,8,128]{3,2,1,0:T(8,128)S(1)} %bitcast.31, bf16[256,768]{1,0:T(8,128)(2,1)S(1)} %copy-done.6, bf16[384,640]{1,0:T(8,128)(2,1)S(1)} %get-tuple-element.16.c_ref, f32[2,2,128,640]{3,2,1,0:T(8,128)S(1)} %get-tuple-element.15.refs_5_.k_ref, bf16[256,768]{1,0:T(8,128)(2,1)S(1)} %copy-done.5), custom_call_target="tpu_custom_call" | custom-call | tf_op jit(solution)/shard_map/pallas_call | solution.py:442
  52.6 17.8 %all_to_all.11 = f32[32,16,128]{2,1,0:T(8,128)S(1)} all-to-all(f32[32,16,128]{2,1,0:T(8,128)S(1)} %bitcast.32), channel_id=1, replica_groups=mesh['wide'=32,'narrow'=8] {'wide'}, dimensions={0} | all-to-all | bytes 524288 | tf_op jit(solution)/shard_map/all_to_all | solution.py:445
  70.7 1.5 %collective-permute-start.10 = (f32[256,128]{1,0:T(8,128)S(1)}, f32[256,128]{1,0:T(8,128)S(1)}, u32[]{:S(2)}, u32[]{:S(2)}) collective-permute-start(f32[256,128]{1,0:T(8,128)S(1)} %shard_map.144.refs_0_), channel_id=1, source_target_pairs={{0,1},{1,0},{2,3},{3,2},{4,5},{5,4},{6,7},{7,6},{8,9},{9,8},{10,11... | collective-permute-start | bytes 393224 | tf_op jit(solution)/shard_map/ppermute | solution.py:408
  72.3 1.1 %collective-permute-start.7 = (f32[256,128]{1,0:T(8,128)S(1)}, f32[256,128]{1,0:T(8,128)S(1)}, u32[]{:S(2)}, u32[]{:S(2)}) collective-permute-start(f32[256,128]{1,0:T(8,128)S(1)} %shard_map.144.refs_0_), channel_id=1, source_target_pairs={{0,4},{1,5},{2,6},{3,7},{4,0},{5,1},{6,2},{7,3},{8,12},{9,13},{10,... | collective-permute-start | bytes 393224 | tf_op jit(solution)/shard_map/ppermute | solution.py:408
  73.4 1.1 %collective-permute-start.9 = (f32[256,128]{1,0:T(8,128)S(1)}, f32[256,128]{1,0:T(8,128)S(1)}, u32[]{:S(2)}, u32[]{:S(2)}) collective-permute-start(f32[256,128]{1,0:T(8,128)S(1)} %shard_map.144.refs_0_), channel_id=1, source_target_pairs={{0,6},{1,7},{2,0},{3,1},{4,2},{5,3},{6,4},{7,5},{8,14},{9,15},{10,... | collective-permute-start | bytes 393224 | tf_op jit(solution)/shard_map/ppermute | solution.py:408
  74.4 1.0 %collective-permute-start.8 = (f32[256,128]{1,0:T(8,128)S(1)}, f32[256,128]{1,0:T(8,128)S(1)}, u32[]{:S(2)}, u32[]{:S(2)}) collective-permute-start(f32[256,128]{1,0:T(8,128)S(1)} %shard_map.144.refs_0_), channel_id=1, source_target_pairs={{0,2},{1,3},{2,4},{3,5},{4,6},{5,7},{6,0},{7,1},{8,10},{9,11},{10,... | collective-permute-start | bytes 393224 | tf_op jit(solution)/shard_map/ppermute | solution.py:408
  75.8 2.1 %collective-permute-start.13 = (f32[256,128]{1,0:T(8,128)S(1)}, f32[256,128]{1,0:T(8,128)S(1)}, u32[]{:S(2)}, u32[]{:S(2)}) collective-permute-start(f32[256,128]{1,0:T(8,128)S(1)} %collective-permute-done.10.refs_4_), channel_id=1, source_target_pairs={{0,6},{1,7},{2,0},{3,1},{4,2},{5,3},{6,4},{7,5},{8,14},{9,15},{10,... | collective-permute-start | bytes 393224 | tf_op jit(solution)/shard_map/ppermute | solution.py:408
  78.0 2.2 %collective-permute-done.7.refs_1_ = f32[256,128]{1,0:T(8,128)S(1)} collective-permute-done((f32[256,128]{1,0:T(8,128)S(1)}, f32[256,128]{1,0:T(8,128)S(1)}, u32[]{:S(2)}, u32[]{:S(2)}) %collective-permute-start.7) | collective-permute-done | bytes 131104 | tf_op jit(solution)/shard_map/ppermute | solution.py:408
  80.6 1.0 %collective-permute-done.9.refs_3_ = f32[256,128]{1,0:T(8,128)S(1)} collective-permute-done((f32[256,128]{1,0:T(8,128)S(1)}, f32[256,128]{1,0:T(8,128)S(1)}, u32[]{:S(2)}, u32[]{:S(2)}) %collective-permute-start.9) | collective-permute-done | bytes 131104 | tf_op jit(solution)/shard_map/ppermute | solution.py:408
  81.6 0.8 collective-permute-done.8.refs_2_
  83.0 1.1 %collective-permute-done.12.refs_6_ = f32[256,128]{1,0:T(8,128)S(1)} collective-permute-done((f32[256,128]{1,0:T(8,128)S(1)}, f32[256,128]{1,0:T(8,128)S(1)}, u32[]{:S(2)}, u32[]{:S(2)}) %collective-permute-start.12) | collective-permute-done | bytes 131104 | tf_op jit(solution)/shard_map/ppermute | solution.py:408
  84.1 1.0 %collective-permute-done.11.refs_5_ = f32[256,128]{1,0:T(8,128)S(1)} collective-permute-done((f32[256,128]{1,0:T(8,128)S(1)}, f32[256,128]{1,0:T(8,128)S(1)}, u32[]{:S(2)}, u32[]{:S(2)}) %collective-permute-start.11) | collective-permute-done | bytes 131104 | tf_op jit(solution)/shard_map/ppermute | solution.py:408
  85.1 1.2 %shard_map.145.local_ref = f32[1600,128]{1,0:T(8,128)S(1)} custom-call(f32[256,128]{1,0:T(8,128)S(1)} %shard_map.144.refs_0_, f32[256,128]{1,0:T(8,128)S(1)} %collective-permute-done.7.refs_1_, f32[256,128]{1,0:T(8,128)S(1)} %collective-permute-done.8.refs_2_, f32[256,128]{1,0:T(8,128)S(1)} %collective-permute-done.9.refs_3_, ...), custom_call_target="tpu_custom_call" | custom-call | tf_op jit(solution)/shard_map/pallas_call | solution.py:453
  86.3 2.7 %shard_map.146 = f32[1600,128]{1,0:T(8,128)} custom-call(f32[1600,128]{1,0:T(8,128)S(1)} %shard_map.145.local_ref, s32[64,128]{1,0:T(8,128)S(1)} %bitcast.39, f32[200,25]{1,0:T(8,128)S(1)} %bitcast.40), custom_call_target="tpu_custom_call" | custom-call | tf_op jit(solution)/shard_map/pallas_call | solution.py:454
  (39 shorter events, 2.8 us)
Async XLA Ops:
  0.0 5.5 %copy-start.7 = (bf16[8,80,192]{2,1,0:T(8,128)(2,1)S(1)}, bf16[8,80,192]{2,1,0:T(8,128)(2,1)}, u32[]{:S(2)}) copy-start(bf16[8,80,192]{2,1,0:T(8,128)(2,1)} %constant.17.clone.table_ref) | copy-start | bytes 737284
  2.5 1.1 %copy-start = (f32[1,25,2,4096]{3,2,1,0:T(2,128)S(1)}, f32[1,25,2,4096]{3,2,1,0:T(2,128)}, u32[]{:S(2)}) copy-start(f32[1,25,2,4096]{3,2,1,0:T(2,128)} %param.14) | copy-start | bytes 2457604
  6.7 3.9 %copy-start.3 = (f32[2,9,64,2,8]{2,4,3,1,0:T(8,128)S(1)}, f32[2,9,64,2,8]{2,4,3,1,0:T(8,128)}, u32[]{:S(2)}) copy-start(f32[2,9,64,2,8]{2,4,3,1,0:T(8,128)} %param.19) | copy-start | bytes 221188
  6.8 14.2 %copy-start.11 = (f32[25,25]{1,0:T(8,128)S(1)}, f32[25,25]{1,0:T(8,128)}, u32[]{:S(2)}) copy-start(f32[25,25]{1,0:T(8,128)} %param.18) | copy-start | bytes 7504
  6.8 14.2 %copy-start.4 = (bf16[400,640]{1,0:T(8,128)(2,1)S(1)}, bf16[400,640]{1,0:T(8,128)(2,1)}, u32[]{:S(2)}) copy-start(bf16[400,640]{1,0:T(8,128)(2,1)} %constant.18.clone.table_ref) | copy-start | bytes 1536004
  6.8 13.2 %collective-permute-start = (f32[512,128]{1,0:T(8,128)S(1)}, f32[512,128]{1,0:T(8,128)S(1)}, u32[]{:S(2)}, u32[]{:S(2)}) collective-permute-start(f32[512,128]{1,0:T(8,128)S(1)} %get-tuple-element.21), channel_id=1, source_target_pairs={{0,2},{1,3},{2,0},{3,1},{4,6},{5,7},{6,4},{7,5},{8,10},{9,11},{10,... | collective-permute-start | bytes 786440 | tf_op jit(solution)/shard_map/ppermute | solution.py:404
  8.5 17.4 %copy-start.2 = (bf16[512,768]{1,0:T(8,128)(2,1)S(1)}, bf16[512,768]{1,0:T(8,128)(2,1)}, u32[]{:S(2)}) copy-start(bf16[512,768]{1,0:T(8,128)(2,1)} %constant.19.clone.refs_4_) | copy-start | bytes 2359300
  8.5 6.5 %collective-permute-start.2 = (f32[256,128]{1,0:T(8,128)S(1)}, f32[256,128]{1,0:T(8,128)S(1)}, u32[]{:S(2)}, u32[]{:S(2)}) collective-permute-start(f32[256,128]{1,0:T(8,128)S(1)} %get-tuple-element.17), channel_id=1, source_target_pairs={{0,1},{1,0},{2,3},{3,2},{4,5},{5,4},{6,7},{7,6},{8,9},{9,8},{10,11... | collective-permute-start | bytes 393224 | tf_op jit(solution)/shard_map/ppermute | solution.py:404
  9.3 7.4 %collective-permute-start.1 = (f32[256,128]{1,0:T(8,128)S(1)}, f32[256,128]{1,0:T(8,128)S(1)}, u32[]{:S(2)}, u32[]{:S(2)}) collective-permute-start(f32[256,128]{1,0:T(8,128)S(1)} %get-tuple-element.18), channel_id=1, source_target_pairs={{0,1},{1,0},{2,3},{3,2},{4,5},{5,4},{6,7},{7,6},{8,9},{9,8},{10,11... | collective-permute-start | bytes 393224 | tf_op jit(solution)/shard_map/ppermute | solution.py:404
  10.7 9.2 %collective-permute-start.3 = (f32[64,128]{1,0:T(8,128)S(1)}, f32[64,128]{1,0:T(8,128)S(1)}, u32[]{:S(2)}, u32[]{:S(2)}) collective-permute-start(f32[64,128]{1,0:T(8,128)S(1)} %shard_map.139), channel_id=1, source_target_pairs={{0,7},{1,6},{2,5},{3,4},{4,3},{5,2},{6,1},{7,0},{8,15},{9,14},{10,... | collective-permute-start | bytes 98312 | tf_op jit(solution)/shard_map/ppermute | solution.py:420
  16.7 6.7 %collective-permute-start.4 = (f32[256,128]{1,0:T(8,128)S(1)}, f32[256,128]{1,0:T(8,128)S(1)}, u32[]{:S(2)}, u32[]{:S(2)}) collective-permute-start(f32[256,128]{1,0:T(8,128)S(1)} %get-tuple-element.11._0), channel_id=1, source_target_pairs={{0,4},{1,5},{2,6},{3,7},{4,0},{5,1},{6,2},{7,3},{8,12},{9,13},{10,... | collective-permute-start | bytes 393224 | tf_op jit(solution)/shard_map/ppermute | solution.py:404
  19.7 6.2 %collective-permute-start.5 = (f32[256,128]{1,0:T(8,128)S(1)}, f32[256,128]{1,0:T(8,128)S(1)}, u32[]{:S(2)}, u32[]{:S(2)}) collective-permute-start(f32[256,128]{1,0:T(8,128)S(1)} %get-tuple-element.12._1), channel_id=1, source_target_pairs={{0,6},{1,7},{2,4},{3,5},{4,2},{5,3},{6,0},{7,1},{8,14},{9,15},{10,... | collective-permute-start | bytes 393224 | tf_op jit(solution)/shard_map/ppermute | solution.py:404
  20.0 5.9 %collective-permute-start.6 = (f32[256,128]{1,0:T(8,128)S(1)}, f32[256,128]{1,0:T(8,128)S(1)}, u32[]{:S(2)}, u32[]{:S(2)}) collective-permute-start(f32[256,128]{1,0:T(8,128)S(1)} %get-tuple-element.14), channel_id=1, source_target_pairs={{0,1},{1,0},{2,3},{3,2},{4,5},{5,4},{6,7},{7,6},{8,9},{9,8},{10,11... | collective-permute-start | bytes 393224 | tf_op jit(solution)/shard_map/ppermute | solution.py:404
  25.9 25.3 %copy-start.5 = (bf16[256,768]{1,0:T(8,128)(2,1)S(1)}, bf16[256,768]{1,0:T(8,128)(2,1)}, u32[]{:S(2)}) copy-start(bf16[256,768]{1,0:T(8,128)(2,1)} %constant.21.clone.inverse_ref) | copy-start | bytes 1179652
  25.9 25.3 %copy-start.6 = (bf16[256,768]{1,0:T(8,128)(2,1)S(1)}, bf16[256,768]{1,0:T(8,128)(2,1)}, u32[]{:S(2)}) copy-start(bf16[256,768]{1,0:T(8,128)(2,1)} %constant.20.clone.forward_ref) | copy-start | bytes 1179652
  51.2 19.2 %copy-start.1 = (bf16[1536,256]{1,0:T(8,128)(2,1)S(1)}, bf16[1536,256]{1,0:T(8,128)(2,1)}, u32[]{:S(2)}) copy-start(bf16[1536,256]{1,0:T(8,128)(2,1)} %constant.22.clone.table_ref) | copy-start | bytes 2359300
  52.6 32.5 %copy-start.8 = (bf16[8,64,240]{2,1,0:T(8,128)(2,1)S(1)}, bf16[8,64,240]{2,1,0:T(8,128)(2,1)}, u32[]{:S(2)}) copy-start(bf16[8,64,240]{2,1,0:T(8,128)(2,1)} %constant.23.clone.refs_8_) | copy-start | bytes 737284
  70.7 15.6 %copy-start.9 = (s32[1,2,4096]{2,1,0:T(2,128)S(1)}, s32[1,2,4096]{2,1,0:T(2,128)}, u32[]{:S(2)}) copy-start(s32[1,2,4096]{2,1,0:T(2,128)} %param.16) | copy-start | bytes 98308
  70.7 15.6 %copy-start.10 = (f32[8,25,25]{2,0,1:T(8,128)S(1)}, f32[8,25,25]{2,0,1:T(8,128)}, u32[]{:S(2)}) copy-start(f32[8,25,25]{2,0,1:T(8,128)} %param.20) | copy-start | bytes 60004
  70.7 5.1 %collective-permute-start.10 = (f32[256,128]{1,0:T(8,128)S(1)}, f32[256,128]{1,0:T(8,128)S(1)}, u32[]{:S(2)}, u32[]{:S(2)}) collective-permute-start(f32[256,128]{1,0:T(8,128)S(1)} %shard_map.144.refs_0_), channel_id=1, source_target_pairs={{0,1},{1,0},{2,3},{3,2},{4,5},{5,4},{6,7},{7,6},{8,9},{9,8},{10,11... | collective-permute-start | bytes 393224 | tf_op jit(solution)/shard_map/ppermute | solution.py:408
  72.3 7.8 %collective-permute-start.7 = (f32[256,128]{1,0:T(8,128)S(1)}, f32[256,128]{1,0:T(8,128)S(1)}, u32[]{:S(2)}, u32[]{:S(2)}) collective-permute-start(f32[256,128]{1,0:T(8,128)S(1)} %shard_map.144.refs_0_), channel_id=1, source_target_pairs={{0,4},{1,5},{2,6},{3,7},{4,0},{5,1},{6,2},{7,3},{8,12},{9,13},{10,... | collective-permute-start | bytes 393224 | tf_op jit(solution)/shard_map/ppermute | solution.py:408
  73.4 8.3 %collective-permute-start.9 = (f32[256,128]{1,0:T(8,128)S(1)}, f32[256,128]{1,0:T(8,128)S(1)}, u32[]{:S(2)}, u32[]{:S(2)}) collective-permute-start(f32[256,128]{1,0:T(8,128)S(1)} %shard_map.144.refs_0_), channel_id=1, source_target_pairs={{0,6},{1,7},{2,0},{3,1},{4,2},{5,3},{6,4},{7,5},{8,14},{9,15},{10,... | collective-permute-start | bytes 393224 | tf_op jit(solution)/shard_map/ppermute | solution.py:408
  74.4 8.0 %collective-permute-start.8 = (f32[256,128]{1,0:T(8,128)S(1)}, f32[256,128]{1,0:T(8,128)S(1)}, u32[]{:S(2)}, u32[]{:S(2)}) collective-permute-start(f32[256,128]{1,0:T(8,128)S(1)} %shard_map.144.refs_0_), channel_id=1, source_target_pairs={{0,2},{1,3},{2,4},{3,5},{4,6},{5,7},{6,0},{7,1},{8,10},{9,11},{10,... | collective-permute-start | bytes 393224 | tf_op jit(solution)/shard_map/ppermute | solution.py:408
  75.8 7.2 %collective-permute-start.13 = (f32[256,128]{1,0:T(8,128)S(1)}, f32[256,128]{1,0:T(8,128)S(1)}, u32[]{:S(2)}, u32[]{:S(2)}) collective-permute-start(f32[256,128]{1,0:T(8,128)S(1)} %collective-permute-done.10.refs_4_), channel_id=1, source_target_pairs={{0,6},{1,7},{2,0},{3,1},{4,2},{5,3},{6,4},{7,5},{8,14},{9,15},{10,... | collective-permute-start | bytes 393224 | tf_op jit(solution)/shard_map/ppermute | solution.py:408
  77.9 6.2 %collective-permute-start.12 = (f32[256,128]{1,0:T(8,128)S(1)}, f32[256,128]{1,0:T(8,128)S(1)}, u32[]{:S(2)}, u32[]{:S(2)}) collective-permute-start(f32[256,128]{1,0:T(8,128)S(1)} %collective-permute-done.10.refs_4_), channel_id=1, source_target_pairs={{0,2},{1,3},{2,4},{3,5},{4,6},{5,7},{6,0},{7,1},{8,10},{9,11},{10,... | collective-permute-start | bytes 393224 | tf_op jit(solution)/shard_map/ppermute | solution.py:408
  80.1 5.0 %collective-permute-start.11 = (f32[256,128]{1,0:T(8,128)S(1)}, f32[256,128]{1,0:T(8,128)S(1)}, u32[]{:S(2)}, u32[]{:S(2)}) collective-permute-start(f32[256,128]{1,0:T(8,128)S(1)} %collective-permute-done.7.refs_1_), channel_id=1, source_target_pairs={{0,1},{1,0},{2,3},{3,2},{4,5},{5,4},{6,7},{7,6},{8,9},{9,8},{10,11... | collective-permute-start | bytes 393224 | tf_op jit(solution)/shard_map/ppermute | solution.py:408

commit v5 on v4

--- a/solution.py
+++ b/solution.py
@@ -194,19 +194,19 @@
     return total, last
 
 
-GROUP = 32
+GROUP = 64
 BATCH = 25
 
 
 def head_kernel(leaf_ref, aux_ref, out_ref):
-    w_cat = operator_rows(aux_ref, 128)
-    degree = degree_column().astype(F32)
+    w_cat = operator_rows(aux_ref, 64)
+    degree = degree_column()
 
     def group(g, carry):
         b = g * GROUP
-        kept = jnp.where(degree <= lane_rows(aux_ref, b, GROUP), load_blocks(leaf_ref, b), 0.0)
-        octant = lane_rows(aux_ref, 64 + b, GROUP).astype(jnp.int32)
-        store_blocks(out_ref, b, *translate(w_cat, kept, octant))
+        code = lane_rows(aux_ref, b, GROUP).astype(jnp.int32)
+        kept = jnp.where(degree <= (code & 7), load_blocks(leaf_ref, b), 0.0)
+        store_blocks(out_ref, b, *translate(w_cat, kept, code >> 3))
         return carry
 
     lax.fori_loop(0, 64 // GROUP, group, 0)
@@ -418,7 +418,7 @@
 
     packed = call(pack_kernel, shape(64, 128), [pltpu.VMEM((72, 128), F32)])(kernel)
     mirror = lax.ppermute(packed, "narrow", [(n, 7 - n) for n in range(8)])
-    aux = [orders.astype(F32), octants.astype(F32), jnp.pad(m2m, ((0, 0), (0, 128 - NC)))]
+    aux = [(8 * octants + orders).astype(F32), jnp.pad(m2m, ((0, 0), (0, 128 - NC)))]
     moments = call(head_kernel, shape(NC * 64, 128))(leaves, jnp.concatenate(aux, axis=0))
     whole = pl.BlockSpec(memory_space=pltpu.VMEM)
     anywhere = pl.BlockSpec(memory_space=pl.ANY)

time: 89.3 us -> 88.4 us (0.990)
  no operation moved by 1% of the time
where the time goes in v5:
time: 88.4 us; the launch traced here: 88.2 us
  blocking collectives  42.7 us (48%)
  starting transfers between devices  17.5 us (20%)
  waiting for transfers between devices  14.1 us (16%)
  Pallas kernels  10.7 us (12%)
  other arithmetic  1.73 us (2%)
  local copies, waits for them, and re-layouts  1.28 us (1%)
    all_to_all x2, blocking collectives, shards(): lax.all_to_all(along.reshape(32, 16, 128), 'wide', split_axis=0, concat_a...  42.7 us
    ppermute x6, starting transfers between devices, swap(): return lax.ppermute(array, 'narrow', [(n, n ^ partner) for n in range(8)])  7.94 us
    ppermute x7, starting transfers between devices, shift(): lax.ppermute(array, 'narrow', [(n, stepped(n, step, 1)) for n in range(8)])  7.29 us
    ppermute x7, waiting for transfers between devices, shift(): lax.ppermute(array, 'narrow', [(n, stepped(n, step, 1)) for n in range(8)])  7.06 us
    ppermute x6, waiting for transfers between devices, swap(): return lax.ppermute(array, 'narrow', [(n, n ^ partner) for n in range(8)])  7 us
    pallas_call x1, Pallas kernels, shards(): call(tail_kernel, shape(NC * 64, 128), [pltpu.VMEM((256, 128), F32)])  2.63 us
    ppermute x1, starting transfers between devices, shards(): mirror = lax.ppermute(packed, 'narrow', [(n, 7 - n) for n in range(8)])  2.24 us
    pallas_call x1, Pallas kernels, shards(): call(head_kernel, shape(NC * 64, 128))(leaves, jnp.concatenate(aux, axis=0))  1.78 us
  transfers between devices with their start and end apart: 14, of which 11 were waited for; matrix products, arithmetic and copies ran while one was open for 0% of the time, Pallas kernels for 2%

profile of v5, /device:TPU:2, one launch (start us, length us, event | category | flops | bytes accessed | tf_op | source)
XLA Modules:
  0.0 88.2 jit_solution(12650046601007386049)
XLA Ops:
  0.0 0.8 add_convert_fusion
  0.8 0.9 %select_maximum_fusion.aux_ref = f32[264,128]{1,0:T(8,128)S(1)} fusion(f32[200,25]{1,0:T(8,128)} %bitcast.41, f32[64,128]{1,0:T(8,128)S(1)} %add_convert_fusion), kind=kLoop, calls=%fused_computation | loop fusion | flops 101376 | bytes 187936 | tf_op jit(solution)/shard_map/concatenate | solution.py:422
  1.8 1.1 %copy-done = f32[1,25,2,4096]{3,2,1,0:T(2,128)S(1)} copy-done((f32[1,25,2,4096]{3,2,1,0:T(2,128)S(1)}, f32[1,25,2,4096]{3,2,1,0:T(2,128)}, u32[]{:S(2)}) %copy-start) | copy-done | bytes 819224
  2.9 1.8 %shard_map.136.ms = f32[1600,128]{1,0:T(8,128)S(1)} custom-call(f32[1600,128]{1,0:T(8,128)S(1)} %bitcast.35, f32[264,128]{1,0:T(8,128)S(1)} %select_maximum_fusion.aux_ref), custom_call_target="tpu_custom_call" | custom-call | tf_op jit(solution)/shard_map/pallas_call | solution.py:422
  4.7 1.2 %shard_map.137 = f32[2048,128]{1,0:T(8,128)S(1)} custom-call(f32[1600,128]{1,0:T(8,128)S(1)} %shard_map.136.ms, bf16[8,80,192]{2,1,0:T(8,128)(2,1)S(1)} %copy-done.7), custom_call_target="tpu_custom_call" | custom-call | tf_op jit(solution)/shard_map/pallas_call | solution.py:425
  6.0 1.7 %collective-permute-start = (f32[512,128]{1,0:T(8,128)S(1)}, f32[512,128]{1,0:T(8,128)S(1)}, u32[]{:S(2)}, u32[]{:S(2)}) collective-permute-start(f32[512,128]{1,0:T(8,128)S(1)} %get-tuple-element.21), channel_id=1, source_target_pairs={{0,2},{1,3},{2,0},{3,1},{4,6},{5,7},{6,4},{7,5},{8,10},{9,11},{10,... | collective-permute-start | bytes 786440 | tf_op jit(solution)/shard_map/ppermute | solution.py:404
  7.7 0.8 collective-permute-start.2
  8.5 1.3 %collective-permute-start.1 = (f32[256,128]{1,0:T(8,128)S(1)}, f32[256,128]{1,0:T(8,128)S(1)}, u32[]{:S(2)}, u32[]{:S(2)}) collective-permute-start(f32[256,128]{1,0:T(8,128)S(1)} %get-tuple-element.18), channel_id=1, source_target_pairs={{0,1},{1,0},{2,3},{3,2},{4,5},{5,4},{6,7},{7,6},{8,9},{9,8},{10,11... | collective-permute-start | bytes 393224 | tf_op jit(solution)/shard_map/ppermute | solution.py:404
  9.9 2.2 %collective-permute-start.3 = (f32[64,128]{1,0:T(8,128)S(1)}, f32[64,128]{1,0:T(8,128)S(1)}, u32[]{:S(2)}, u32[]{:S(2)}) collective-permute-start(f32[64,128]{1,0:T(8,128)S(1)} %shard_map.139), channel_id=1, source_target_pairs={{0,7},{1,6},{2,5},{3,4},{4,3},{5,2},{6,1},{7,0},{8,15},{9,14},{10,... | collective-permute-start | bytes 98312 | tf_op jit(solution)/shard_map/ppermute | solution.py:420
  12.1 2.1 %collective-permute-done.2.mid_other = f32[256,128]{1,0:T(8,128)S(1)} collective-permute-done((f32[256,128]{1,0:T(8,128)S(1)}, f32[256,128]{1,0:T(8,128)S(1)}, u32[]{:S(2)}, u32[]{:S(2)}) %collective-permute-start.2) | collective-permute-done | bytes 131104 | tf_op jit(solution)/shard_map/ppermute | solution.py:404
  14.2 1.7 %collective-permute-done.1.far_other = f32[256,128]{1,0:T(8,128)S(1)} collective-permute-done((f32[256,128]{1,0:T(8,128)S(1)}, f32[256,128]{1,0:T(8,128)S(1)}, u32[]{:S(2)}, u32[]{:S(2)}) %collective-permute-start.1) | collective-permute-done | bytes 131104 | tf_op jit(solution)/shard_map/ppermute | solution.py:404
  15.9 3.0 %collective-permute-start.4 = (f32[256,128]{1,0:T(8,128)S(1)}, f32[256,128]{1,0:T(8,128)S(1)}, u32[]{:S(2)}, u32[]{:S(2)}) collective-permute-start(f32[256,128]{1,0:T(8,128)S(1)} %get-tuple-element.11._0), channel_id=1, source_target_pairs={{0,4},{1,5},{2,6},{3,7},{4,0},{5,1},{6,2},{7,3},{8,12},{9,13},{10,... | collective-permute-start | bytes 393224 | tf_op jit(solution)/shard_map/ppermute | solution.py:404
  19.2 1.0 %collective-permute-start.6 = (f32[256,128]{1,0:T(8,128)S(1)}, f32[256,128]{1,0:T(8,128)S(1)}, u32[]{:S(2)}, u32[]{:S(2)}) collective-permute-start(f32[256,128]{1,0:T(8,128)S(1)} %get-tuple-element.14), channel_id=1, source_target_pairs={{0,1},{1,0},{2,3},{3,2},{4,5},{5,4},{6,7},{7,6},{8,9},{9,8},{10,11... | collective-permute-start | bytes 393224 | tf_op jit(solution)/shard_map/ppermute | solution.py:404
  20.1 1.7 %shard_map.141 = (f32[2,2,128,640]{3,2,1,0:T(8,128)S(1)}, bf16[384,640]{1,0:T(8,128)(2,1)S(1)}) custom-call(f32[2,9,2,8,64]{4,3,2,1,0:T(8,128)S(1)} %bitcast.37, f32[64,128]{1,0:T(8,128)S(1)} %collective-permute-done.3._2.mirror_ref, f32[32,32]{1,0:T(8,128)S(1)} %pad.9.coupling_ref, bf16[400,640]{1,0:T(8,128)(2,1)S(1)} %copy-done.4), custom_call_target="tpu_custom_call" | custom-call | tf_op jit(solution)/shard_map/pallas_call | solution.py:436
  21.8 0.8 collective-permute-done.4.refs_1_
  22.6 2.5 %collective-permute-done.5.refs_2_ = f32[256,128]{1,0:T(8,128)S(1)} collective-permute-done((f32[256,128]{1,0:T(8,128)S(1)}, f32[256,128]{1,0:T(8,128)S(1)}, u32[]{:S(2)}, u32[]{:S(2)}) %collective-permute-start.5) | collective-permute-done | bytes 131104 | tf_op jit(solution)/shard_map/ppermute | solution.py:404
  25.5 24.9 %all_to_all.10 = f32[32,16,128]{2,1,0:T(8,128)S(1)} all-to-all(f32[32,16,128]{2,1,0:T(8,128)S(1)} %bitcast.34), channel_id=1, replica_groups=mesh['wide'=32,'narrow'=8] {'wide'}, dimensions={0} | all-to-all | bytes 524288 | tf_op jit(solution)/shard_map/all_to_all | solution.py:441
  50.4 1.4 %shard_map.143 = f32[32,2,8,128]{3,2,1,0:T(8,128)S(1)} custom-call(f32[32,2,8,128]{3,2,1,0:T(8,128)S(1)} %bitcast.31, bf16[256,768]{1,0:T(8,128)(2,1)S(1)} %copy-done.6, bf16[384,640]{1,0:T(8,128)(2,1)S(1)} %get-tuple-element.16.c_ref, f32[2,2,128,640]{3,2,1,0:T(8,128)S(1)} %get-tuple-element.15.refs_5_.k_ref, bf16[256,768]{1,0:T(8,128)(2,1)S(1)} %copy-done.5), custom_call_target="tpu_custom_call" | custom-call | tf_op jit(solution)/shard_map/pallas_call | solution.py:442
  51.8 17.8 %all_to_all.11 = f32[32,16,128]{2,1,0:T(8,128)S(1)} all-to-all(f32[32,16,128]{2,1,0:T(8,128)S(1)} %bitcast.32), channel_id=1, replica_groups=mesh['wide'=32,'narrow'=8] {'wide'}, dimensions={0} | all-to-all | bytes 524288 | tf_op jit(solution)/shard_map/all_to_all | solution.py:445
  69.9 1.5 %collective-permute-start.10 = (f32[256,128]{1,0:T(8,128)S(1)}, f32[256,128]{1,0:T(8,128)S(1)}, u32[]{:S(2)}, u32[]{:S(2)}) collective-permute-start(f32[256,128]{1,0:T(8,128)S(1)} %shard_map.144.refs_0_), channel_id=1, source_target_pairs={{0,1},{1,0},{2,3},{3,2},{4,5},{5,4},{6,7},{7,6},{8,9},{9,8},{10,11... | collective-permute-start | bytes 393224 | tf_op jit(solution)/shard_map/ppermute | solution.py:408
  71.5 1.1 %collective-permute-start.7 = (f32[256,128]{1,0:T(8,128)S(1)}, f32[256,128]{1,0:T(8,128)S(1)}, u32[]{:S(2)}, u32[]{:S(2)}) collective-permute-start(f32[256,128]{1,0:T(8,128)S(1)} %shard_map.144.refs_0_), channel_id=1, source_target_pairs={{0,4},{1,5},{2,6},{3,7},{4,0},{5,1},{6,2},{7,3},{8,12},{9,13},{10,... | collective-permute-start | bytes 393224 | tf_op jit(solution)/shard_map/ppermute | solution.py:408
  72.6 1.1 %collective-permute-start.9 = (f32[256,128]{1,0:T(8,128)S(1)}, f32[256,128]{1,0:T(8,128)S(1)}, u32[]{:S(2)}, u32[]{:S(2)}) collective-permute-start(f32[256,128]{1,0:T(8,128)S(1)} %shard_map.144.refs_0_), channel_id=1, source_target_pairs={{0,6},{1,7},{2,0},{3,1},{4,2},{5,3},{6,4},{7,5},{8,14},{9,15},{10,... | collective-permute-start | bytes 393224 | tf_op jit(solution)/shard_map/ppermute | solution.py:408
  73.6 1.0 %collective-permute-start.8 = (f32[256,128]{1,0:T(8,128)S(1)}, f32[256,128]{1,0:T(8,128)S(1)}, u32[]{:S(2)}, u32[]{:S(2)}) collective-permute-start(f32[256,128]{1,0:T(8,128)S(1)} %shard_map.144.refs_0_), channel_id=1, source_target_pairs={{0,2},{1,3},{2,4},{3,5},{4,6},{5,7},{6,0},{7,1},{8,10},{9,11},{10,... | collective-permute-start | bytes 393224 | tf_op jit(solution)/shard_map/ppermute | solution.py:408
  75.0 2.1 %collective-permute-start.13 = (f32[256,128]{1,0:T(8,128)S(1)}, f32[256,128]{1,0:T(8,128)S(1)}, u32[]{:S(2)}, u32[]{:S(2)}) collective-permute-start(f32[256,128]{1,0:T(8,128)S(1)} %collective-permute-done.10.refs_4_), channel_id=1, source_target_pairs={{0,6},{1,7},{2,0},{3,1},{4,2},{5,3},{6,4},{7,5},{8,14},{9,15},{10,... | collective-permute-start | bytes 393224 | tf_op jit(solution)/shard_map/ppermute | solution.py:408
  77.1 2.2 %collective-permute-done.7.refs_1_ = f32[256,128]{1,0:T(8,128)S(1)} collective-permute-done((f32[256,128]{1,0:T(8,128)S(1)}, f32[256,128]{1,0:T(8,128)S(1)}, u32[]{:S(2)}, u32[]{:S(2)}) %collective-permute-start.7) | collective-permute-done | bytes 131104 | tf_op jit(solution)/shard_map/ppermute | solution.py:408
  79.8 1.0 %collective-permute-done.9.refs_3_ = f32[256,128]{1,0:T(8,128)S(1)} collective-permute-done((f32[256,128]{1,0:T(8,128)S(1)}, f32[256,128]{1,0:T(8,128)S(1)}, u32[]{:S(2)}, u32[]{:S(2)}) %collective-permute-start.9) | collective-permute-done | bytes 131104 | tf_op jit(solution)/shard_map/ppermute | solution.py:408
  80.8 0.8 collective-permute-done.8.refs_2_
  81.6 0.6 collective-permute-done.13.refs_7_
  82.2 1.1 %collective-permute-done.12.refs_6_ = f32[256,128]{1,0:T(8,128)S(1)} collective-permute-done((f32[256,128]{1,0:T(8,128)S(1)}, f32[256,128]{1,0:T(8,128)S(1)}, u32[]{:S(2)}, u32[]{:S(2)}) %collective-permute-start.12) | collective-permute-done | bytes 131104 | tf_op jit(solution)/shard_map/ppermute | solution.py:408
  83.3 1.0 %collective-permute-done.11.refs_5_ = f32[256,128]{1,0:T(8,128)S(1)} collective-permute-done((f32[256,128]{1,0:T(8,128)S(1)}, f32[256,128]{1,0:T(8,128)S(1)}, u32[]{:S(2)}, u32[]{:S(2)}) %collective-permute-start.11) | collective-permute-done | bytes 131104 | tf_op jit(solution)/shard_map/ppermute | solution.py:408
  84.3 1.2 %shard_map.145.local_ref = f32[1600,128]{1,0:T(8,128)S(1)} custom-call(f32[256,128]{1,0:T(8,128)S(1)} %shard_map.144.refs_0_, f32[256,128]{1,0:T(8,128)S(1)} %collective-permute-done.7.refs_1_, f32[256,128]{1,0:T(8,128)S(1)} %collective-permute-done.8.refs_2_, f32[256,128]{1,0:T(8,128)S(1)} %collective-permute-done.9.refs_3_, ...), custom_call_target="tpu_custom_call" | custom-call | tf_op jit(solution)/shard_map/pallas_call | solution.py:453
  85.5 2.6 %shard_map.146 = f32[1600,128]{1,0:T(8,128)} custom-call(f32[1600,128]{1,0:T(8,128)S(1)} %shard_map.145.local_ref, s32[64,128]{1,0:T(8,128)S(1)} %bitcast.39, f32[200,25]{1,0:T(8,128)S(1)} %bitcast.40), custom_call_target="tpu_custom_call" | custom-call | tf_op jit(solution)/shard_map/pallas_call | solution.py:454
  (38 shorter events, 2.1 us)
Async XLA Ops:
  0.0 4.7 %copy-start.7 = (bf16[8,80,192]{2,1,0:T(8,128)(2,1)S(1)}, bf16[8,80,192]{2,1,0:T(8,128)(2,1)}, u32[]{:S(2)}) copy-start(bf16[8,80,192]{2,1,0:T(8,128)(2,1)} %constant.19.clone.table_ref) | copy-start | bytes 737284
  1.7 1.1 %copy-start = (f32[1,25,2,4096]{3,2,1,0:T(2,128)S(1)}, f32[1,25,2,4096]{3,2,1,0:T(2,128)}, u32[]{:S(2)}) copy-start(f32[1,25,2,4096]{3,2,1,0:T(2,128)} %param.14) | copy-start | bytes 2457604
  5.9 3.9 %copy-start.3 = (f32[2,9,64,2,8]{2,4,3,1,0:T(8,128)S(1)}, f32[2,9,64,2,8]{2,4,3,1,0:T(8,128)}, u32[]{:S(2)}) copy-start(f32[2,9,64,2,8]{2,4,3,1,0:T(8,128)} %param.19) | copy-start | bytes 221188
  5.9 14.2 %copy-start.11 = (f32[25,25]{1,0:T(8,128)S(1)}, f32[25,25]{1,0:T(8,128)}, u32[]{:S(2)}) copy-start(f32[25,25]{1,0:T(8,128)} %param.18) | copy-start | bytes 7504
  5.9 14.2 %copy-start.4 = (bf16[400,640]{1,0:T(8,128)(2,1)S(1)}, bf16[400,640]{1,0:T(8,128)(2,1)}, u32[]{:S(2)}) copy-start(bf16[400,640]{1,0:T(8,128)(2,1)} %constant.20.clone.table_ref) | copy-start | bytes 1536004
  6.0 13.2 %collective-permute-start = (f32[512,128]{1,0:T(8,128)S(1)}, f32[512,128]{1,0:T(8,128)S(1)}, u32[]{:S(2)}, u32[]{:S(2)}) collective-permute-start(f32[512,128]{1,0:T(8,128)S(1)} %get-tuple-element.21), channel_id=1, source_target_pairs={{0,2},{1,3},{2,0},{3,1},{4,6},{5,7},{6,4},{7,5},{8,10},{9,11},{10,... | collective-permute-start | bytes 786440 | tf_op jit(solution)/shard_map/ppermute | solution.py:404
  7.7 17.4 %copy-start.2 = (bf16[512,768]{1,0:T(8,128)(2,1)S(1)}, bf16[512,768]{1,0:T(8,128)(2,1)}, u32[]{:S(2)}) copy-start(bf16[512,768]{1,0:T(8,128)(2,1)} %constant.21.clone.refs_4_) | copy-start | bytes 2359300
  7.7 6.5 %collective-permute-start.2 = (f32[256,128]{1,0:T(8,128)S(1)}, f32[256,128]{1,0:T(8,128)S(1)}, u32[]{:S(2)}, u32[]{:S(2)}) collective-permute-start(f32[256,128]{1,0:T(8,128)S(1)} %get-tuple-element.17), channel_id=1, source_target_pairs={{0,1},{1,0},{2,3},{3,2},{4,5},{5,4},{6,7},{7,6},{8,9},{9,8},{10,11... | collective-permute-start | bytes 393224 | tf_op jit(solution)/shard_map/ppermute | solution.py:404
  8.5 7.4 %collective-permute-start.1 = (f32[256,128]{1,0:T(8,128)S(1)}, f32[256,128]{1,0:T(8,128)S(1)}, u32[]{:S(2)}, u32[]{:S(2)}) collective-permute-start(f32[256,128]{1,0:T(8,128)S(1)} %get-tuple-element.18), channel_id=1, source_target_pairs={{0,1},{1,0},{2,3},{3,2},{4,5},{5,4},{6,7},{7,6},{8,9},{9,8},{10,11... | collective-permute-start | bytes 393224 | tf_op jit(solution)/shard_map/ppermute | solution.py:404
  9.9 9.2 %collective-permute-start.3 = (f32[64,128]{1,0:T(8,128)S(1)}, f32[64,128]{1,0:T(8,128)S(1)}, u32[]{:S(2)}, u32[]{:S(2)}) collective-permute-start(f32[64,128]{1,0:T(8,128)S(1)} %shard_map.139), channel_id=1, source_target_pairs={{0,7},{1,6},{2,5},{3,4},{4,3},{5,2},{6,1},{7,0},{8,15},{9,14},{10,... | collective-permute-start | bytes 98312 | tf_op jit(solution)/shard_map/ppermute | solution.py:420
  15.9 6.7 %collective-permute-start.4 = (f32[256,128]{1,0:T(8,128)S(1)}, f32[256,128]{1,0:T(8,128)S(1)}, u32[]{:S(2)}, u32[]{:S(2)}) collective-permute-start(f32[256,128]{1,0:T(8,128)S(1)} %get-tuple-element.11._0), channel_id=1, source_target_pairs={{0,4},{1,5},{2,6},{3,7},{4,0},{5,1},{6,2},{7,3},{8,12},{9,13},{10,... | collective-permute-start | bytes 393224 | tf_op jit(solution)/shard_map/ppermute | solution.py:404
  18.9 6.2 %collective-permute-start.5 = (f32[256,128]{1,0:T(8,128)S(1)}, f32[256,128]{1,0:T(8,128)S(1)}, u32[]{:S(2)}, u32[]{:S(2)}) collective-permute-start(f32[256,128]{1,0:T(8,128)S(1)} %get-tuple-element.12._1), channel_id=1, source_target_pairs={{0,6},{1,7},{2,4},{3,5},{4,2},{5,3},{6,0},{7,1},{8,14},{9,15},{10,... | collective-permute-start | bytes 393224 | tf_op jit(solution)/shard_map/ppermute | solution.py:404
  19.2 5.9 %collective-permute-start.6 = (f32[256,128]{1,0:T(8,128)S(1)}, f32[256,128]{1,0:T(8,128)S(1)}, u32[]{:S(2)}, u32[]{:S(2)}) collective-permute-start(f32[256,128]{1,0:T(8,128)S(1)} %get-tuple-element.14), channel_id=1, source_target_pairs={{0,1},{1,0},{2,3},{3,2},{4,5},{5,4},{6,7},{7,6},{8,9},{9,8},{10,11... | collective-permute-start | bytes 393224 | tf_op jit(solution)/shard_map/ppermute | solution.py:404
  25.1 25.3 %copy-start.5 = (bf16[256,768]{1,0:T(8,128)(2,1)S(1)}, bf16[256,768]{1,0:T(8,128)(2,1)}, u32[]{:S(2)}) copy-start(bf16[256,768]{1,0:T(8,128)(2,1)} %constant.23.clone.inverse_ref) | copy-start | bytes 1179652
  25.1 25.3 %copy-start.6 = (bf16[256,768]{1,0:T(8,128)(2,1)S(1)}, bf16[256,768]{1,0:T(8,128)(2,1)}, u32[]{:S(2)}) copy-start(bf16[256,768]{1,0:T(8,128)(2,1)} %constant.22.clone.forward_ref) | copy-start | bytes 1179652
  50.4 19.2 %copy-start.1 = (bf16[1536,256]{1,0:T(8,128)(2,1)S(1)}, bf16[1536,256]{1,0:T(8,128)(2,1)}, u32[]{:S(2)}) copy-start(bf16[1536,256]{1,0:T(8,128)(2,1)} %constant.24.clone.table_ref) | copy-start | bytes 2359300
  51.7 32.5 %copy-start.8 = (bf16[8,64,240]{2,1,0:T(8,128)(2,1)S(1)}, bf16[8,64,240]{2,1,0:T(8,128)(2,1)}, u32[]{:S(2)}) copy-start(bf16[8,64,240]{2,1,0:T(8,128)(2,1)} %constant.25.clone.refs_8_) | copy-start | bytes 737284
  69.9 15.6 %copy-start.9 = (s32[1,2,4096]{2,1,0:T(2,128)S(1)}, s32[1,2,4096]{2,1,0:T(2,128)}, u32[]{:S(2)}) copy-start(s32[1,2,4096]{2,1,0:T(2,128)} %param.16) | copy-start | bytes 98308
  69.9 15.6 %copy-start.10 = (f32[8,25,25]{2,0,1:T(8,128)S(1)}, f32[8,25,25]{2,0,1:T(8,128)}, u32[]{:S(2)}) copy-start(f32[8,25,25]{2,0,1:T(8,128)} %param.20) | copy-start | bytes 60004
  69.9 5.1 %collective-permute-start.10 = (f32[256,128]{1,0:T(8,128)S(1)}, f32[256,128]{1,0:T(8,128)S(1)}, u32[]{:S(2)}, u32[]{:S(2)}) collective-permute-start(f32[256,128]{1,0:T(8,128)S(1)} %shard_map.144.refs_0_), channel_id=1, source_target_pairs={{0,1},{1,0},{2,3},{3,2},{4,5},{5,4},{6,7},{7,6},{8,9},{9,8},{10,11... | collective-permute-start | bytes 393224 | tf_op jit(solution)/shard_map/ppermute | solution.py:408
  71.5 7.8 %collective-permute-start.7 = (f32[256,128]{1,0:T(8,128)S(1)}, f32[256,128]{1,0:T(8,128)S(1)}, u32[]{:S(2)}, u32[]{:S(2)}) collective-permute-start(f32[256,128]{1,0:T(8,128)S(1)} %shard_map.144.refs_0_), channel_id=1, source_target_pairs={{0,4},{1,5},{2,6},{3,7},{4,0},{5,1},{6,2},{7,3},{8,12},{9,13},{10,... | collective-permute-start | bytes 393224 | tf_op jit(solution)/shard_map/ppermute | solution.py:408
  72.6 8.3 %collective-permute-start.9 = (f32[256,128]{1,0:T(8,128)S(1)}, f32[256,128]{1,0:T(8,128)S(1)}, u32[]{:S(2)}, u32[]{:S(2)}) collective-permute-start(f32[256,128]{1,0:T(8,128)S(1)} %shard_map.144.refs_0_), channel_id=1, source_target_pairs={{0,6},{1,7},{2,0},{3,1},{4,2},{5,3},{6,4},{7,5},{8,14},{9,15},{10,... | collective-permute-start | bytes 393224 | tf_op jit(solution)/shard_map/ppermute | solution.py:408
  73.6 8.0 %collective-permute-start.8 = (f32[256,128]{1,0:T(8,128)S(1)}, f32[256,128]{1,0:T(8,128)S(1)}, u32[]{:S(2)}, u32[]{:S(2)}) collective-permute-start(f32[256,128]{1,0:T(8,128)S(1)} %shard_map.144.refs_0_), channel_id=1, source_target_pairs={{0,2},{1,3},{2,4},{3,5},{4,6},{5,7},{6,0},{7,1},{8,10},{9,11},{10,... | collective-permute-start | bytes 393224 | tf_op jit(solution)/shard_map/ppermute | solution.py:408
  75.0 7.3 %collective-permute-start.13 = (f32[256,128]{1,0:T(8,128)S(1)}, f32[256,128]{1,0:T(8,128)S(1)}, u32[]{:S(2)}, u32[]{:S(2)}) collective-permute-start(f32[256,128]{1,0:T(8,128)S(1)} %collective-permute-done.10.refs_4_), channel_id=1, source_target_pairs={{0,6},{1,7},{2,0},{3,1},{4,2},{5,3},{6,4},{7,5},{8,14},{9,15},{10,... | collective-permute-start | bytes 393224 | tf_op jit(solution)/shard_map/ppermute | solution.py:408
  77.1 6.2 %collective-permute-start.12 = (f32[256,128]{1,0:T(8,128)S(1)}, f32[256,128]{1,0:T(8,128)S(1)}, u32[]{:S(2)}, u32[]{:S(2)}) collective-permute-start(f32[256,128]{1,0:T(8,128)S(1)} %collective-permute-done.10.refs_4_), channel_id=1, source_target_pairs={{0,2},{1,3},{2,4},{3,5},{4,6},{5,7},{6,0},{7,1},{8,10},{9,11},{10,... | collective-permute-start | bytes 393224 | tf_op jit(solution)/shard_map/ppermute | solution.py:408
  79.3 5.0 %collective-permute-start.11 = (f32[256,128]{1,0:T(8,128)S(1)}, f32[256,128]{1,0:T(8,128)S(1)}, u32[]{:S(2)}, u32[]{:S(2)}) collective-permute-start(f32[256,128]{1,0:T(8,128)S(1)} %collective-permute-done.7.refs_1_), channel_id=1, source_target_pairs={{0,1},{1,0},{2,3},{3,2},{4,5},{5,4},{6,7},{7,6},{8,9},{9,8},{10,11... | collective-permute-start | bytes 393224 | tf_op jit(solution)/shard_map/ppermute | solution.py:408

commit v6 on v5

--- a/solution.py
+++ b/solution.py
@@ -198,15 +198,21 @@
 BATCH = 25
 
 
-def head_kernel(leaf_ref, aux_ref, out_ref):
-    w_cat = operator_rows(aux_ref, 64)
+def head_kernel(leaf_hbm, order_hbm, octant_hbm, op_hbm, out_ref, leaf_ref, order_ref, octant_ref, op_ref, ws, sems):
+    ends = [(op_hbm, op_ref), (order_hbm, order_ref), (octant_hbm, octant_ref), (leaf_hbm, leaf_ref)]
+    copies = [pltpu.make_async_copy(a, b, sems.at[i]) for i, (a, b) in enumerate(ends)]
+    for copy in copies:
+        copy.start()
+    copies[0].wait()
+    w_cat = load_operators(op_ref, ws)
     degree = degree_column()
+    for copy in copies[1:]:
+        copy.wait()
 
     def group(g, carry):
         b = g * GROUP
-        code = lane_rows(aux_ref, b, GROUP).astype(jnp.int32)
-        kept = jnp.where(degree <= (code & 7), load_blocks(leaf_ref, b), 0.0)
-        store_blocks(out_ref, b, *translate(w_cat, kept, code >> 3))
+        kept = jnp.where(degree <= lane_rows(order_ref, b, GROUP), load_blocks(leaf_ref, b), 0.0)
+        store_blocks(out_ref, b, *translate(w_cat, kept, lane_rows(octant_ref, b, GROUP)))
         return carry
 
     lax.fori_loop(0, 64 // GROUP, group, 0)
@@ -418,8 +424,20 @@
 
     packed = call(pack_kernel, shape(64, 128), [pltpu.VMEM((72, 128), F32)])(kernel)
     mirror = lax.ppermute(packed, "narrow", [(n, 7 - n) for n in range(8)])
-    aux = [(8 * octants + orders).astype(F32), jnp.pad(m2m, ((0, 0), (0, 128 - NC)))]
-    moments = call(head_kernel, shape(NC * 64, 128))(leaves, jnp.concatenate(aux, axis=0))
+    inputs = [pltpu.with_memory_space_constraint(array, pltpu.HBM) for array in (leaves, orders, octants, m2m)]
+    moments = call(
+        head_kernel,
+        shape(NC * 64, 128),
+        [
+            pltpu.VMEM((NC * 64, 128), F32),
+            pltpu.VMEM((64, 128), jnp.int32),
+            pltpu.VMEM((64, 128), jnp.int32),
+            pltpu.VMEM((NC * 8, NC), F32),
+            pltpu.VMEM((256, 128), F32),
+            pltpu.SemaphoreType.DMA((4,)),
+        ],
+        [pl.BlockSpec(memory_space=pltpu.HBM)] * 4,
+    )(*inputs)
     whole = pl.BlockSpec(memory_space=pltpu.VMEM)
     anywhere = pl.BlockSpec(memory_space=pl.ANY)
     chunks = call(z_forward_kernel, shape(2048, 128))(moments, jnp.asarray(Z_FORWARD))

time: 88.4 us -> 86.7 us (0.981)
  other arithmetic: 1.73 us -> 0 us
  Pallas kernels: 10.7 us -> 12 us
  local copies, waits for them, and re-layouts: 1.28 us -> 0.14 us
    pallas_call x1, Pallas kernels: 1.78 us -> 3.03 us  [shards(): call(head_kernel, shape(NC * 64, 128), [pltpu.VMEM((NC * 64, 128), F32),...]
    unnamed x24 -> x22, local copies, waits for them, and re-layouts: 1.2 us -> 0.06 us
    concatenate x1 -> x0, other arithmetic: 0.9 us -> none  [shards(): jnp.concatenate(aux, axis=0)]
where the time goes in v6:
time: 86.7 us; the launch traced here: 86.5 us
  blocking collectives  42.7 us (49%)
  starting transfers between devices  17.5 us (20%)
  waiting for transfers between devices  14 us (16%)
  Pallas kernels  12 us (14%)
    all_to_all x2, blocking collectives, shards(): lax.all_to_all(along.reshape(32, 16, 128), 'wide', split_axis=0, concat_a...  42.7 us
    ppermute x6, starting transfers between devices, swap(): return lax.ppermute(array, 'narrow', [(n, n ^ partner) for n in range(8)])  7.95 us
    ppermute x7, starting transfers between devices, shift(): lax.ppermute(array, 'narrow', [(n, stepped(n, step, 1)) for n in range(8)])  7.3 us
    ppermute x7, waiting for transfers between devices, shift(): lax.ppermute(array, 'narrow', [(n, stepped(n, step, 1)) for n in range(8)])  7.04 us
    ppermute x6, waiting for transfers between devices, swap(): return lax.ppermute(array, 'narrow', [(n, n ^ partner) for n in range(8)])  7 us
    pallas_call x1, Pallas kernels, shards(): call(head_kernel, shape(NC * 64, 128), [pltpu.VMEM((NC * 64, 128), F32),...  3.03 us
    pallas_call x1, Pallas kernels, shards(): call(tail_kernel, shape(NC * 64, 128), [pltpu.VMEM((256, 128), F32)])  2.63 us
    ppermute x1, starting transfers between devices, shards(): mirror = lax.ppermute(packed, 'narrow', [(n, 7 - n) for n in range(8)])  2.23 us
  transfers between devices with their start and end apart: 14, of which 11 were waited for; matrix products, arithmetic and copies ran while one was open for 0% of the time, Pallas kernels for 2%

profile of v6, /device:TPU:2, one launch (start us, length us, event | category | flops | bytes accessed | tf_op | source)
XLA Modules:
  0.0 86.5 jit_solution(16462498085245354581)
XLA Ops:
  0.0 3.0 %shard_map.136.ms = f32[1600,128]{1,0:T(8,128)S(1)} custom-call(f32[1600,128]{1,0:T(8,128)} %bitcast.40, s32[64,128]{1,0:T(8,128)} %bitcast.42, s32[64,128]{1,0:T(8,128)} %bitcast.37, f32[200,25]{1,0:T(8,128)} %bitcast.41), custom_call_target="tpu_custom_call" | custom-call | tf_op jit(solution)/shard_map/pallas_call | solution.py:428
  3.1 1.2 %shard_map.137 = f32[2048,128]{1,0:T(8,128)S(1)} custom-call(f32[1600,128]{1,0:T(8,128)S(1)} %shard_map.136.ms, bf16[8,80,192]{2,1,0:T(8,128)(2,1)S(1)} %copy-done.6), custom_call_target="tpu_custom_call" | custom-call | tf_op jit(solution)/shard_map/pallas_call | solution.py:443
  4.3 1.7 %collective-permute-start = (f32[512,128]{1,0:T(8,128)S(1)}, f32[512,128]{1,0:T(8,128)S(1)}, u32[]{:S(2)}, u32[]{:S(2)}) collective-permute-start(f32[512,128]{1,0:T(8,128)S(1)} %get-tuple-element.21), channel_id=1, source_target_pairs={{0,2},{1,3},{2,0},{3,1},{4,6},{5,7},{6,4},{7,5},{8,10},{9,11},{10,... | collective-permute-start | bytes 786440 | tf_op jit(solution)/shard_map/ppermute | solution.py:410
  6.0 0.8 collective-permute-start.2
  6.8 1.3 %collective-permute-start.1 = (f32[256,128]{1,0:T(8,128)S(1)}, f32[256,128]{1,0:T(8,128)S(1)}, u32[]{:S(2)}, u32[]{:S(2)}) collective-permute-start(f32[256,128]{1,0:T(8,128)S(1)} %get-tuple-element.18), channel_id=1, source_target_pairs={{0,1},{1,0},{2,3},{3,2},{4,5},{5,4},{6,7},{7,6},{8,9},{9,8},{10,11... | collective-permute-start | bytes 393224 | tf_op jit(solution)/shard_map/ppermute | solution.py:410
  8.2 2.2 %collective-permute-start.3 = (f32[64,128]{1,0:T(8,128)S(1)}, f32[64,128]{1,0:T(8,128)S(1)}, u32[]{:S(2)}, u32[]{:S(2)}) collective-permute-start(f32[64,128]{1,0:T(8,128)S(1)} %shard_map.139), channel_id=1, source_target_pairs={{0,7},{1,6},{2,5},{3,4},{4,3},{5,2},{6,1},{7,0},{8,15},{9,14},{10,... | collective-permute-start | bytes 98312 | tf_op jit(solution)/shard_map/ppermute | solution.py:426
  10.5 2.1 %collective-permute-done.2.mid_other = f32[256,128]{1,0:T(8,128)S(1)} collective-permute-done((f32[256,128]{1,0:T(8,128)S(1)}, f32[256,128]{1,0:T(8,128)S(1)}, u32[]{:S(2)}, u32[]{:S(2)}) %collective-permute-start.2) | collective-permute-done | bytes 131104 | tf_op jit(solution)/shard_map/ppermute | solution.py:410
  12.5 1.7 %collective-permute-done.1.far_other = f32[256,128]{1,0:T(8,128)S(1)} collective-permute-done((f32[256,128]{1,0:T(8,128)S(1)}, f32[256,128]{1,0:T(8,128)S(1)}, u32[]{:S(2)}, u32[]{:S(2)}) %collective-permute-start.1) | collective-permute-done | bytes 131104 | tf_op jit(solution)/shard_map/ppermute | solution.py:410
  14.3 3.0 %collective-permute-start.4 = (f32[256,128]{1,0:T(8,128)S(1)}, f32[256,128]{1,0:T(8,128)S(1)}, u32[]{:S(2)}, u32[]{:S(2)}) collective-permute-start(f32[256,128]{1,0:T(8,128)S(1)} %get-tuple-element.11._0), channel_id=1, source_target_pairs={{0,4},{1,5},{2,6},{3,7},{4,0},{5,1},{6,2},{7,3},{8,12},{9,13},{10,... | collective-permute-start | bytes 393224 | tf_op jit(solution)/shard_map/ppermute | solution.py:410
  17.5 1.0 %collective-permute-start.6 = (f32[256,128]{1,0:T(8,128)S(1)}, f32[256,128]{1,0:T(8,128)S(1)}, u32[]{:S(2)}, u32[]{:S(2)}) collective-permute-start(f32[256,128]{1,0:T(8,128)S(1)} %get-tuple-element.14), channel_id=1, source_target_pairs={{0,1},{1,0},{2,3},{3,2},{4,5},{5,4},{6,7},{7,6},{8,9},{9,8},{10,11... | collective-permute-start | bytes 393224 | tf_op jit(solution)/shard_map/ppermute | solution.py:410
  18.5 1.7 %shard_map.141 = (f32[2,2,128,640]{3,2,1,0:T(8,128)S(1)}, bf16[384,640]{1,0:T(8,128)(2,1)S(1)}) custom-call(f32[2,9,2,8,64]{4,3,2,1,0:T(8,128)S(1)} %bitcast.36, f32[64,128]{1,0:T(8,128)S(1)} %collective-permute-done.3._2.mirror_ref, f32[32,32]{1,0:T(8,128)S(1)} %pad.4.coupling_ref, bf16[400,640]{1,0:T(8,128)(2,1)S(1)} %copy-done.3), custom_call_target="tpu_custom_call" | custom-call | tf_op jit(solution)/shard_map/pallas_call | solution.py:454
  20.2 0.7 collective-permute-done.4.refs_1_
  20.9 2.5 %collective-permute-done.5.refs_2_ = f32[256,128]{1,0:T(8,128)S(1)} collective-permute-done((f32[256,128]{1,0:T(8,128)S(1)}, f32[256,128]{1,0:T(8,128)S(1)}, u32[]{:S(2)}, u32[]{:S(2)}) %collective-permute-start.5) | collective-permute-done | bytes 131104 | tf_op jit(solution)/shard_map/ppermute | solution.py:410
  23.5 0.4 shard_map.142
  23.8 24.9 %all_to_all.10 = f32[32,16,128]{2,1,0:T(8,128)S(1)} all-to-all(f32[32,16,128]{2,1,0:T(8,128)S(1)} %bitcast.34), channel_id=1, replica_groups=mesh['wide'=32,'narrow'=8] {'wide'}, dimensions={0} | all-to-all | bytes 524288 | tf_op jit(solution)/shard_map/all_to_all | solution.py:459
  48.7 1.4 %shard_map.143 = f32[32,2,8,128]{3,2,1,0:T(8,128)S(1)} custom-call(f32[32,2,8,128]{3,2,1,0:T(8,128)S(1)} %bitcast.31, bf16[256,768]{1,0:T(8,128)(2,1)S(1)} %copy-done.5, bf16[384,640]{1,0:T(8,128)(2,1)S(1)} %get-tuple-element.16.c_ref, f32[2,2,128,640]{3,2,1,0:T(8,128)S(1)} %get-tuple-element.15.refs_5_.k_ref, bf16[256,768]{1,0:T(8,128)(2,1)S(1)} %copy-done.4), custom_call_target="tpu_custom_call" | custom-call | tf_op jit(solution)/shard_map/pallas_call | solution.py:460
  50.1 17.8 %all_to_all.11 = f32[32,16,128]{2,1,0:T(8,128)S(1)} all-to-all(f32[32,16,128]{2,1,0:T(8,128)S(1)} %bitcast.32), channel_id=1, replica_groups=mesh['wide'=32,'narrow'=8] {'wide'}, dimensions={0} | all-to-all | bytes 524288 | tf_op jit(solution)/shard_map/all_to_all | solution.py:463
  68.3 1.5 %collective-permute-start.10 = (f32[256,128]{1,0:T(8,128)S(1)}, f32[256,128]{1,0:T(8,128)S(1)}, u32[]{:S(2)}, u32[]{:S(2)}) collective-permute-start(f32[256,128]{1,0:T(8,128)S(1)} %shard_map.144.refs_0_), channel_id=1, source_target_pairs={{0,1},{1,0},{2,3},{3,2},{4,5},{5,4},{6,7},{7,6},{8,9},{9,8},{10,11... | collective-permute-start | bytes 393224 | tf_op jit(solution)/shard_map/ppermute | solution.py:414
  69.8 1.1 %collective-permute-start.7 = (f32[256,128]{1,0:T(8,128)S(1)}, f32[256,128]{1,0:T(8,128)S(1)}, u32[]{:S(2)}, u32[]{:S(2)}) collective-permute-start(f32[256,128]{1,0:T(8,128)S(1)} %shard_map.144.refs_0_), channel_id=1, source_target_pairs={{0,4},{1,5},{2,6},{3,7},{4,0},{5,1},{6,2},{7,3},{8,12},{9,13},{10,... | collective-permute-start | bytes 393224 | tf_op jit(solution)/shard_map/ppermute | solution.py:414
  70.9 1.1 %collective-permute-start.9 = (f32[256,128]{1,0:T(8,128)S(1)}, f32[256,128]{1,0:T(8,128)S(1)}, u32[]{:S(2)}, u32[]{:S(2)}) collective-permute-start(f32[256,128]{1,0:T(8,128)S(1)} %shard_map.144.refs_0_), channel_id=1, source_target_pairs={{0,6},{1,7},{2,0},{3,1},{4,2},{5,3},{6,4},{7,5},{8,14},{9,15},{10,... | collective-permute-start | bytes 393224 | tf_op jit(solution)/shard_map/ppermute | solution.py:414
  72.0 1.0 %collective-permute-start.8 = (f32[256,128]{1,0:T(8,128)S(1)}, f32[256,128]{1,0:T(8,128)S(1)}, u32[]{:S(2)}, u32[]{:S(2)}) collective-permute-start(f32[256,128]{1,0:T(8,128)S(1)} %shard_map.144.refs_0_), channel_id=1, source_target_pairs={{0,2},{1,3},{2,4},{3,5},{4,6},{5,7},{6,0},{7,1},{8,10},{9,11},{10,... | collective-permute-start | bytes 393224 | tf_op jit(solution)/shard_map/ppermute | solution.py:414
  73.0 0.4 collective-permute-done.10.refs_4_
  73.3 2.1 %collective-permute-start.13 = (f32[256,128]{1,0:T(8,128)S(1)}, f32[256,128]{1,0:T(8,128)S(1)}, u32[]{:S(2)}, u32[]{:S(2)}) collective-permute-start(f32[256,128]{1,0:T(8,128)S(1)} %collective-permute-done.10.refs_4_), channel_id=1, source_target_pairs={{0,6},{1,7},{2,0},{3,1},{4,2},{5,3},{6,4},{7,5},{8,14},{9,15},{10,... | collective-permute-start | bytes 393224 | tf_op jit(solution)/shard_map/ppermute | solution.py:414
  75.5 2.2 %collective-permute-done.7.refs_1_ = f32[256,128]{1,0:T(8,128)S(1)} collective-permute-done((f32[256,128]{1,0:T(8,128)S(1)}, f32[256,128]{1,0:T(8,128)S(1)}, u32[]{:S(2)}, u32[]{:S(2)}) %collective-permute-start.7) | collective-permute-done | bytes 131104 | tf_op jit(solution)/shard_map/ppermute | solution.py:414
  77.7 0.5 collective-permute-start.11
  78.1 1.0 %collective-permute-done.9.refs_3_ = f32[256,128]{1,0:T(8,128)S(1)} collective-permute-done((f32[256,128]{1,0:T(8,128)S(1)}, f32[256,128]{1,0:T(8,128)S(1)}, u32[]{:S(2)}, u32[]{:S(2)}) %collective-permute-start.9) | collective-permute-done | bytes 131104 | tf_op jit(solution)/shard_map/ppermute | solution.py:414
  79.2 0.8 collective-permute-done.8.refs_2_
  79.9 0.6 collective-permute-done.13.refs_7_
  80.6 1.1 %collective-permute-done.12.refs_6_ = f32[256,128]{1,0:T(8,128)S(1)} collective-permute-done((f32[256,128]{1,0:T(8,128)S(1)}, f32[256,128]{1,0:T(8,128)S(1)}, u32[]{:S(2)}, u32[]{:S(2)}) %collective-permute-start.12) | collective-permute-done | bytes 131104 | tf_op jit(solution)/shard_map/ppermute | solution.py:414
  81.7 1.0 %collective-permute-done.11.refs_5_ = f32[256,128]{1,0:T(8,128)S(1)} collective-permute-done((f32[256,128]{1,0:T(8,128)S(1)}, f32[256,128]{1,0:T(8,128)S(1)}, u32[]{:S(2)}, u32[]{:S(2)}) %collective-permute-start.11) | collective-permute-done | bytes 131104 | tf_op jit(solution)/shard_map/ppermute | solution.py:414
  82.6 1.2 %shard_map.145.local_ref = f32[1600,128]{1,0:T(8,128)S(1)} custom-call(f32[256,128]{1,0:T(8,128)S(1)} %shard_map.144.refs_0_, f32[256,128]{1,0:T(8,128)S(1)} %collective-permute-done.7.refs_1_, f32[256,128]{1,0:T(8,128)S(1)} %collective-permute-done.8.refs_2_, f32[256,128]{1,0:T(8,128)S(1)} %collective-permute-done.9.refs_3_, ...), custom_call_target="tpu_custom_call" | custom-call | tf_op jit(solution)/shard_map/pallas_call | solution.py:471
  83.9 2.6 %shard_map.146 = f32[1600,128]{1,0:T(8,128)} custom-call(f32[1600,128]{1,0:T(8,128)S(1)} %shard_map.145.local_ref, s32[64,128]{1,0:T(8,128)S(1)} %bitcast.38, f32[200,25]{1,0:T(8,128)S(1)} %bitcast.39), custom_call_target="tpu_custom_call" | custom-call | tf_op jit(solution)/shard_map/pallas_call | solution.py:472
  (34 shorter events, 0.9 us)
Async XLA Ops:
  0.0 3.0 %copy-start.6 = (bf16[8,80,192]{2,1,0:T(8,128)(2,1)S(1)}, bf16[8,80,192]{2,1,0:T(8,128)(2,1)}, u32[]{:S(2)}) copy-start(bf16[8,80,192]{2,1,0:T(8,128)(2,1)} %constant.17.clone.table_ref) | copy-start | bytes 737284
  4.2 3.9 %copy-start.2 = (f32[2,9,64,2,8]{2,4,3,1,0:T(8,128)S(1)}, f32[2,9,64,2,8]{2,4,3,1,0:T(8,128)}, u32[]{:S(2)}) copy-start(f32[2,9,64,2,8]{2,4,3,1,0:T(8,128)} %param.19) | copy-start | bytes 221188
  4.3 14.2 %copy-start.10 = (f32[25,25]{1,0:T(8,128)S(1)}, f32[25,25]{1,0:T(8,128)}, u32[]{:S(2)}) copy-start(f32[25,25]{1,0:T(8,128)} %param.18) | copy-start | bytes 7504
  4.3 14.2 %copy-start.3 = (bf16[400,640]{1,0:T(8,128)(2,1)S(1)}, bf16[400,640]{1,0:T(8,128)(2,1)}, u32[]{:S(2)}) copy-start(bf16[400,640]{1,0:T(8,128)(2,1)} %constant.18.clone.table_ref) | copy-start | bytes 1536004
  4.3 13.2 %collective-permute-start = (f32[512,128]{1,0:T(8,128)S(1)}, f32[512,128]{1,0:T(8,128)S(1)}, u32[]{:S(2)}, u32[]{:S(2)}) collective-permute-start(f32[512,128]{1,0:T(8,128)S(1)} %get-tuple-element.21), channel_id=1, source_target_pairs={{0,2},{1,3},{2,0},{3,1},{4,6},{5,7},{6,4},{7,5},{8,10},{9,11},{10,... | collective-permute-start | bytes 786440 | tf_op jit(solution)/shard_map/ppermute | solution.py:410
  6.0 17.4 %copy-start.1 = (bf16[512,768]{1,0:T(8,128)(2,1)S(1)}, bf16[512,768]{1,0:T(8,128)(2,1)}, u32[]{:S(2)}) copy-start(bf16[512,768]{1,0:T(8,128)(2,1)} %constant.19.clone.refs_4_) | copy-start | bytes 2359300
  6.0 6.5 %collective-permute-start.2 = (f32[256,128]{1,0:T(8,128)S(1)}, f32[256,128]{1,0:T(8,128)S(1)}, u32[]{:S(2)}, u32[]{:S(2)}) collective-permute-start(f32[256,128]{1,0:T(8,128)S(1)} %get-tuple-element.17), channel_id=1, source_target_pairs={{0,1},{1,0},{2,3},{3,2},{4,5},{5,4},{6,7},{7,6},{8,9},{9,8},{10,11... | collective-permute-start | bytes 393224 | tf_op jit(solution)/shard_map/ppermute | solution.py:410
  6.8 7.4 %collective-permute-start.1 = (f32[256,128]{1,0:T(8,128)S(1)}, f32[256,128]{1,0:T(8,128)S(1)}, u32[]{:S(2)}, u32[]{:S(2)}) collective-permute-start(f32[256,128]{1,0:T(8,128)S(1)} %get-tuple-element.18), channel_id=1, source_target_pairs={{0,1},{1,0},{2,3},{3,2},{4,5},{5,4},{6,7},{7,6},{8,9},{9,8},{10,11... | collective-permute-start | bytes 393224 | tf_op jit(solution)/shard_map/ppermute | solution.py:410
  8.2 9.2 %collective-permute-start.3 = (f32[64,128]{1,0:T(8,128)S(1)}, f32[64,128]{1,0:T(8,128)S(1)}, u32[]{:S(2)}, u32[]{:S(2)}) collective-permute-start(f32[64,128]{1,0:T(8,128)S(1)} %shard_map.139), channel_id=1, source_target_pairs={{0,7},{1,6},{2,5},{3,4},{4,3},{5,2},{6,1},{7,0},{8,15},{9,14},{10,... | collective-permute-start | bytes 98312 | tf_op jit(solution)/shard_map/ppermute | solution.py:426
  14.3 6.7 %collective-permute-start.4 = (f32[256,128]{1,0:T(8,128)S(1)}, f32[256,128]{1,0:T(8,128)S(1)}, u32[]{:S(2)}, u32[]{:S(2)}) collective-permute-start(f32[256,128]{1,0:T(8,128)S(1)} %get-tuple-element.11._0), channel_id=1, source_target_pairs={{0,4},{1,5},{2,6},{3,7},{4,0},{5,1},{6,2},{7,3},{8,12},{9,13},{10,... | collective-permute-start | bytes 393224 | tf_op jit(solution)/shard_map/ppermute | solution.py:410
  17.3 6.2 %collective-permute-start.5 = (f32[256,128]{1,0:T(8,128)S(1)}, f32[256,128]{1,0:T(8,128)S(1)}, u32[]{:S(2)}, u32[]{:S(2)}) collective-permute-start(f32[256,128]{1,0:T(8,128)S(1)} %get-tuple-element.12._1), channel_id=1, source_target_pairs={{0,6},{1,7},{2,4},{3,5},{4,2},{5,3},{6,0},{7,1},{8,14},{9,15},{10,... | collective-permute-start | bytes 393224 | tf_op jit(solution)/shard_map/ppermute | solution.py:410
  17.5 5.9 %collective-permute-start.6 = (f32[256,128]{1,0:T(8,128)S(1)}, f32[256,128]{1,0:T(8,128)S(1)}, u32[]{:S(2)}, u32[]{:S(2)}) collective-permute-start(f32[256,128]{1,0:T(8,128)S(1)} %get-tuple-element.14), channel_id=1, source_target_pairs={{0,1},{1,0},{2,3},{3,2},{4,5},{5,4},{6,7},{7,6},{8,9},{9,8},{10,11... | collective-permute-start | bytes 393224 | tf_op jit(solution)/shard_map/ppermute | solution.py:410
  23.4 25.3 %copy-start.4 = (bf16[256,768]{1,0:T(8,128)(2,1)S(1)}, bf16[256,768]{1,0:T(8,128)(2,1)}, u32[]{:S(2)}) copy-start(bf16[256,768]{1,0:T(8,128)(2,1)} %constant.21.clone.inverse_ref) | copy-start | bytes 1179652
  23.4 25.3 %copy-start.5 = (bf16[256,768]{1,0:T(8,128)(2,1)S(1)}, bf16[256,768]{1,0:T(8,128)(2,1)}, u32[]{:S(2)}) copy-start(bf16[256,768]{1,0:T(8,128)(2,1)} %constant.20.clone.forward_ref) | copy-start | bytes 1179652
  48.7 19.2 %copy-start = (bf16[1536,256]{1,0:T(8,128)(2,1)S(1)}, bf16[1536,256]{1,0:T(8,128)(2,1)}, u32[]{:S(2)}) copy-start(bf16[1536,256]{1,0:T(8,128)(2,1)} %constant.22.clone.table_ref) | copy-start | bytes 2359300
  50.1 32.5 %copy-start.7 = (bf16[8,64,240]{2,1,0:T(8,128)(2,1)S(1)}, bf16[8,64,240]{2,1,0:T(8,128)(2,1)}, u32[]{:S(2)}) copy-start(bf16[8,64,240]{2,1,0:T(8,128)(2,1)} %constant.23.clone.refs_8_) | copy-start | bytes 737284
  68.3 15.6 %copy-start.8 = (s32[1,2,4096]{2,1,0:T(2,128)S(1)}, s32[1,2,4096]{2,1,0:T(2,128)}, u32[]{:S(2)}) copy-start(s32[1,2,4096]{2,1,0:T(2,128)} %param.16) | copy-start | bytes 98308
  68.3 15.6 %copy-start.9 = (f32[8,25,25]{2,0,1:T(8,128)S(1)}, f32[8,25,25]{2,0,1:T(8,128)}, u32[]{:S(2)}) copy-start(f32[8,25,25]{2,0,1:T(8,128)} %param.20) | copy-start | bytes 60004
  68.3 5.1 %collective-permute-start.10 = (f32[256,128]{1,0:T(8,128)S(1)}, f32[256,128]{1,0:T(8,128)S(1)}, u32[]{:S(2)}, u32[]{:S(2)}) collective-permute-start(f32[256,128]{1,0:T(8,128)S(1)} %shard_map.144.refs_0_), channel_id=1, source_target_pairs={{0,1},{1,0},{2,3},{3,2},{4,5},{5,4},{6,7},{7,6},{8,9},{9,8},{10,11... | collective-permute-start | bytes 393224 | tf_op jit(solution)/shard_map/ppermute | solution.py:414
  69.8 7.8 %collective-permute-start.7 = (f32[256,128]{1,0:T(8,128)S(1)}, f32[256,128]{1,0:T(8,128)S(1)}, u32[]{:S(2)}, u32[]{:S(2)}) collective-permute-start(f32[256,128]{1,0:T(8,128)S(1)} %shard_map.144.refs_0_), channel_id=1, source_target_pairs={{0,4},{1,5},{2,6},{3,7},{4,0},{5,1},{6,2},{7,3},{8,12},{9,13},{10,... | collective-permute-start | bytes 393224 | tf_op jit(solution)/shard_map/ppermute | solution.py:414
  70.9 8.3 %collective-permute-start.9 = (f32[256,128]{1,0:T(8,128)S(1)}, f32[256,128]{1,0:T(8,128)S(1)}, u32[]{:S(2)}, u32[]{:S(2)}) collective-permute-start(f32[256,128]{1,0:T(8,128)S(1)} %shard_map.144.refs_0_), channel_id=1, source_target_pairs={{0,6},{1,7},{2,0},{3,1},{4,2},{5,3},{6,4},{7,5},{8,14},{9,15},{10,... | collective-permute-start | bytes 393224 | tf_op jit(solution)/shard_map/ppermute | solution.py:414
  72.0 8.0 %collective-permute-start.8 = (f32[256,128]{1,0:T(8,128)S(1)}, f32[256,128]{1,0:T(8,128)S(1)}, u32[]{:S(2)}, u32[]{:S(2)}) collective-permute-start(f32[256,128]{1,0:T(8,128)S(1)} %shard_map.144.refs_0_), channel_id=1, source_target_pairs={{0,2},{1,3},{2,4},{3,5},{4,6},{5,7},{6,0},{7,1},{8,10},{9,11},{10,... | collective-permute-start | bytes 393224 | tf_op jit(solution)/shard_map/ppermute | solution.py:414
  73.3 7.2 %collective-permute-start.13 = (f32[256,128]{1,0:T(8,128)S(1)}, f32[256,128]{1,0:T(8,128)S(1)}, u32[]{:S(2)}, u32[]{:S(2)}) collective-permute-start(f32[256,128]{1,0:T(8,128)S(1)} %collective-permute-done.10.refs_4_), channel_id=1, source_target_pairs={{0,6},{1,7},{2,0},{3,1},{4,2},{5,3},{6,4},{7,5},{8,14},{9,15},{10,... | collective-permute-start | bytes 393224 | tf_op jit(solution)/shard_map/ppermute | solution.py:414
  75.5 6.2 %collective-permute-start.12 = (f32[256,128]{1,0:T(8,128)S(1)}, f32[256,128]{1,0:T(8,128)S(1)}, u32[]{:S(2)}, u32[]{:S(2)}) collective-permute-start(f32[256,128]{1,0:T(8,128)S(1)} %collective-permute-done.10.refs_4_), channel_id=1, source_target_pairs={{0,2},{1,3},{2,4},{3,5},{4,6},{5,7},{6,0},{7,1},{8,10},{9,11},{10,... | collective-permute-start | bytes 393224 | tf_op jit(solution)/shard_map/ppermute | solution.py:414
  77.7 5.0 %collective-permute-start.11 = (f32[256,128]{1,0:T(8,128)S(1)}, f32[256,128]{1,0:T(8,128)S(1)}, u32[]{:S(2)}, u32[]{:S(2)}) collective-permute-start(f32[256,128]{1,0:T(8,128)S(1)} %collective-permute-done.7.refs_1_), channel_id=1, source_target_pairs={{0,1},{1,0},{2,3},{3,2},{4,5},{5,4},{6,7},{7,6},{8,9},{9,8},{10,11... | collective-permute-start | bytes 393224 | tf_op jit(solution)/shard_map/ppermute | solution.py:414

commit v7 on v6

--- a/solution.py
+++ b/solution.py
@@ -194,7 +194,7 @@
     return total, last
 
 
-GROUP = 64
+GROUP = 32
 BATCH = 25
 
 
@@ -365,19 +365,24 @@
     lax.fori_loop(0, NC // BATCH, coefficients, 0)
 
 
-def tail_kernel(local_ref, octant_ref, op_ref, out_ref, ws):
+def tail_kernel(local_ref, octant_ref, op_ref, out_hbm, ws, out_ref, sems):
     w_cat = load_operators(op_ref, ws)
-
-    def group(g, carry):
-        b = g * GROUP
-        store_blocks(out_ref, b, *translate(w_cat, load_blocks(local_ref, b), lane_rows(octant_ref, b, GROUP)))
-        return carry
-
-    lax.fori_loop(0, 64 // GROUP, group, 0)
-
-
-def call(kernel, out_shape, scratch=(), in_specs=None):
+    copies = []
+    for half in range(2):
+        for b in range(32 * half, 32 * half + 32, GROUP):
+            store_blocks(out_ref, b, *translate(w_cat, load_blocks(local_ref, b), lane_rows(octant_ref, b, GROUP)))
+        rows = pl.ds(32 * half, 32)
+        done = out_ref.reshape(NC, 64, 128).at[:, rows]
+        copies.append(pltpu.make_async_copy(done, out_hbm.at[:, rows], sems.at[half]))
+        copies[half].start()
+    for copy in copies:
+        copy.wait()
+
+
+def call(kernel, out_shape, scratch=(), in_specs=None, out_specs=None):
     args = {}
+    if out_specs is not None:
+        args["out_specs"] = out_specs
     if in_specs is not None:
         args["in_specs"] = in_specs
     return pl.pallas_call(
@@ -469,7 +474,13 @@
     far_other, above_other, below_other = shift(far, ACROSS), shift(other, ABOVE), shift(other, BELOW)
     planes = [plane, far, above, below, other, far_other, above_other, below_other]
     local = call(z_inverse_kernel, shape(NC * 64, 128), [pltpu.VMEM((2048, 128), F32)])(*planes, jnp.asarray(Z_INVERSE))
-    children = call(tail_kernel, shape(NC * 64, 128), [pltpu.VMEM((256, 128), F32)])(local, octants, l2l)
+    children = call(
+        tail_kernel,
+        shape(NC, 64, 128),
+        [pltpu.VMEM((256, 128), F32), pltpu.VMEM((NC * 64, 128), F32), pltpu.SemaphoreType.DMA((2,))],
+        [whole] * 3,
+        pl.BlockSpec(memory_space=pltpu.HBM),
+    )(local, octants, l2l)
     children = children.reshape(NC, 32, 2, 128).swapaxes(1, 2)
     return children.reshape(1, NC, 2, 4096)
 

time: 86.7 us -> 86.7 us (level)
  no operation moved by 1% of the time
where the time goes in v7:
time: 86.7 us; the launch traced here: 86.6 us
  blocking collectives  42.7 us (49%)
  starting transfers between devices  17.5 us (20%)
  waiting for transfers between devices  14 us (16%)
  Pallas kernels  11.9 us (14%)
    all_to_all x2, blocking collectives, shards(): lax.all_to_all(along.reshape(32, 16, 128), 'wide', split_axis=0, concat_a...  42.7 us
    ppermute x6, starting transfers between devices, swap(): return lax.ppermute(array, 'narrow', [(n, n ^ partner) for n in range(8)])  7.95 us
    ppermute x7, starting transfers between devices, shift(): lax.ppermute(array, 'narrow', [(n, stepped(n, step, 1)) for n in range(8)])  7.32 us
    ppermute x7, waiting for transfers between devices, shift(): lax.ppermute(array, 'narrow', [(n, stepped(n, step, 1)) for n in range(8)])  7.01 us
    ppermute x6, waiting for transfers between devices, swap(): return lax.ppermute(array, 'narrow', [(n, n ^ partner) for n in range(8)])  6.99 us
    pallas_call x1, Pallas kernels, shards(): call(head_kernel, shape(NC * 64, 128), [pltpu.VMEM((NC * 64, 128), F32),...  3.05 us
    pallas_call x1, Pallas kernels, shards(): call(tail_kernel, shape(NC, 64, 128), [pltpu.VMEM((256, 128), F32), pltpu...  2.49 us
    ppermute x1, starting transfers between devices, shards(): mirror = lax.ppermute(packed, 'narrow', [(n, 7 - n) for n in range(8)])  2.23 us
  transfers between devices with their start and end apart: 14, of which 11 were waited for; matrix products, arithmetic and copies ran while one was open for 0% of the time, Pallas kernels for 2%

profile of v7, /device:TPU:2, one launch (start us, length us, event | category | flops | bytes accessed | tf_op | source)
XLA Modules:
  0.0 86.6 jit_solution(5890301728529442538)
XLA Ops:
  0.0 3.1 %shard_map.136.ms = f32[1600,128]{1,0:T(8,128)S(1)} custom-call(f32[1600,128]{1,0:T(8,128)} %bitcast.40, s32[64,128]{1,0:T(8,128)} %bitcast.42, s32[64,128]{1,0:T(8,128)} %bitcast.37, f32[200,25]{1,0:T(8,128)} %bitcast.41), custom_call_target="tpu_custom_call" | custom-call | tf_op jit(solution)/shard_map/pallas_call | solution.py:433
  3.1 1.2 %shard_map.137 = f32[2048,128]{1,0:T(8,128)S(1)} custom-call(f32[1600,128]{1,0:T(8,128)S(1)} %shard_map.136.ms, bf16[8,80,192]{2,1,0:T(8,128)(2,1)S(1)} %copy-done.6), custom_call_target="tpu_custom_call" | custom-call | tf_op jit(solution)/shard_map/pallas_call | solution.py:448
  4.3 1.7 %collective-permute-start = (f32[512,128]{1,0:T(8,128)S(1)}, f32[512,128]{1,0:T(8,128)S(1)}, u32[]{:S(2)}, u32[]{:S(2)}) collective-permute-start(f32[512,128]{1,0:T(8,128)S(1)} %get-tuple-element.21), channel_id=1, source_target_pairs={{0,2},{1,3},{2,0},{3,1},{4,6},{5,7},{6,4},{7,5},{8,10},{9,11},{10,... | collective-permute-start | bytes 786440 | tf_op jit(solution)/shard_map/ppermute | solution.py:415
  6.1 0.8 collective-permute-start.2
  6.9 1.3 %collective-permute-start.1 = (f32[256,128]{1,0:T(8,128)S(1)}, f32[256,128]{1,0:T(8,128)S(1)}, u32[]{:S(2)}, u32[]{:S(2)}) collective-permute-start(f32[256,128]{1,0:T(8,128)S(1)} %get-tuple-element.18), channel_id=1, source_target_pairs={{0,1},{1,0},{2,3},{3,2},{4,5},{5,4},{6,7},{7,6},{8,9},{9,8},{10,11... | collective-permute-start | bytes 393224 | tf_op jit(solution)/shard_map/ppermute | solution.py:415
  8.3 2.2 %collective-permute-start.3 = (f32[64,128]{1,0:T(8,128)S(1)}, f32[64,128]{1,0:T(8,128)S(1)}, u32[]{:S(2)}, u32[]{:S(2)}) collective-permute-start(f32[64,128]{1,0:T(8,128)S(1)} %shard_map.139), channel_id=1, source_target_pairs={{0,7},{1,6},{2,5},{3,4},{4,3},{5,2},{6,1},{7,0},{8,15},{9,14},{10,... | collective-permute-start | bytes 98312 | tf_op jit(solution)/shard_map/ppermute | solution.py:431
  10.5 2.1 %collective-permute-done.2.mid_other = f32[256,128]{1,0:T(8,128)S(1)} collective-permute-done((f32[256,128]{1,0:T(8,128)S(1)}, f32[256,128]{1,0:T(8,128)S(1)}, u32[]{:S(2)}, u32[]{:S(2)}) %collective-permute-start.2) | collective-permute-done | bytes 131104 | tf_op jit(solution)/shard_map/ppermute | solution.py:415
  12.6 1.7 %collective-permute-done.1.far_other = f32[256,128]{1,0:T(8,128)S(1)} collective-permute-done((f32[256,128]{1,0:T(8,128)S(1)}, f32[256,128]{1,0:T(8,128)S(1)}, u32[]{:S(2)}, u32[]{:S(2)}) %collective-permute-start.1) | collective-permute-done | bytes 131104 | tf_op jit(solution)/shard_map/ppermute | solution.py:415
  14.3 3.0 %collective-permute-start.4 = (f32[256,128]{1,0:T(8,128)S(1)}, f32[256,128]{1,0:T(8,128)S(1)}, u32[]{:S(2)}, u32[]{:S(2)}) collective-permute-start(f32[256,128]{1,0:T(8,128)S(1)} %get-tuple-element.11._0), channel_id=1, source_target_pairs={{0,4},{1,5},{2,6},{3,7},{4,0},{5,1},{6,2},{7,3},{8,12},{9,13},{10,... | collective-permute-start | bytes 393224 | tf_op jit(solution)/shard_map/ppermute | solution.py:415
  17.5 1.0 %collective-permute-start.6 = (f32[256,128]{1,0:T(8,128)S(1)}, f32[256,128]{1,0:T(8,128)S(1)}, u32[]{:S(2)}, u32[]{:S(2)}) collective-permute-start(f32[256,128]{1,0:T(8,128)S(1)} %get-tuple-element.14), channel_id=1, source_target_pairs={{0,1},{1,0},{2,3},{3,2},{4,5},{5,4},{6,7},{7,6},{8,9},{9,8},{10,11... | collective-permute-start | bytes 393224 | tf_op jit(solution)/shard_map/ppermute | solution.py:415
  18.5 1.7 %shard_map.141 = (f32[2,2,128,640]{3,2,1,0:T(8,128)S(1)}, bf16[384,640]{1,0:T(8,128)(2,1)S(1)}) custom-call(f32[2,9,2,8,64]{4,3,2,1,0:T(8,128)S(1)} %bitcast.36, f32[64,128]{1,0:T(8,128)S(1)} %collective-permute-done.3._2.mirror_ref, f32[32,32]{1,0:T(8,128)S(1)} %pad.4.coupling_ref, bf16[400,640]{1,0:T(8,128)(2,1)S(1)} %copy-done.3), custom_call_target="tpu_custom_call" | custom-call | tf_op jit(solution)/shard_map/pallas_call | solution.py:459
  20.2 0.7 collective-permute-done.4.refs_1_
  20.9 2.5 %collective-permute-done.5.refs_2_ = f32[256,128]{1,0:T(8,128)S(1)} collective-permute-done((f32[256,128]{1,0:T(8,128)S(1)}, f32[256,128]{1,0:T(8,128)S(1)}, u32[]{:S(2)}, u32[]{:S(2)}) %collective-permute-start.5) | collective-permute-done | bytes 131104 | tf_op jit(solution)/shard_map/ppermute | solution.py:415
  23.5 0.4 shard_map.142
  23.8 24.9 %all_to_all.10 = f32[32,16,128]{2,1,0:T(8,128)S(1)} all-to-all(f32[32,16,128]{2,1,0:T(8,128)S(1)} %bitcast.34), channel_id=1, replica_groups=mesh['wide'=32,'narrow'=8] {'wide'}, dimensions={0} | all-to-all | bytes 524288 | tf_op jit(solution)/shard_map/all_to_all | solution.py:464
  48.8 1.4 %shard_map.143 = f32[32,2,8,128]{3,2,1,0:T(8,128)S(1)} custom-call(f32[32,2,8,128]{3,2,1,0:T(8,128)S(1)} %bitcast.31, bf16[256,768]{1,0:T(8,128)(2,1)S(1)} %copy-done.5, bf16[384,640]{1,0:T(8,128)(2,1)S(1)} %get-tuple-element.16.c_ref, f32[2,2,128,640]{3,2,1,0:T(8,128)S(1)} %get-tuple-element.15.refs_5_.k_ref, bf16[256,768]{1,0:T(8,128)(2,1)S(1)} %copy-done.4), custom_call_target="tpu_custom_call" | custom-call | tf_op jit(solution)/shard_map/pallas_call | solution.py:465
  50.1 17.8 %all_to_all.11 = f32[32,16,128]{2,1,0:T(8,128)S(1)} all-to-all(f32[32,16,128]{2,1,0:T(8,128)S(1)} %bitcast.32), channel_id=1, replica_groups=mesh['wide'=32,'narrow'=8] {'wide'}, dimensions={0} | all-to-all | bytes 524288 | tf_op jit(solution)/shard_map/all_to_all | solution.py:468
  68.3 1.5 %collective-permute-start.10 = (f32[256,128]{1,0:T(8,128)S(1)}, f32[256,128]{1,0:T(8,128)S(1)}, u32[]{:S(2)}, u32[]{:S(2)}) collective-permute-start(f32[256,128]{1,0:T(8,128)S(1)} %shard_map.144.refs_0_), channel_id=1, source_target_pairs={{0,1},{1,0},{2,3},{3,2},{4,5},{5,4},{6,7},{7,6},{8,9},{9,8},{10,11... | collective-permute-start | bytes 393224 | tf_op jit(solution)/shard_map/ppermute | solution.py:419
  69.8 1.1 %collective-permute-start.7 = (f32[256,128]{1,0:T(8,128)S(1)}, f32[256,128]{1,0:T(8,128)S(1)}, u32[]{:S(2)}, u32[]{:S(2)}) collective-permute-start(f32[256,128]{1,0:T(8,128)S(1)} %shard_map.144.refs_0_), channel_id=1, source_target_pairs={{0,4},{1,5},{2,6},{3,7},{4,0},{5,1},{6,2},{7,3},{8,12},{9,13},{10,... | collective-permute-start | bytes 393224 | tf_op jit(solution)/shard_map/ppermute | solution.py:419
  70.9 1.1 %collective-permute-start.9 = (f32[256,128]{1,0:T(8,128)S(1)}, f32[256,128]{1,0:T(8,128)S(1)}, u32[]{:S(2)}, u32[]{:S(2)}) collective-permute-start(f32[256,128]{1,0:T(8,128)S(1)} %shard_map.144.refs_0_), channel_id=1, source_target_pairs={{0,6},{1,7},{2,0},{3,1},{4,2},{5,3},{6,4},{7,5},{8,14},{9,15},{10,... | collective-permute-start | bytes 393224 | tf_op jit(solution)/shard_map/ppermute | solution.py:419
  72.0 1.0 %collective-permute-start.8 = (f32[256,128]{1,0:T(8,128)S(1)}, f32[256,128]{1,0:T(8,128)S(1)}, u32[]{:S(2)}, u32[]{:S(2)}) collective-permute-start(f32[256,128]{1,0:T(8,128)S(1)} %shard_map.144.refs_0_), channel_id=1, source_target_pairs={{0,2},{1,3},{2,4},{3,5},{4,6},{5,7},{6,0},{7,1},{8,10},{9,11},{10,... | collective-permute-start | bytes 393224 | tf_op jit(solution)/shard_map/ppermute | solution.py:419
  73.0 0.4 collective-permute-done.10.refs_4_
  73.4 2.2 %collective-permute-start.13 = (f32[256,128]{1,0:T(8,128)S(1)}, f32[256,128]{1,0:T(8,128)S(1)}, u32[]{:S(2)}, u32[]{:S(2)}) collective-permute-start(f32[256,128]{1,0:T(8,128)S(1)} %collective-permute-done.10.refs_4_), channel_id=1, source_target_pairs={{0,6},{1,7},{2,0},{3,1},{4,2},{5,3},{6,4},{7,5},{8,14},{9,15},{10,... | collective-permute-start | bytes 393224 | tf_op jit(solution)/shard_map/ppermute | solution.py:419
  75.5 2.2 %collective-permute-done.7.refs_1_ = f32[256,128]{1,0:T(8,128)S(1)} collective-permute-done((f32[256,128]{1,0:T(8,128)S(1)}, f32[256,128]{1,0:T(8,128)S(1)}, u32[]{:S(2)}, u32[]{:S(2)}) %collective-permute-start.7) | collective-permute-done | bytes 131104 | tf_op jit(solution)/shard_map/ppermute | solution.py:419
  77.7 0.5 collective-permute-start.11
  78.2 1.0 %collective-permute-done.9.refs_3_ = f32[256,128]{1,0:T(8,128)S(1)} collective-permute-done((f32[256,128]{1,0:T(8,128)S(1)}, f32[256,128]{1,0:T(8,128)S(1)}, u32[]{:S(2)}, u32[]{:S(2)}) %collective-permute-start.9) | collective-permute-done | bytes 131104 | tf_op jit(solution)/shard_map/ppermute | solution.py:419
  79.2 0.8 collective-permute-done.8.refs_2_
  80.0 0.6 collective-permute-done.13.refs_7_
  80.6 1.1 %collective-permute-done.12.refs_6_ = f32[256,128]{1,0:T(8,128)S(1)} collective-permute-done((f32[256,128]{1,0:T(8,128)S(1)}, f32[256,128]{1,0:T(8,128)S(1)}, u32[]{:S(2)}, u32[]{:S(2)}) %collective-permute-start.12) | collective-permute-done | bytes 131104 | tf_op jit(solution)/shard_map/ppermute | solution.py:419
  81.7 0.9 %collective-permute-done.11.refs_5_ = f32[256,128]{1,0:T(8,128)S(1)} collective-permute-done((f32[256,128]{1,0:T(8,128)S(1)}, f32[256,128]{1,0:T(8,128)S(1)}, u32[]{:S(2)}, u32[]{:S(2)}) %collective-permute-start.11) | collective-permute-done | bytes 131104 | tf_op jit(solution)/shard_map/ppermute | solution.py:419
  82.6 1.2 %shard_map.145.local_ref = f32[1600,128]{1,0:T(8,128)S(1)} custom-call(f32[256,128]{1,0:T(8,128)S(1)} %shard_map.144.refs_0_, f32[256,128]{1,0:T(8,128)S(1)} %collective-permute-done.7.refs_1_, f32[256,128]{1,0:T(8,128)S(1)} %collective-permute-done.8.refs_2_, f32[256,128]{1,0:T(8,128)S(1)} %collective-permute-done.9.refs_3_, ...), custom_call_target="tpu_custom_call" | custom-call | tf_op jit(solution)/shard_map/pallas_call | solution.py:476
  83.9 2.5 %shard_map.146 = f32[25,64,128]{2,1,0:T(8,128)} custom-call(f32[1600,128]{1,0:T(8,128)S(1)} %shard_map.145.local_ref, s32[64,128]{1,0:T(8,128)S(1)} %bitcast.38, f32[200,25]{1,0:T(8,128)S(1)} %bitcast.39), custom_call_target="tpu_custom_call" | custom-call | tf_op jit(solution)/shard_map/pallas_call | solution.py:477
  (34 shorter events, 0.9 us)
Async XLA Ops:
  0.0 3.1 %copy-start.6 = (bf16[8,80,192]{2,1,0:T(8,128)(2,1)S(1)}, bf16[8,80,192]{2,1,0:T(8,128)(2,1)}, u32[]{:S(2)}) copy-start(bf16[8,80,192]{2,1,0:T(8,128)(2,1)} %constant.17.clone.table_ref) | copy-start | bytes 737284
  4.3 3.9 %copy-start.2 = (f32[2,9,64,2,8]{2,4,3,1,0:T(8,128)S(1)}, f32[2,9,64,2,8]{2,4,3,1,0:T(8,128)}, u32[]{:S(2)}) copy-start(f32[2,9,64,2,8]{2,4,3,1,0:T(8,128)} %param.19) | copy-start | bytes 221188
  4.3 14.2 %copy-start.10 = (f32[25,25]{1,0:T(8,128)S(1)}, f32[25,25]{1,0:T(8,128)}, u32[]{:S(2)}) copy-start(f32[25,25]{1,0:T(8,128)} %param.18) | copy-start | bytes 7504
  4.3 14.2 %copy-start.3 = (bf16[400,640]{1,0:T(8,128)(2,1)S(1)}, bf16[400,640]{1,0:T(8,128)(2,1)}, u32[]{:S(2)}) copy-start(bf16[400,640]{1,0:T(8,128)(2,1)} %constant.18.clone.table_ref) | copy-start | bytes 1536004
  4.3 13.2 %collective-permute-start = (f32[512,128]{1,0:T(8,128)S(1)}, f32[512,128]{1,0:T(8,128)S(1)}, u32[]{:S(2)}, u32[]{:S(2)}) collective-permute-start(f32[512,128]{1,0:T(8,128)S(1)} %get-tuple-element.21), channel_id=1, source_target_pairs={{0,2},{1,3},{2,0},{3,1},{4,6},{5,7},{6,4},{7,5},{8,10},{9,11},{10,... | collective-permute-start | bytes 786440 | tf_op jit(solution)/shard_map/ppermute | solution.py:415
  6.0 17.4 %copy-start.1 = (bf16[512,768]{1,0:T(8,128)(2,1)S(1)}, bf16[512,768]{1,0:T(8,128)(2,1)}, u32[]{:S(2)}) copy-start(bf16[512,768]{1,0:T(8,128)(2,1)} %constant.19.clone.refs_4_) | copy-start | bytes 2359300
  6.1 6.5 %collective-permute-start.2 = (f32[256,128]{1,0:T(8,128)S(1)}, f32[256,128]{1,0:T(8,128)S(1)}, u32[]{:S(2)}, u32[]{:S(2)}) collective-permute-start(f32[256,128]{1,0:T(8,128)S(1)} %get-tuple-element.17), channel_id=1, source_target_pairs={{0,1},{1,0},{2,3},{3,2},{4,5},{5,4},{6,7},{7,6},{8,9},{9,8},{10,11... | collective-permute-start | bytes 393224 | tf_op jit(solution)/shard_map/ppermute | solution.py:415
  6.9 7.4 %collective-permute-start.1 = (f32[256,128]{1,0:T(8,128)S(1)}, f32[256,128]{1,0:T(8,128)S(1)}, u32[]{:S(2)}, u32[]{:S(2)}) collective-permute-start(f32[256,128]{1,0:T(8,128)S(1)} %get-tuple-element.18), channel_id=1, source_target_pairs={{0,1},{1,0},{2,3},{3,2},{4,5},{5,4},{6,7},{7,6},{8,9},{9,8},{10,11... | collective-permute-start | bytes 393224 | tf_op jit(solution)/shard_map/ppermute | solution.py:415
  8.3 9.2 %collective-permute-start.3 = (f32[64,128]{1,0:T(8,128)S(1)}, f32[64,128]{1,0:T(8,128)S(1)}, u32[]{:S(2)}, u32[]{:S(2)}) collective-permute-start(f32[64,128]{1,0:T(8,128)S(1)} %shard_map.139), channel_id=1, source_target_pairs={{0,7},{1,6},{2,5},{3,4},{4,3},{5,2},{6,1},{7,0},{8,15},{9,14},{10,... | collective-permute-start | bytes 98312 | tf_op jit(solution)/shard_map/ppermute | solution.py:431
  14.3 6.7 %collective-permute-start.4 = (f32[256,128]{1,0:T(8,128)S(1)}, f32[256,128]{1,0:T(8,128)S(1)}, u32[]{:S(2)}, u32[]{:S(2)}) collective-permute-start(f32[256,128]{1,0:T(8,128)S(1)} %get-tuple-element.11._0), channel_id=1, source_target_pairs={{0,4},{1,5},{2,6},{3,7},{4,0},{5,1},{6,2},{7,3},{8,12},{9,13},{10,... | collective-permute-start | bytes 393224 | tf_op jit(solution)/shard_map/ppermute | solution.py:415
  17.3 6.2 %collective-permute-start.5 = (f32[256,128]{1,0:T(8,128)S(1)}, f32[256,128]{1,0:T(8,128)S(1)}, u32[]{:S(2)}, u32[]{:S(2)}) collective-permute-start(f32[256,128]{1,0:T(8,128)S(1)} %get-tuple-element.12._1), channel_id=1, source_target_pairs={{0,6},{1,7},{2,4},{3,5},{4,2},{5,3},{6,0},{7,1},{8,14},{9,15},{10,... | collective-permute-start | bytes 393224 | tf_op jit(solution)/shard_map/ppermute | solution.py:415
  17.5 5.9 %collective-permute-start.6 = (f32[256,128]{1,0:T(8,128)S(1)}, f32[256,128]{1,0:T(8,128)S(1)}, u32[]{:S(2)}, u32[]{:S(2)}) collective-permute-start(f32[256,128]{1,0:T(8,128)S(1)} %get-tuple-element.14), channel_id=1, source_target_pairs={{0,1},{1,0},{2,3},{3,2},{4,5},{5,4},{6,7},{7,6},{8,9},{9,8},{10,11... | collective-permute-start | bytes 393224 | tf_op jit(solution)/shard_map/ppermute | solution.py:415
  23.5 25.3 %copy-start.4 = (bf16[256,768]{1,0:T(8,128)(2,1)S(1)}, bf16[256,768]{1,0:T(8,128)(2,1)}, u32[]{:S(2)}) copy-start(bf16[256,768]{1,0:T(8,128)(2,1)} %constant.21.clone.inverse_ref) | copy-start | bytes 1179652
  23.5 25.3 %copy-start.5 = (bf16[256,768]{1,0:T(8,128)(2,1)S(1)}, bf16[256,768]{1,0:T(8,128)(2,1)}, u32[]{:S(2)}) copy-start(bf16[256,768]{1,0:T(8,128)(2,1)} %constant.20.clone.forward_ref) | copy-start | bytes 1179652
  48.8 19.2 %copy-start = (bf16[1536,256]{1,0:T(8,128)(2,1)S(1)}, bf16[1536,256]{1,0:T(8,128)(2,1)}, u32[]{:S(2)}) copy-start(bf16[1536,256]{1,0:T(8,128)(2,1)} %constant.22.clone.table_ref) | copy-start | bytes 2359300
  50.1 32.5 %copy-start.7 = (bf16[8,64,240]{2,1,0:T(8,128)(2,1)S(1)}, bf16[8,64,240]{2,1,0:T(8,128)(2,1)}, u32[]{:S(2)}) copy-start(bf16[8,64,240]{2,1,0:T(8,128)(2,1)} %constant.23.clone.refs_8_) | copy-start | bytes 737284
  68.3 15.6 %copy-start.8 = (s32[1,2,4096]{2,1,0:T(2,128)S(1)}, s32[1,2,4096]{2,1,0:T(2,128)}, u32[]{:S(2)}) copy-start(s32[1,2,4096]{2,1,0:T(2,128)} %param.16) | copy-start | bytes 98308
  68.3 15.6 %copy-start.9 = (f32[8,25,25]{2,0,1:T(8,128)S(1)}, f32[8,25,25]{2,0,1:T(8,128)}, u32[]{:S(2)}) copy-start(f32[8,25,25]{2,0,1:T(8,128)} %param.20) | copy-start | bytes 60004
  68.3 5.1 %collective-permute-start.10 = (f32[256,128]{1,0:T(8,128)S(1)}, f32[256,128]{1,0:T(8,128)S(1)}, u32[]{:S(2)}, u32[]{:S(2)}) collective-permute-start(f32[256,128]{1,0:T(8,128)S(1)} %shard_map.144.refs_0_), channel_id=1, source_target_pairs={{0,1},{1,0},{2,3},{3,2},{4,5},{5,4},{6,7},{7,6},{8,9},{9,8},{10,11... | collective-permute-start | bytes 393224 | tf_op jit(solution)/shard_map/ppermute | solution.py:419
  69.8 7.8 %collective-permute-start.7 = (f32[256,128]{1,0:T(8,128)S(1)}, f32[256,128]{1,0:T(8,128)S(1)}, u32[]{:S(2)}, u32[]{:S(2)}) collective-permute-start(f32[256,128]{1,0:T(8,128)S(1)} %shard_map.144.refs_0_), channel_id=1, source_target_pairs={{0,4},{1,5},{2,6},{3,7},{4,0},{5,1},{6,2},{7,3},{8,12},{9,13},{10,... | collective-permute-start | bytes 393224 | tf_op jit(solution)/shard_map/ppermute | solution.py:419
  70.9 8.3 %collective-permute-start.9 = (f32[256,128]{1,0:T(8,128)S(1)}, f32[256,128]{1,0:T(8,128)S(1)}, u32[]{:S(2)}, u32[]{:S(2)}) collective-permute-start(f32[256,128]{1,0:T(8,128)S(1)} %shard_map.144.refs_0_), channel_id=1, source_target_pairs={{0,6},{1,7},{2,0},{3,1},{4,2},{5,3},{6,4},{7,5},{8,14},{9,15},{10,... | collective-permute-start | bytes 393224 | tf_op jit(solution)/shard_map/ppermute | solution.py:419
  72.0 8.0 %collective-permute-start.8 = (f32[256,128]{1,0:T(8,128)S(1)}, f32[256,128]{1,0:T(8,128)S(1)}, u32[]{:S(2)}, u32[]{:S(2)}) collective-permute-start(f32[256,128]{1,0:T(8,128)S(1)} %shard_map.144.refs_0_), channel_id=1, source_target_pairs={{0,2},{1,3},{2,4},{3,5},{4,6},{5,7},{6,0},{7,1},{8,10},{9,11},{10,... | collective-permute-start | bytes 393224 | tf_op jit(solution)/shard_map/ppermute | solution.py:419
  73.4 7.2 %collective-permute-start.13 = (f32[256,128]{1,0:T(8,128)S(1)}, f32[256,128]{1,0:T(8,128)S(1)}, u32[]{:S(2)}, u32[]{:S(2)}) collective-permute-start(f32[256,128]{1,0:T(8,128)S(1)} %collective-permute-done.10.refs_4_), channel_id=1, source_target_pairs={{0,6},{1,7},{2,0},{3,1},{4,2},{5,3},{6,4},{7,5},{8,14},{9,15},{10,... | collective-permute-start | bytes 393224 | tf_op jit(solution)/shard_map/ppermute | solution.py:419
  75.5 6.2 %collective-permute-start.12 = (f32[256,128]{1,0:T(8,128)S(1)}, f32[256,128]{1,0:T(8,128)S(1)}, u32[]{:S(2)}, u32[]{:S(2)}) collective-permute-start(f32[256,128]{1,0:T(8,128)S(1)} %collective-permute-done.10.refs_4_), channel_id=1, source_target_pairs={{0,2},{1,3},{2,4},{3,5},{4,6},{5,7},{6,0},{7,1},{8,10},{9,11},{10,... | collective-permute-start | bytes 393224 | tf_op jit(solution)/shard_map/ppermute | solution.py:419
  77.7 5.0 %collective-permute-start.11 = (f32[256,128]{1,0:T(8,128)S(1)}, f32[256,128]{1,0:T(8,128)S(1)}, u32[]{:S(2)}, u32[]{:S(2)}) collective-permute-start(f32[256,128]{1,0:T(8,128)S(1)} %collective-permute-done.7.refs_1_), channel_id=1, source_target_pairs={{0,1},{1,0},{2,3},{3,2},{4,5},{5,4},{6,7},{7,6},{8,9},{9,8},{10,11... | collective-permute-start | bytes 393224 | tf_op jit(solution)/shard_map/ppermute | solution.py:419
